TPU v7x, 32 devices: a whole 2x2x4 slice. The times are simulated.
32 devices in a mesh: rep: 2 (over x), fsdp: 16 (over z, y, core).
Axes of the slice: x: 2, y: 2, z: 4, core: 2. Of those that a mesh axis runs over, the one named last changes fastest.
Arguments:
- tokens: bfloat16 [12288, 1536], P(('rep', 'fsdp')), may hold values from -6 to 6
- cotangent: bfloat16 [12288, 1536], P(('rep', 'fsdp')), may hold values from -6 to 6
- routes: int32 [12288, 8], P(('rep', 'fsdp')), may hold values from 0 to 15, all different within a row; in each aligned block of 384 rows (0 to 383, 384 to 767, ...) at most 240 rows name the same one
- gates: float32 [12288, 8], P(('rep', 'fsdp')), may hold values from 0.0625 to 0.25
- starts: int32 [32], P(('rep', 'fsdp')), may hold values from 0 to 128
- norm1_gain: float32 [1536], P('fsdp'), may hold values from 0.1 to 1.9
- w_query: float32 [1536, 1536], P('fsdp'), may hold values from -0.21875 to 0.21875
- w_key: float32 [1536, 512], P('fsdp'), may hold values from -0.21875 to 0.21875
- w_value: float32 [1536, 512], P('fsdp'), may hold values from -0.15625 to 0.15625
- w_out: float32 [1536, 1536], P('fsdp'), may hold values from -0.625 to 0.625
- norm2_gain: float32 [1536], P('fsdp'), may hold values from 0.1 to 1.9
- w_gate: float32 [1536, 16, 512], P('fsdp'), may hold values from -0.15625 to 0.15625
- w_up: float32 [1536, 16, 512], P('fsdp'), may hold values from -0.15625 to 0.15625
- w_down: float32 [512, 16, 1536], P('fsdp'), may hold values from -1 to 1
Outputs:
- output: float32 [12288, 1536], P(('rep', 'fsdp'))
- input_grad: float32 [12288, 1536], P(('rep', 'fsdp'))
- norm1_gain_grad: float32 [1536], P('fsdp')
- w_query_grad: float32 [1536, 1536], P('fsdp')
- w_key_grad: float32 [1536, 512], P('fsdp')
- w_value_grad: float32 [1536, 512], P('fsdp')
- w_out_grad: float32 [1536, 1536], P('fsdp')
- norm2_gain_grad: float32 [1536], P('fsdp')
- w_gate_grad: float32 [1536, 16, 512], P('fsdp')
- w_up_grad: float32 [1536, 16, 512], P('fsdp')
- w_down_grad: float32 [512, 16, 1536], P('fsdp')
Inputs may be any that keep to these rules, and one draw needn't show every extreme that they name: `routes`: each row names 8 different experts; in the rows of one device no expert is named by more than 240 rows, and in some device one expert is named by exactly 240.
All inputs are finite; a program needn't handle non-finite values.
Results may differ from a plain program's by a relative error of at most 0.023.
Values may be sent and summed in bfloat16 or wider, within the bound.
A program may use at most 448 MiB of HBM per device.

v0:
```python
import math

import jax
import jax.numpy as jnp
from jax import lax
from jax.sharding import PartitionSpec as P

HEADS = 24
KV_HEADS = 8
HEAD = 64
EXP = 16
PIECE = 256
CAP = 240


EPSILON = 1e-05
NEG_FILL = -1e30


def rope_tables(length, head_dim):
    half_dim = head_dim // 2
    positions = jnp.arange(length, dtype=jnp.float32)[:, None]
    inverse_rates = jnp.exp(
        jnp.arange(half_dim, dtype=jnp.float32) * (-2.0 * math.log(10000.0) / head_dim)
    )
    angles = positions * inverse_rates[None, :]
    return (jnp.cos(angles)[:, None, :], jnp.sin(angles)[:, None, :])


def rotate(values, cosine_table, sine_table):
    half_dim = values.shape[-1] // 2
    leading_half_dims = values[..., :half_dim]
    second_half = values[..., half_dim:]
    return jnp.concatenate(
        [
            leading_half_dims * cosine_table - second_half * sine_table,
            second_half * cosine_table + leading_half_dims * sine_table,
        ],
        axis=-1,
    )


def rotate_back(gradients, cosine_table, sine_table):
    half_dim = gradients.shape[-1] // 2
    leading_half_dims = gradients[..., :half_dim]
    second_half = gradients[..., half_dim:]
    return jnp.concatenate(
        [
            leading_half_dims * cosine_table + second_half * sine_table,
            second_half * cosine_table - leading_half_dims * sine_table,
        ],
        axis=-1,
    )


def piece_mask(length, piece_start):
    places = jnp.arange(length, dtype=jnp.int32)
    inside = (places >= piece_start) & (places < piece_start + PIECE)
    return (places[:, None] >= places[None, :]) | inside[:, None] & inside[None, :]


def shards(
    tokens,
    cotangent,
    routes,
    gates,
    starts,
    norm1_gain,
    w_query,
    w_key,
    w_value,
    w_out,
    norm2_gain,
    w_gate,
    w_up,
    w_down,
):
    inputs = tokens.astype(jnp.float32)
    length = inputs.shape[0]
    model_width = inputs.shape[1]
    head_count = HEADS
    kv_heads = KV_HEADS
    head_dim = HEAD
    group_size = head_count // kv_heads
    score_scale = 1.0 / math.sqrt(head_dim)
    experts = EXP
    capacity = CAP
    gain_attn, query_w, key_w, value_w, out_w, gain_ffn = (
        lax.all_gather(norm1_gain.astype(jnp.bfloat16), "fsdp", axis=0, tiled=True),
        lax.all_gather(w_query.astype(jnp.bfloat16), "fsdp", axis=0, tiled=True),
        lax.all_gather(w_key.astype(jnp.bfloat16), "fsdp", axis=0, tiled=True),
        lax.all_gather(w_value.astype(jnp.bfloat16), "fsdp", axis=0, tiled=True),
        lax.all_gather(w_out.astype(jnp.bfloat16), "fsdp", axis=0, tiled=True),
        lax.all_gather(norm2_gain.astype(jnp.bfloat16), "fsdp", axis=0, tiled=True),
    )
    gate_w, up_w, down_w = (
        lax.all_gather(w_gate.astype(jnp.bfloat16), "fsdp", axis=0, tiled=True),
        lax.all_gather(w_up.astype(jnp.bfloat16), "fsdp", axis=0, tiled=True),
        lax.all_gather(w_down.astype(jnp.bfloat16), "fsdp", axis=0, tiled=True),
    )
    gain_one = gain_attn.astype(jnp.float32)
    inv_one = lax.rsqrt(jnp.mean(inputs * inputs, axis=1, keepdims=True) + EPSILON)
    normed = (inputs * inv_one * gain_one).astype(jnp.bfloat16)
    query_raw = jnp.dot(normed, query_w, preferred_element_type=jnp.float32).reshape(
        length, head_count, head_dim
    )
    key_unrotated = jnp.dot(normed, key_w, preferred_element_type=jnp.float32).reshape(
        length, kv_heads, head_dim
    )
    value_reduced_precision = (
        jnp.dot(normed, value_w, preferred_element_type=jnp.float32)
        .astype(jnp.bfloat16)
        .reshape(length, kv_heads, head_dim)
    )
    cosine_table, sine_table = rope_tables(length, head_dim)
    query_rotated = (
        rotate(query_raw, cosine_table, sine_table)
        .astype(jnp.bfloat16)
        .reshape(length, kv_heads, group_size, head_dim)
    )
    key_rotated = rotate(key_unrotated, cosine_table, sine_table).astype(jnp.bfloat16)
    allowed = piece_mask(length, starts[0])
    scores = (
        jnp.einsum("voua,zoa->ouvz", query_rotated, key_rotated, preferred_element_type=jnp.float32)
        * score_scale
    )
    scores = jnp.where(allowed, scores, NEG_FILL)
    row_peak = jnp.max(scores, axis=3, keepdims=True)
    exponent = jnp.exp(scores - row_peak)
    row_total = jnp.sum(exponent, axis=3, keepdims=True)
    attn_probs = exponent / row_total
    log_total = row_peak + jnp.log(row_total)
    attended = (
        jnp.einsum(
            "xkfq,qxb->fxkb",
            attn_probs.astype(jnp.bfloat16),
            value_reduced_precision,
            preferred_element_type=jnp.float32,
        )
        .astype(jnp.bfloat16)
        .reshape(length, model_width)
    )
    residual = inputs + jnp.dot(attended, out_w, preferred_element_type=jnp.float32)
    gain_two = gain_ffn.astype(jnp.float32)
    inv_two = lax.rsqrt(jnp.mean(residual * residual, axis=1, keepdims=True) + EPSILON)
    normed_two = (residual * inv_two * gain_two).astype(jnp.bfloat16)
    top_k = routes.shape[1]
    onehot = (routes[:, :, None] == jnp.arange(experts, dtype=jnp.int32)[None, None, :]).astype(
        jnp.int32
    )
    chosen = jnp.sum(onehot, axis=1)
    before = jnp.cumsum(chosen, axis=0) - chosen
    slot_pair = jnp.sum(onehot * before[:, None, :], axis=2)
    target = (routes * capacity + slot_pair).reshape(length * top_k)
    token_ids = jnp.broadcast_to(
        jnp.arange(length, dtype=jnp.int32)[:, None], (length, top_k)
    ).reshape(length * top_k)
    source = jnp.zeros((experts * capacity,), jnp.int32).at[target].set(token_ids)
    slot_rows = jnp.take(normed_two, source, axis=0).reshape(experts, capacity, model_width)
    gate_pre = jnp.einsum("ecd,deh->ech", slot_rows, gate_w, preferred_element_type=jnp.float32)
    up_pre = jnp.einsum("ecd,deh->ech", slot_rows, up_w, preferred_element_type=jnp.float32)
    sigmoid_gate = jax.nn.sigmoid(gate_pre)
    swish = gate_pre * sigmoid_gate
    inner_act = (swish * up_pre).astype(jnp.bfloat16)
    expert_out = jnp.einsum(
        "ech,hed->ecd", inner_act, down_w, preferred_element_type=jnp.float32
    ).reshape(experts * capacity, model_width)
    picked = jnp.take(expert_out, target, axis=0).reshape(length, top_k, model_width)
    output = residual + jnp.sum(gates[:, :, None] * picked, axis=1)
    grad_out = cotangent.astype(jnp.float32)
    weighted = (
        (gates[:, :, None] * grad_out[:, None, :])
        .astype(jnp.bfloat16)
        .reshape(length * top_k, model_width)
    )
    grad_slots = (
        jnp.zeros((experts * capacity, model_width), jnp.bfloat16)
        .at[target]
        .set(weighted)
        .reshape(experts, capacity, model_width)
    )
    gate_w, up_w, down_w = (
        lax.all_gather(w_gate.astype(jnp.bfloat16), "fsdp", axis=0, tiled=True),
        lax.all_gather(w_up.astype(jnp.bfloat16), "fsdp", axis=0, tiled=True),
        lax.all_gather(w_down.astype(jnp.bfloat16), "fsdp", axis=0, tiled=True),
    )
    grad_inner = jnp.einsum("ecd,hed->ech", grad_slots, down_w, preferred_element_type=jnp.float32)
    grad_down = jnp.einsum(
        "ech,ecd->hed", inner_act, grad_slots, preferred_element_type=jnp.float32
    )
    grad_gate_pre = (
        grad_inner * up_pre * sigmoid_gate * (1.0 + gate_pre * (1.0 - sigmoid_gate))
    ).astype(jnp.bfloat16)
    grad_up_pre = (grad_inner * swish).astype(jnp.bfloat16)
    grad_gate_w = jnp.einsum(
        "ecd,ech->deh", slot_rows, grad_gate_pre, preferred_element_type=jnp.float32
    )
    grad_up_w = jnp.einsum(
        "ecd,ech->deh", slot_rows, grad_up_pre, preferred_element_type=jnp.float32
    )
    grad_rows = jnp.einsum(
        "ech,deh->ecd", grad_gate_pre, gate_w, preferred_element_type=jnp.float32
    )
    grad_rows = (
        grad_rows
        + jnp.einsum("ech,deh->ecd", grad_up_pre, up_w, preferred_element_type=jnp.float32)
    ).reshape(experts * capacity, model_width)
    grad_normed_two = jnp.sum(
        jnp.take(grad_rows, target, axis=0).reshape(length, top_k, model_width), axis=1
    )
    gain_attn, query_w, key_w, value_w, out_w, gain_ffn = (
        lax.all_gather(norm1_gain.astype(jnp.bfloat16), "fsdp", axis=0, tiled=True),
        lax.all_gather(w_query.astype(jnp.bfloat16), "fsdp", axis=0, tiled=True),
        lax.all_gather(w_key.astype(jnp.bfloat16), "fsdp", axis=0, tiled=True),
        lax.all_gather(w_value.astype(jnp.bfloat16), "fsdp", axis=0, tiled=True),
        lax.all_gather(w_out.astype(jnp.bfloat16), "fsdp", axis=0, tiled=True),
        lax.all_gather(norm2_gain.astype(jnp.bfloat16), "fsdp", axis=0, tiled=True),
    )
    gain_one = gain_attn.astype(jnp.float32)
    gain_two = gain_ffn.astype(jnp.float32)
    scaled_two = grad_normed_two * gain_two
    grad_resid = (
        grad_out
        + inv_two * scaled_two
        - residual * inv_two**3 * jnp.mean(scaled_two * residual, axis=1, keepdims=True)
    )
    grad_gain_two = jnp.sum(grad_normed_two * residual * inv_two, axis=0)
    grad_mixed = grad_resid.astype(jnp.bfloat16)
    grad_out_w = jnp.einsum("td,te->de", attended, grad_mixed, preferred_element_type=jnp.float32)
    attention_context_gradient = (
        jnp.einsum("te,de->td", grad_mixed, out_w, preferred_element_type=jnp.float32)
        .astype(jnp.bfloat16)
        .reshape(length, kv_heads, group_size, head_dim)
    )
    scores = (
        jnp.einsum("voua,zoa->ouvz", query_rotated, key_rotated, preferred_element_type=jnp.float32)
        * score_scale
    )
    scores = jnp.where(allowed, scores, NEG_FILL)
    attn_probs = jnp.exp(scores - log_total)
    grad_probs = jnp.einsum(
        "voua,zoa->ouvz",
        attention_context_gradient,
        value_reduced_precision,
        preferred_element_type=jnp.float32,
    )
    grad_value = (
        jnp.einsum(
            "fxyq,yfxk->qfk",
            attn_probs.astype(jnp.bfloat16),
            attention_context_gradient,
            preferred_element_type=jnp.float32,
        )
        .astype(jnp.bfloat16)
        .reshape(length, kv_heads * head_dim)
    )
    inner_sum = jnp.sum(attn_probs * grad_probs, axis=3, keepdims=True)
    logit_gradient = (attn_probs * (grad_probs - inner_sum)).astype(jnp.bfloat16)
    grad_query_rot = (
        jnp.einsum(
            "xkfq,qxb->fxkb", logit_gradient, key_rotated, preferred_element_type=jnp.float32
        ).reshape(length, head_count, head_dim)
        * score_scale
    )
    grad_key_rot = (
        jnp.einsum(
            "fxyq,yfxk->qfk", logit_gradient, query_rotated, preferred_element_type=jnp.float32
        )
        * score_scale
    )
    grad_query = (
        rotate_back(grad_query_rot, cosine_table, sine_table)
        .astype(jnp.bfloat16)
        .reshape(length, model_width)
    )
    grad_key = (
        rotate_back(grad_key_rot, cosine_table, sine_table)
        .astype(jnp.bfloat16)
        .reshape(length, kv_heads * head_dim)
    )
    grad_query_w = jnp.einsum("td,te->de", normed, grad_query, preferred_element_type=jnp.float32)
    grad_key_w = jnp.einsum("td,te->de", normed, grad_key, preferred_element_type=jnp.float32)
    grad_value_w = jnp.einsum("td,te->de", normed, grad_value, preferred_element_type=jnp.float32)
    grad_normed = jnp.einsum("te,de->td", grad_query, query_w, preferred_element_type=jnp.float32)
    grad_normed = grad_normed + jnp.einsum(
        "te,de->td", grad_key, key_w, preferred_element_type=jnp.float32
    )
    grad_normed = grad_normed + jnp.einsum(
        "te,de->td", grad_value, value_w, preferred_element_type=jnp.float32
    )
    scaled_one = grad_normed * gain_one
    input_grad = (
        grad_resid
        + inv_one * scaled_one
        - inputs * inv_one**3 * jnp.mean(scaled_one * inputs, axis=1, keepdims=True)
    )
    grad_gain_one = jnp.sum(grad_normed * inputs * inv_one, axis=0)
    down_part = lax.psum_scatter(
        grad_down.astype(jnp.bfloat16), "fsdp", scatter_dimension=0, tiled=True
    )
    gate_part, up_part = (
        lax.psum_scatter(
            grad_gate_w.astype(jnp.bfloat16), "fsdp", scatter_dimension=0, tiled=True
        ).astype(jnp.float32),
        lax.psum_scatter(
            grad_up_w.astype(jnp.bfloat16), "fsdp", scatter_dimension=0, tiled=True
        ).astype(jnp.float32),
    )
    gain_one_part, query_slice, key_part, value_part, out_part, gain_two_part = (
        lax.psum_scatter(
            grad_gain_one.astype(jnp.bfloat16), "fsdp", scatter_dimension=0, tiled=True
        ).astype(jnp.float32),
        lax.psum_scatter(
            grad_query_w.astype(jnp.bfloat16), "fsdp", scatter_dimension=0, tiled=True
        ).astype(jnp.float32),
        lax.psum_scatter(
            grad_key_w.astype(jnp.bfloat16), "fsdp", scatter_dimension=0, tiled=True
        ).astype(jnp.float32),
        lax.psum_scatter(
            grad_value_w.astype(jnp.bfloat16), "fsdp", scatter_dimension=0, tiled=True
        ).astype(jnp.float32),
        lax.psum_scatter(
            grad_out_w.astype(jnp.bfloat16), "fsdp", scatter_dimension=0, tiled=True
        ).astype(jnp.float32),
        lax.psum_scatter(
            grad_gain_two.astype(jnp.bfloat16), "fsdp", scatter_dimension=0, tiled=True
        ).astype(jnp.float32),
    )
    summed = (
        lax.psum(gain_one_part.astype(jnp.bfloat16), "rep").astype(jnp.float32),
        lax.psum(query_slice.astype(jnp.bfloat16), "rep").astype(jnp.float32),
        lax.psum(key_part.astype(jnp.bfloat16), "rep").astype(jnp.float32),
        lax.psum(value_part.astype(jnp.bfloat16), "rep").astype(jnp.float32),
        lax.psum(out_part.astype(jnp.bfloat16), "rep").astype(jnp.float32),
        lax.psum(gain_two_part.astype(jnp.bfloat16), "rep").astype(jnp.float32),
        lax.psum(gate_part.astype(jnp.bfloat16), "rep").astype(jnp.float32),
        lax.psum(up_part.astype(jnp.bfloat16), "rep").astype(jnp.float32),
        lax.psum(down_part, "rep").astype(jnp.float32),
    )
    return (
        output,
        input_grad,
        summed[0],
        summed[1],
        summed[2],
        summed[3],
        summed[4],
        summed[5],
        summed[6],
        summed[7],
        summed[8],
    )


def solution(mesh):
    placed = (
        P(("rep", "fsdp"), None),
        P(("rep", "fsdp"), None),
        P(("rep", "fsdp"), None),
        P(("rep", "fsdp"), None),
        P(("rep", "fsdp")),
        P("fsdp"),
        P("fsdp", None),
        P("fsdp", None),
        P("fsdp", None),
        P("fsdp", None),
        P("fsdp"),
        P("fsdp", None, None),
        P("fsdp", None, None),
        P("fsdp", None, None),
    )
    return jax.shard_map(
        shards,
        mesh=mesh,
        in_specs=placed,
        out_specs=(
            P(("rep", "fsdp"), None),
            P(("rep", "fsdp"), None),
            P("fsdp"),
            P("fsdp", None),
            P("fsdp", None),
            P("fsdp", None),
            P("fsdp", None),
            P("fsdp"),
            P("fsdp", None, None),
            P("fsdp", None, None),
            P("fsdp", None, None),
        ),
        check_vma=False,
    )
```

profile of v0, /device:TPU:0, one launch (start us, length us, event | category | flops | bytes accessed | tf_op | source)
XLA Modules:
  0.0 1981.9 jit_solution(9467320436240195633)
XLA Ops:
  14.5 2.8 copy.130
  17.4 4.9 copy.132
  30.0 35.8 %all-reduce.5 = (bf16[1536]{0:T(1024)(128)(2,1)S(1)}, bf16[1536]{0:T(1024)(128)(2,1)S(1)}) all-reduce(bf16[1536]{0:T(1024)(128)(2,1)S(1)} %dynamic-update-slice, bf16[1536]{0:T(1024)(128)(2,1)S(1)} %dynamic-update-slice.1), channel_id=1, replica_groups=mesh['rep'=2,'fsdp'=16] {'fsdp'}, use_global_device_ids=true, to_apply=%add | all-reduce | flops 3072 | bytes 12288
  68.1 12.3 scatter_custom_fusion
  81.4 22.2 %scatter_custom_fusion.1 = bf16[3840,1536]{1,0:T(8,128)(2,1)} fusion(s32[3072]{0:T(1024)} %bitcast.167, f32[384,1536]{1,0:T(8,128)S(1)} %convert_element_type.214, f32[3072]{0:T(1024)} %mul.528, bf16[]{:T(256)} %constant.62.clone.1), kind=kCustom, calls=%fused_computation.26 | custom fusion | flops 9437184 | bytes 14168576 | tf_op jit(solution)/shard_map/scatter | solution.py:179
  113.6 36.4 %all-gather.12.cloned.1.call-done = bf16[1536,1536]{1,0:T(8,128)(2,1)} async-done(((bf16[96,1536]{1,0:T(8,128)(2,1)}), bf16[1536,1536]{1,0:T(8,128)(2,1)}) %all-gather.12.cloned.1.call-update) | async-done | bytes 4718608 | tf_op jit(solution)/shard_map/all_gather | solution.py:90
  150.1 4.9 fusion.60
  155.4 6.4 fusion.66
  161.8 7.3 fusion.5
  169.2 7.8 fusion.31
  176.9 27.8 %all-gather.14.cloned.1.call-done = bf16[1536,1536]{1,0:T(8,128)(2,1)} async-done(((bf16[96,1536]{1,0:T(8,128)(2,1)}), bf16[1536,1536]{1,0:T(8,128)(2,1)}) %all-gather.14.cloned.1.call-update) | async-done | bytes 4718608 | tf_op jit(solution)/shard_map/all_gather | solution.py:93
  204.7 4.6 multiply_reduce_fusion.2
  211.0 13.7 gather_fusion
  225.4 108.5 %all-gather.20.cloned.1.call-done = bf16[512,16,1536]{2,0,1:T(8,128)(2,1)} async-done(((bf16[32,16,1536]{2,0,1:T(8,128)(2,1)}), bf16[512,16,1536]{2,0,1:T(8,128)(2,1)}) %all-gather.20.cloned.1.call-update) | async-done | bytes 25165840 | tf_op jit(solution)/shard_map/all_gather | solution.py:99
  333.9 18.6 fusion.68
  352.4 112.0 %all-gather.16.cloned.1.call-done = bf16[1536,16,512]{2,0,1:T(8,128)(2,1)} async-done(((bf16[96,16,512]{2,0,1:T(8,128)(2,1)}), bf16[1536,16,512]{2,0,1:T(8,128)(2,1)}) %all-gather.16.cloned.1.call-update) | async-done | bytes 25165840 | tf_op jit(solution)/shard_map/all_gather | solution.py:97
  464.4 19.1 fusion.13
  483.5 111.6 %all-gather.18.cloned.1.call-done = bf16[1536,16,512]{2,0,1:T(8,128)(2,1)} async-done(((bf16[96,16,512]{2,0,1:T(8,128)(2,1)}), bf16[1536,16,512]{2,0,1:T(8,128)(2,1)}) %all-gather.18.cloned.1.call-update) | async-done | bytes 25165840 | tf_op jit(solution)/shard_map/all_gather | solution.py:98
  595.1 24.5 %multiply_convert_fusion.2 = (bf16[16,240,512]{2,1,0:T(8,128)(2,1)}, bf16[16,240,512]{2,1,0:T(8,128)(2,1)}, bf16[16,240,512]{2,1,0:T(8,128)(2,1)}) fusion(f32[16,240,512]{2,1,0:T(8,128)} %fusion.13, f32[16,240,512]{2,1,0:T(8,128)} %fusion.68, bf16[1536,16,512]{2,0,1:T(8,128)(2,1)} %all-gather.18.cloned.1.call-done, bf16[16,240,1536]{2,1,0:T(8,128)(2,1)} %bitcast.140, ...), kind=kOutput, calls=%fused_computation.31 | convolution fusion | flops 6075187200 | bytes 64491264 | tf_op jit(solution)/shard_map/ecd,deh->ech/dot_general | solution.py:161
  619.6 17.3 fusion.67
  636.9 28.3 %gather_fusion.1 = f32[3072,1536]{1,0:T(8,128)} fusion(f32[3840,1536]{1,0:T(8,128)} %bitcast.138, s32[3072]{0:T(1024)S(1)} %copy-done.44), kind=kCustom, calls=%fused_computation.clone | custom fusion | bytes 37761024 | tf_op jit(solution)/shard_map/jit(_take)/gather | solution.py:168
  665.2 21.8 %fusion.69 = f32[16,240,1536]{2,1,0:T(8,128)} fusion(bf16[16,240,512]{2,1,0:T(8,128)(2,1)} %get-tuple-element.54, bf16[1536,16,512]{2,0,1:T(8,128)(2,1)} %all-gather.16.cloned.1.call-done), kind=kOutput, calls=%fused_computation.142 | convolution fusion | flops 6039797760 | bytes 52690944 | tf_op jit(solution)/shard_map/ech,deh->ecd/dot_general | solution.py:201
  687.0 25.3 %convolution_add_fusion = f32[16,240,1536]{2,1,0:T(8,128)} fusion(f32[16,240,1536]{2,1,0:T(8,128)} %fusion.69, bf16[16,240,512]{2,1,0:T(8,128)(2,1)} %get-tuple-element.55, bf16[1536,16,512]{2,0,1:T(8,128)(2,1)} %all-gather.18.cloned.1.call-done), kind=kOutput, calls=%fused_computation.13 | convolution fusion | flops 6045696000 | bytes 76283904 | tf_op jit(solution)/shard_map/ech,deh->ecd/dot_general | solution.py:206
  712.4 28.4 %gather_fusion.2 = f32[3072,1536]{1,0:T(8,128)} fusion(f32[3840,1536]{1,0:T(8,128)} %bitcast.137, s32[3072]{0:T(1024)S(1)} %copy-done.44), kind=kCustom, calls=%fused_computation.1.clone | custom fusion | bytes 37761024 | tf_op jit(solution)/shard_map/jit(_take)/gather | solution.py:209
  740.8 32.4 %bitcast_reduce_fusion = (f32[384,1536]{1,0:T(8,128)S(1)}, f32[384,1536]{1,0:T(8,128)S(1)}) fusion(f32[3072,1536]{1,0:T(8,128)} %gather_fusion.2, pred[3072]{0:T(1024)(128)(4,1)S(1)} %copy-done.53, f32[3072,1536]{1,0:T(8,128)} %gather_fusion.1, f32[384,8]{1,0:T(8,128)S(1)} %copy-done.17), kind=kLoop, calls=%fused_computation.8 | loop fusion | flops 22413312 | bytes 42482688 | tf_op jit(solution)/shard_map/reduce_sum | solution.py:208
  780.8 7.5 fusion.37
  788.3 9.5 fusion.2
  800.3 10.7 fusion.4
  817.2 5.8 convolution_convert_fusion
  823.1 4.7 convolution_multiply_fusion
  829.3 4.7 convolution_convert_fusion.1
  834.1 16.8 convert_bitcast_fusion
  850.9 32.9 %copy.112 = bf16[512,16,1536]{2,1,0:T(8,128)(2,1)} copy(bf16[512,16,1536]{0,2,1:T(8,128)(2,1)} %convert_bitcast_fusion) | data formatting | bytes 50331648 | tf_op jit(solution)/shard_map/convert_element_type | solution.py:299
  884.5 17.1 convert_bitcast_fusion.2
  901.5 32.6 %copy.110 = bf16[1536,16,512]{2,1,0:T(8,128)(2,1)} copy(bf16[1536,16,512]{0,2,1:T(8,128)(2,1)} %convert_bitcast_fusion.2) | data formatting | bytes 50331648 | tf_op jit(solution)/shard_map/convert_element_type | solution.py:303
  934.2 17.8 convert_bitcast_fusion.1
  952.0 32.8 %copy.111 = bf16[1536,16,512]{2,1,0:T(8,128)(2,1)} copy(bf16[1536,16,512]{0,2,1:T(8,128)(2,1)} %convert_bitcast_fusion.1) | data formatting | bytes 50331648 | tf_op jit(solution)/shard_map/convert_element_type | solution.py:306
  984.9 16.4 reduce-scatter.14.cloned.1.call-done
  1001.3 79.0 %reduce-scatter.8.cloned.1.call-done = bf16[96,1536]{1,0:T(8,128)(2,1)} async-done(((bf16[1536,1536]{1,0:T(8,128)(2,1)}), bf16[96,1536]{1,0:T(8,128)(2,1)}) %reduce-scatter.8.cloned.1.call-update) | async-done | bytes 294928 | tf_op jit(solution)/shard_map/reduce_scatter | solution.py:313
  1080.3 246.8 %reduce-scatter.20.cloned.1.call-done = bf16[32,16,1536]{2,1,0:T(8,128)(2,1)} async-done(((bf16[512,16,1536]{2,1,0:T(8,128)(2,1)}), bf16[32,16,1536]{2,1,0:T(8,128)(2,1)}) %reduce-scatter.20.cloned.1.call-update) | async-done | bytes 1572880 | tf_op jit(solution)/shard_map/reduce_scatter | solution.py:298
  1327.1 247.1 %reduce-scatter.16.cloned.1.call-done = bf16[96,16,512]{2,1,0:T(8,128)(2,1)} async-done(((bf16[1536,16,512]{2,1,0:T(8,128)(2,1)}), bf16[96,16,512]{2,1,0:T(8,128)(2,1)}) %reduce-scatter.16.cloned.1.call-update) | async-done | bytes 1572880 | tf_op jit(solution)/shard_map/reduce_scatter | solution.py:302
  1574.2 247.0 %reduce-scatter.18.cloned.1.call-done = bf16[96,16,512]{2,1,0:T(8,128)(2,1)} async-done(((bf16[1536,16,512]{2,1,0:T(8,128)(2,1)}), bf16[96,16,512]{2,1,0:T(8,128)(2,1)}) %reduce-scatter.18.cloned.1.call-update) | async-done | bytes 1572880 | tf_op jit(solution)/shard_map/reduce_scatter | solution.py:305
  1821.9 4.9 fusion.70
  1828.3 3.3 fusion.30
  1831.5 32.7 %all-reduce.4 = (bf16[1536]{0:T(1024)(128)(2,1)}, bf16[1536]{0:T(1024)(128)(2,1)}) all-reduce(bf16[1536]{0:T(1024)(128)(2,1)} %get-tuple-element.36, bf16[1536]{0:T(1024)(128)(2,1)S(1)} %copy-done.52), channel_id=2, replica_groups=mesh['rep'=2,'fsdp'=16] {'fsdp'}, use_global_device_ids=true, to_apply=%region_16.18.clone | all-reduce | flops 3072 | bytes 12288
  1866.3 5.6 all-reduce.6
  1874.9 3.7 fusion.27
  1878.6 83.0 %all-reduce.10.cloned.1.call-done = (bf16[96,1536]{1,0:T(8,128)(2,1)}, bf16[96,512]{1,0:T(8,128)(2,1)}, bf16[96,512]{1,0:T(8,128)(2,1)}, bf16[96,1536]{1,0:T(8,1...) async-done(((bf16[96,1536]{1,0:T(8,128)(2,1)}, bf16[96,512]{1,0:T(8,128)(2,1)}, bf16[96,512]{1,0:T(8,128)(2,1)}, ...) | async-done | bytes 5505040 | tf_op jit(solution)/shard_map/psum | solution.py:331
  (235 shorter events, 67.7 us)
Async XLA Ops:
  7.2 7.3 copy-start.10
  7.2 101.1 %all-gather.8.cloned.1.call-start = ((), (), s32[]{:S(2)}) async-start(), calls=%async_computation.7 | async-start | bytes 1671168 | tf_op jit(solution)/shard_map/all_gather | solution.py:92
  9.0 101.8 %all-gather.10.cloned.1.call-start = ((), (), s32[]{:S(2)}) async-start(), calls=%async_computation.8 | async-start | bytes 1671168 | tf_op jit(solution)/shard_map/all_gather | solution.py:91
  10.6 139.4 %all-gather.12.cloned.1.call-start = ((), (), s32[]{:S(2)}) async-start(), calls=%async_computation.9 | async-start | bytes 5013504 | tf_op jit(solution)/shard_map/all_gather | solution.py:90
  12.5 192.2 %all-gather.14.cloned.1.call-start = ((), (), s32[]{:S(2)}) async-start(), calls=%async_computation.10 | async-start | bytes 5013504 | tf_op jit(solution)/shard_map/all_gather | solution.py:93
  14.4 319.4 %all-gather.20.cloned.1.call-start = ((), (), s32[]{:S(2)}) async-start(), calls=%async_computation.13 | async-start | bytes 26738688 | tf_op jit(solution)/shard_map/all_gather | solution.py:99
  17.3 5.0 copy-start.11
  17.3 447.1 %all-gather.16.cloned.1.call-start = ((), (), s32[]{:S(2)}) async-start(), calls=%async_computation.11 | async-start | bytes 26738688 | tf_op jit(solution)/shard_map/all_gather | solution.py:97
  22.3 572.8 %all-gather.18.cloned.1.call-start = ((), (), s32[]{:S(2)}) async-start(), calls=%async_computation.12 | async-start | bytes 26738688 | tf_op jit(solution)/shard_map/all_gather | solution.py:98
  25.2 41.3 %copy-start.54 = (f32[384,8]{0,1:T(8,128)S(1)}, f32[384,8]{0,1:T(8,128)}, u32[]{:S(2)}) copy-start(f32[384,8]{0,1:T(8,128)} %param.19) | copy-start | bytes 36868
  25.2 55.9 %copy-start.7 = (bf16[384,1536]{1,0:T(8,128)(2,1)S(1)}, bf16[384,1536]{1,0:T(8,128)(2,1)}, u32[]{:S(2)}) copy-start(bf16[384,1536]{1,0:T(8,128)(2,1)} %param.17) | copy-start | bytes 3538948
  25.2 959.7 %reduce-scatter.12.cloned.1.call-start = ((), (), s32[]{:S(2)}) async-start(), calls=%async_computation.16 | async-start | bytes 1671168 | tf_op jit(solution)/shard_map/reduce_scatter | solution.py:319
  66.5 143.5 %copy-start.42 = (f32[1536]{0:T(1024)}, f32[1536]{0:T(1024)S(1)}, u32[]{:S(2)}) copy-start(f32[1536]{0:T(1024)S(1)} %convert_element_type.208) | copy-start | bytes 18436
  66.6 13.8 copy-start.16
  81.1 514.0 %copy-start.39 = (pred[16,240]{1,0:T(8,128)(4,1)}, pred[16,240]{1,0:T(8,128)(4,1)S(1)}, u32[]{:S(2)}) copy-start(pred[16,240]{1,0:T(8,128)(4,1)S(1)} %broadcast_in_dim.43) | copy-start | bytes 11524
  81.4 23.0 %copy-start.3 = (bf16[384,1536]{1,0:T(8,128)(2,1)S(1)}, bf16[384,1536]{1,0:T(8,128)(2,1)}, u32[]{:S(2)}) copy-start(bf16[384,1536]{1,0:T(8,128)(2,1)} %param.16) | copy-start | bytes 3538948
  105.3 44.8 %copy-start.50 = (f32[384]{0:T(512)}, f32[384]{0:T(512)S(1)}, u32[]{:S(2)}) copy-start(f32[384]{0:T(512)S(1)} %get-tuple-element.67) | copy-start | bytes 4612
  108.1 46.8 %copy-start.29 = (f32[384,32]{0,1:T(8,128)}, f32[384,32]{0,1:T(8,128)S(1)}, u32[]{:S(2)}) copy-start(f32[384,32]{0,1:T(8,128)S(1)} %get-tuple-element.72) | copy-start | bytes 147460
  108.1 46.8 %copy-start.32 = (f32[384,32]{0,1:T(8,128)}, f32[384,32]{0,1:T(8,128)S(1)}, u32[]{:S(2)}) copy-start(f32[384,32]{0,1:T(8,128)S(1)} %get-tuple-element.73) | copy-start | bytes 147460
  110.8 58.4 %copy-start.18 = (bf16[384,512]{0,1:T(8,128)(2,1)}, bf16[384,512]{0,1:T(8,128)(2,1)S(1)}, u32[]{:S(2)}) copy-start(bf16[384,512]{0,1:T(8,128)(2,1)S(1)} %copy.93) | copy-start | bytes 1179652
  113.6 41.8 %copy-start.37 = (bf16[384,8,32]{0,2,1:T(8,128)(2,1)}, bf16[384,8,32]{0,2,1:T(8,128)(2,1)S(1)}, u32[]{:S(2)}) copy-start(bf16[384,8,32]{0,2,1:T(8,128)(2,1)S(1)} %get-tuple-element.64) | copy-start | bytes 589828
  113.6 41.8 %copy-start.38 = (bf16[384,8,32]{0,2,1:T(8,128)(2,1)}, bf16[384,8,32]{0,2,1:T(8,128)(2,1)S(1)}, u32[]{:S(2)}) copy-start(bf16[384,8,32]{0,2,1:T(8,128)(2,1)S(1)} %get-tuple-element.65) | copy-start | bytes 589828
  155.3 6.5 copy-start.12
  155.3 6.5 copy-start.14
  176.9 32.4 %copy-start.9 = (bf16[8,64,3,384]{3,1,2,0:T(8,128)(2,1)}, bf16[8,64,3,384]{3,1,2,0:T(8,128)(2,1)S(1)}, u32[]{:S(2)}) copy-start(bf16[8,64,3,384]{3,1,2,0:T(8,128)(2,1)S(1)} %fusion.31) | copy-start | bytes 3538948
  210.0 14.8 copy-start.48
  619.6 17.3 copy-start.44
  712.4 28.4 %copy-start.17 = (f32[384,8]{1,0:T(8,128)S(1)}, f32[384,8]{1,0:T(8,128)}, u32[]{:S(2)}) copy-start(f32[384,8]{1,0:T(8,128)} %copy-done.16) | copy-start | bytes 36868
  712.4 28.4 %copy-start.53 = (pred[3072]{0:T(1024)(128)(4,1)S(1)}, pred[3072]{0:T(1024)(128)(4,1)}, u32[]{:S(2)}) copy-start(pred[3072]{0:T(1024)(128)(4,1)} %compare_and_fusion.1) | copy-start | bytes 9220
  740.8 32.4 %copy-start.2 = (f32[384,1536]{1,0:T(8,128)S(1)}, f32[384,1536]{1,0:T(8,128)}, u32[]{:S(2)}) copy-start(f32[384,1536]{1,0:T(8,128)} %copy-done.1) | copy-start | bytes 7077892
  740.8 32.4 %copy-start.43 = (f32[1536]{0:T(1024)S(1)}, f32[1536]{0:T(1024)}, u32[]{:S(2)}) copy-start(f32[1536]{0:T(1024)} %copy-done.42) | copy-start | bytes 18436
  740.8 32.4 %copy-start.49 = (f32[384]{0:T(512)S(1)}, f32[384]{0:T(512)}, u32[]{:S(2)}) copy-start(f32[384]{0:T(512)} %copy-done.48) | copy-start | bytes 4612
  740.8 33.6 %copy-start.8 = (bf16[384,1536]{1,0:T(8,128)(2,1)S(1)}, bf16[384,1536]{1,0:T(8,128)(2,1)}, u32[]{:S(2)}) copy-start(bf16[384,1536]{1,0:T(8,128)(2,1)} %param.17) | copy-start | bytes 3538948
  780.8 7.5 copy-start.19
  788.3 9.5 copy-start.27
  788.3 9.5 copy-start.4
  788.3 9.5 copy-start.47
  788.3 9.5 copy-start.51
  800.2 184.7 %reduce-scatter.10.cloned.1.call-start = ((), (), s32[]{:S(2)}) async-start(), calls=%async_computation.15 | async-start | bytes 1671168 | tf_op jit(solution)/shard_map/reduce_scatter | solution.py:316
  800.2 10.7 copy-start.13
  800.2 10.7 copy-start.15
  817.1 184.2 %reduce-scatter.14.cloned.1.call-start = ((), (), s32[]{:S(2)}) async-start(), calls=%async_computation.17 | async-start | bytes 5013504 | tf_op jit(solution)/shard_map/reduce_scatter | solution.py:322
  823.0 257.3 %reduce-scatter.8.cloned.1.call-start = ((), (), s32[]{:S(2)}) async-start(), calls=%async_computation.14 | async-start | bytes 5013504 | tf_op jit(solution)/shard_map/reduce_scatter | solution.py:313
  834.1 493.0 %reduce-scatter.20.cloned.1.call-start = ((), (), s32[]{:S(2)}) async-start(), calls=%async_computation.20 | async-start | bytes 26738688 | tf_op jit(solution)/shard_map/reduce_scatter | solution.py:298
  883.8 690.4 %reduce-scatter.16.cloned.1.call-start = ((), (), s32[]{:S(2)}) async-start(), calls=%async_computation.18 | async-start | bytes 26738688 | tf_op jit(solution)/shard_map/reduce_scatter | solution.py:302
  934.1 887.1 %reduce-scatter.18.cloned.1.call-start = ((), (), s32[]{:S(2)}) async-start(), calls=%async_computation.19 | async-start | bytes 26738688 | tf_op jit(solution)/shard_map/reduce_scatter | solution.py:305
  984.8 976.8 %all-reduce.10.cloned.1.call-start = ((), (), s32[]{:S(2)}) async-start(), calls=%async_computation.21 | async-start | bytes 11010048 | tf_op jit(solution)/shard_map/psum | solution.py:331
  1961.6 7.0 copy-start.25
  (29 other events, 72.3 us)
Sparse Core Ops, SparseCore 0:
  10.9 42.5 all-gather.7
  56.4 38.4 all-gather.9
  97.7 52.2 all-gather.11
  152.8 51.9 all-gather.13
  206.7 127.0 all-gather.19
  335.8 128.5 all-gather.15
  466.5 128.5 all-gather.17
  800.3 59.4 reduce-scatter.11
  864.5 58.5 reduce-scatter.9
  926.7 74.5 reduce-scatter.13
  1005.7 74.5 reduce-scatter.7
  1084.3 242.7 reduce-scatter.19
  1331.2 242.9 reduce-scatter.15
  1578.1 243.0 reduce-scatter.17
  1824.1 137.4 all-reduce.9
where the time goes:
time: 1990 us; the launch traced here: 1980 us
  waiting for transfers between devices  1320 us (66%)
  matrix products  257 us (13%)
  local copies, waits for them, and re-layouts  205 us (10%)
  other arithmetic  112 us (6%)
  blocking collectives  74.2 us (4%)
    reduce_scatter x1, waiting for transfers between devices, shards(): lax.psum_scatter(grad_gate_w.astype(jnp.bfloat16), 'fsdp', scatter_dimens...  247 us
    reduce_scatter x1, waiting for transfers between devices, shards(): lax.psum_scatter(grad_up_w.astype(jnp.bfloat16), 'fsdp', scatter_dimensio...  247 us
    reduce_scatter x1, waiting for transfers between devices, shards(): lax.psum_scatter(grad_down.astype(jnp.bfloat16), 'fsdp', scatter_dimensio...  247 us
    all_gather x1, waiting for transfers between devices, shards(): lax.all_gather(w_gate.astype(jnp.bfloat16), 'fsdp', axis=0, tiled=True)  112 us
    all_gather x1, waiting for transfers between devices, shards(): lax.all_gather(w_up.astype(jnp.bfloat16), 'fsdp', axis=0, tiled=True)  112 us
    all_gather x1, waiting for transfers between devices, shards(): lax.all_gather(w_down.astype(jnp.bfloat16), 'fsdp', axis=0, tiled=True)  108 us
    psum x1, waiting for transfers between devices, shards(): lax.psum(query_slice.astype(jnp.bfloat16), 'rep').astype(jnp.float32)  83 us
    reduce_scatter x1, waiting for transfers between devices, shards(): lax.psum_scatter(grad_query_w.astype(jnp.bfloat16), 'fsdp', scatter_dimen...  79 us
  transfers between devices with their start and end apart: 15, of which 11 were waited for; matrix products, arithmetic and copies ran while one was open for 18% of the time, Pallas kernels for 0%

commit v1 on v0

v1 whole, which is shorter than its diff:
```python
import math

import jax
import jax.numpy as jnp
from jax import lax
from jax.experimental import pallas as pl
from jax.experimental.pallas import tpu as pltpu
from jax.sharding import PartitionSpec as P

HEADS = 24
KV_HEADS = 8
HEAD = 64
EXP = 16
PIECE = 256
AXES = ("rep", "fsdp")
EPSILON = 1e-05
NEG_FILL = -1e30
BF = jnp.bfloat16
F32 = jnp.float32
PLANE = 8
EPD = EXP // PLANE


def rope_tables(length, head_dim):
    half_dim = head_dim // 2
    positions = jnp.arange(length, dtype=F32)[:, None]
    inverse_rates = jnp.exp(
        jnp.arange(half_dim, dtype=F32) * (-2.0 * math.log(10000.0) / head_dim)
    )
    angles = positions * inverse_rates[None, :]
    return (jnp.cos(angles)[:, None, :], jnp.sin(angles)[:, None, :])


def rotate(values, cosine_table, sine_table):
    half_dim = values.shape[-1] // 2
    first = values[..., :half_dim]
    second = values[..., half_dim:]
    return jnp.concatenate(
        [
            first * cosine_table - second * sine_table,
            second * cosine_table + first * sine_table,
        ],
        axis=-1,
    )


def rotate_back(gradients, cosine_table, sine_table):
    return rotate(gradients, cosine_table, -sine_table)


def piece_mask(length, piece_start):
    places = jnp.arange(length, dtype=jnp.int32)
    inside = (places >= piece_start) & (places < piece_start + PIECE)
    return (places[:, None] >= places[None, :]) | inside[:, None] & inside[None, :]


def dot(a, b):
    return jnp.dot(a, b, preferred_element_type=F32)


def dot_nt(a, b):
    return lax.dot_general(a, b, (((1,), (1,)), ((), ())), preferred_element_type=F32)


def dot_tn(a, b):
    return lax.dot_general(a, b, (((0,), (0,)), ((), ())), preferred_element_type=F32)


def place(pieces, moves, out_shape):
    scalars = []

    def number(value):
        scalars.append(jnp.asarray(value, jnp.int32))
        return len(scalars) - 1

    plan = []
    for i, src, (lead, row, rows, col, cols) in moves:
        plan.append(
            (i, src, None if lead is None else number(lead), number(row), rows, number(col), cols)
        )

    def kernel(offs, *refs):
        ins, out, sems = refs[: len(pieces)], refs[len(pieces)], refs[len(pieces) + 1]
        copies = []
        for n, (i, src, lead, row, rows, col, cols) in enumerate(plan):
            to = (
                pl.ds(pl.multiple_of(offs[row], 16), rows),
                pl.ds(pl.multiple_of(offs[col], 128), cols),
            )
            if lead is not None:
                to = (offs[lead],) + to
            copies.append(
                pltpu.make_async_copy(ins[i].at[src], out.at[to], sems.at[n])
            )
        for copy in copies:
            copy.start()
        for copy in copies:
            copy.wait()

    return pl.pallas_call(
        kernel,
        out_shape=out_shape,
        in_specs=[pl.BlockSpec(memory_space=pltpu.SMEM)]
        + [pl.BlockSpec(memory_space=pl.ANY)] * len(pieces),
        out_specs=pl.BlockSpec(memory_space=pltpu.VMEM),
        scratch_shapes=[pltpu.SemaphoreType.DMA((len(plan),))],
        compiler_params=pltpu.CompilerParams(vmem_limit_bytes=40 * 2**20),
    )(jnp.stack(scalars), *pieces)


def shards(
    reps,
    group,
    tokens,
    cotangent,
    routes,
    gates,
    starts,
    norm1_gain,
    w_query,
    w_key,
    w_value,
    w_out,
    norm2_gain,
    w_gate,
    w_up,
    w_down,
):
    planes = group // 4
    r, f = lax.axis_index("rep"), lax.axis_index("fsdp")
    xb, yb, c, z = r % 2, (f // 2) % 2, f % 2, f // 4
    mine = xb * 4 + yb * 2 + c

    def perm(to):
        return [
            (a * group + b, to(a, b)[0] * group + to(a, b)[1])
            for a in range(reps)
            for b in range(group)
        ]

    def pp(value, to):
        return lax.ppermute(value, AXES, perm(to))

    def go(value, dx, dy, dc):
        return pp(value, lambda a, b: (a ^ dx, b ^ (dy * 2 + dc)))

    def along(value, k):
        return pp(value, lambda a, b: (a, (b + 4 * k) % group))

    def all_reps(value):
        step = 2
        while step < reps:
            value = value + pp(value, lambda a, b, s=step: (a ^ s, b))
            step *= 2
        return value

    length, width = tokens.shape
    ds = w_query.shape[0]
    hs = w_down.shape[0]
    hid = w_gate.shape[2]
    kvd = w_key.shape[1]
    group_size = HEADS // KV_HEADS
    score_scale = 1.0 / math.sqrt(HEAD)
    half_rows = length // 2

    def split_axes(columns):
        half = columns // 2
        part = (half // 128 + 1) // 2 * 128
        return half, part

    def gather_rows(own):
        columns = own.shape[1]
        half, part = split_axes(columns)
        send = lax.dynamic_slice(own, (0, xb * half), (ds, half))
        stack = jnp.concatenate([send] + [along(send, k) for k in range(1, planes)], axis=0)
        a, b = stack[:, :part], stack[:, part:]
        ax, by = go(a, 1, 0, 0), go(b, 0, 1, 0)
        a_all = {(0, 0): a, (1, 0): ax, (0, 1): go(a, 0, 1, 0), (1, 1): go(ax, 0, 1, 0)}
        b_all = {(0, 0): b, (0, 1): by, (1, 0): go(b, 1, 0, 0), (1, 1): go(by, 1, 0, 0)}
        pieces, moves = [], []
        for held, col, cols in ((a_all, 0, part), (b_all, part, half - part)):
            for (dx, dy), piece in held.items():
                for dc in range(2):
                    pieces.append(piece if dc == 0 else go(piece, 0, 0, 1))
                    for k in range(planes):
                        owner = ((z - k) % planes) * 4 + (yb ^ dy) * 2 + (c ^ dc)
                        moves.append(
                            (
                                len(pieces) - 1,
                                (pl.ds(k * ds, ds),),
                                (None, owner * ds, ds, (xb ^ dx) * half + col, cols),
                            )
                        )
        return place(pieces, moves, jax.ShapeDtypeStruct((width, columns), BF))

    def scatter_rows(grad):
        columns = grad.shape[1]
        half, part = split_axes(columns)
        by_core = grad.reshape(planes, 2, 2, ds, columns)

        def pick(value, index, axis):
            return lax.dynamic_index_in_dim(value, index, axis, keepdims=False)

        kept = pick(by_core, c, 2) + go(pick(by_core, 1 - c, 2), 0, 0, 1)
        kept = kept.reshape(planes, 2, ds, 2, half)
        a, b = kept[..., :part], kept[..., part:]
        a = pick(a, yb, 1) + go(pick(a, 1 - yb, 1), 0, 1, 0)
        b = pick(b, xb, 3) + go(pick(b, 1 - xb, 3), 1, 0, 0)
        a = pick(a, xb, 2) + go(pick(a, 1 - xb, 2), 1, 0, 0)
        b = pick(b, yb, 1) + go(pick(b, 1 - yb, 1), 0, 1, 0)
        both = jnp.concatenate([a, b], axis=2)
        total = pick(both, z, 0).astype(F32)
        for k in range(1, planes):
            total = total + along(pick(both, (z + k) % planes, 0), k).astype(F32)
        total = all_reps(total.astype(BF))
        other = go(total, 1, 0, 0)
        return jnp.where(
            xb == 0,
            jnp.concatenate([total, other], axis=1),
            jnp.concatenate([other, total], axis=1),
        ).astype(F32)

    def gather_tokens(own):
        a, b = own[:half_rows], own[half_rows:]
        ax, by = go(a, 1, 0, 0), go(b, 0, 1, 0)
        a_all = {(0, 0): a, (1, 0): ax, (0, 1): go(a, 0, 1, 0), (1, 1): go(ax, 0, 1, 0)}
        b_all = {(0, 0): b, (0, 1): by, (1, 0): go(b, 1, 0, 0), (1, 1): go(by, 1, 0, 0)}
        parts = []
        for dx in range(2):
            for dy in range(2):
                for dc in range(2):
                    for held in (a_all, b_all):
                        piece = held[(dx, dy)]
                        parts.append(piece if dc == 0 else go(piece, 0, 0, 1))
        return jnp.concatenate(parts, axis=0)

    def scatter_tokens(partial):
        slots = partial.reshape(2, 2, 2, length, width)
        kept = slots[:, :, 0] + go(slots[:, :, 1], 0, 0, 1)
        a, b = kept[:, :, :half_rows], kept[:, :, half_rows:]
        a = a[:, 0] + go(a[:, 1], 0, 1, 0)
        b = b[0] + go(b[1], 1, 0, 0)
        a = a[0].astype(F32) + go(a[1], 1, 0, 0).astype(F32)
        b = b[0].astype(F32) + go(b[1], 0, 1, 0).astype(F32)
        return jnp.concatenate([a, b], axis=0)

    pad = jnp.zeros((ds, 254), BF)
    front = jnp.concatenate(
        [
            w_query.astype(BF),
            w_key.astype(BF),
            w_value.astype(BF),
            norm1_gain.astype(BF)[:, None],
            norm2_gain.astype(BF)[:, None],
            pad,
        ],
        axis=1,
    )
    front = gather_rows(front)
    out_w = gather_rows(w_out.astype(BF))

    gate_up = jnp.concatenate([w_gate.astype(BF), w_up.astype(BF)], axis=2).transpose(1, 0, 2)
    down = w_down.astype(BF).transpose(1, 0, 2)

    def expert_weights(source, e, rows):
        columns = source.shape[2]
        pieces, moves = [], []
        for dy in range(2):
            for dc in range(2):
                target = (mine ^ (dy * 2 + dc)) * EPD + e
                block = lax.dynamic_index_in_dim(source, target, 0, keepdims=False)
                pieces.append(block if dy + dc == 0 else go(block, 0, dy, dc))
                moves.append(
                    (
                        len(pieces) - 1,
                        (),
                        (None, ((yb ^ dy) * 2 + (c ^ dc)) * rows, rows, 0, columns),
                    )
                )
        piece = place(pieces, moves, jax.ShapeDtypeStruct((4 * rows, columns), BF))
        ring, moves = [piece], [(0, (), (None, z * 4 * rows, 4 * rows, 0, columns))]
        for k in range(1, planes):
            ring.append(along(ring[-1], 1))
            moves.append(
                (k, (), (None, ((z - k) % planes) * 4 * rows, 4 * rows, 0, columns))
            )
        return place(ring, moves, jax.ShapeDtypeStruct((planes * 4 * rows, columns), BF))

    expert_in = [expert_weights(gate_up, e, ds) for e in range(EPD)]
    expert_down = [expert_weights(down, e, hs) for e in range(EPD)]

    experts = jnp.arange(EXP, dtype=jnp.int32)[:, None, None]
    share = jnp.sum(jnp.where(routes[None] == experts, gates[None], 0.0), axis=2)
    shares = []
    for j in range(PLANE):
        block = lax.dynamic_slice(share, ((mine ^ j) * EPD, 0), (EPD, length))
        shares.append(block if j == 0 else go(block, j // 4, (j // 2) % 2, j % 2))
    shares = jnp.concatenate(shares, axis=1)

    grads_all = gather_tokens(cotangent)

    inputs = tokens.astype(F32)
    gain_one = front[:, 2560].astype(F32)[None, :]
    gain_two = front[:, 2561].astype(F32)[None, :]
    inv_one = lax.rsqrt(jnp.mean(inputs * inputs, axis=1, keepdims=True) + EPSILON)
    normed = (inputs * inv_one * gain_one).astype(BF)
    mixed = dot(normed, front[:, : width + 2 * kvd])
    query_raw = mixed[:, :width].reshape(length, HEADS, HEAD)
    key_raw = mixed[:, width : width + kvd].reshape(length, KV_HEADS, HEAD)
    value = mixed[:, width + kvd :].astype(BF).reshape(length, KV_HEADS, HEAD)
    cosine_table, sine_table = rope_tables(length, HEAD)
    query_rotated = (
        rotate(query_raw, cosine_table, sine_table)
        .astype(BF)
        .reshape(length, KV_HEADS, group_size, HEAD)
    )
    key_rotated = rotate(key_raw, cosine_table, sine_table).astype(BF)
    allowed = piece_mask(length, starts[0])
    scores = (
        jnp.einsum("voua,zoa->ouvz", query_rotated, key_rotated, preferred_element_type=F32)
        * score_scale
    )
    scores = jnp.where(allowed, scores, NEG_FILL)
    row_peak = jnp.max(scores, axis=3, keepdims=True)
    exponent = jnp.exp(scores - row_peak)
    row_total = jnp.sum(exponent, axis=3, keepdims=True)
    attn_probs = exponent / row_total
    attended = (
        jnp.einsum("xkfq,qxb->fxkb", attn_probs.astype(BF), value, preferred_element_type=F32)
        .astype(BF)
        .reshape(length, width)
    )
    residual = inputs + dot(attended, out_w)
    inv_two = lax.rsqrt(jnp.mean(residual * residual, axis=1, keepdims=True) + EPSILON)
    normed_two = (residual * inv_two * gain_two).astype(BF)

    rows_all = gather_tokens(normed_two)
    out_sum, row_sum = None, None
    in_grads, down_grads = [], []
    for e in range(EPD):
        weight_in, weight_down = expert_in[e], expert_down[e]
        part = shares[e][:, None]
        pre = dot(rows_all, weight_in)
        gate_pre, up_pre = pre[:, :hid], pre[:, hid:]
        sig = jax.nn.sigmoid(gate_pre)
        swish = gate_pre * sig
        act = (part * (swish * up_pre)).astype(BF)
        grad_inner = dot_nt(grads_all, weight_down) * part
        grad_gate = (grad_inner * up_pre * sig * (1.0 + gate_pre * (1.0 - sig))).astype(BF)
        grad_up = (grad_inner * swish).astype(BF)
        grad_pre = jnp.concatenate([grad_gate, grad_up], axis=1)
        out_part = dot(act, weight_down)
        row_part = dot_nt(grad_pre, weight_in)
        out_sum = out_part if e == 0 else out_sum + out_part
        row_sum = row_part if e == 0 else row_sum + row_part
        down_grads.append(dot_tn(act, grads_all).astype(BF))
        in_grads.append(dot_tn(rows_all, grad_pre).astype(BF))
    grad_normed_two = scatter_tokens(row_sum.astype(BF))
    output = residual + scatter_tokens(out_sum.astype(BF))

    def expert_grads(grad, rows):
        columns = grad.shape[1]
        block = 4 * rows

        def own(k):
            return lax.dynamic_slice(grad, (((z - k) % planes) * block, 0), (block, columns))

        total = own(1)
        for k in range(2, planes + 1):
            total = along(total, 1) + own(k % planes)
        total = all_reps(total)
        held = []
        for dy in range(2):
            for dc in range(2):
                shard = lax.dynamic_slice(
                    total, (((yb ^ dy) * 2 + (c ^ dc)) * rows, 0), (rows, columns)
                )
                held.append(shard if dy + dc == 0 else go(shard, 0, dy, dc))
        return held + [go(shard, 1, 0, 0) for shard in held]

    def expert_shards(grads, rows):
        columns = grads[0].shape[1]
        pieces, moves = [], []
        for e in range(EPD):
            for j, shard in enumerate(expert_grads(grads[e], rows)):
                pieces.append(shard)
                moves.append(
                    (len(pieces) - 1, (), ((mine ^ j) * EPD + e, 0, rows, 0, columns))
                )
        whole = place(pieces, moves, jax.ShapeDtypeStruct((EXP, rows, columns), BF))
        return whole.transpose(1, 0, 2).astype(F32)

    in_shards = expert_shards(in_grads, ds)
    down_shards = expert_shards(down_grads, hs)

    grad_out = cotangent.astype(F32)
    scaled_two = grad_normed_two * gain_two
    grad_resid = (
        grad_out
        + inv_two * scaled_two
        - residual * inv_two**3 * jnp.mean(scaled_two * residual, axis=1, keepdims=True)
    )
    grad_gain_two = jnp.sum(grad_normed_two * residual * inv_two, axis=0)
    grad_mixed = grad_resid.astype(BF)
    grad_out_w = dot_tn(attended, grad_mixed)
    context_grad = dot_nt(grad_mixed, out_w).astype(BF).reshape(length, KV_HEADS, group_size, HEAD)
    grad_probs = jnp.einsum("voua,zoa->ouvz", context_grad, value, preferred_element_type=F32)
    grad_value = (
        jnp.einsum("fxyq,yfxk->qfk", attn_probs.astype(BF), context_grad, preferred_element_type=F32)
        .astype(BF)
        .reshape(length, kvd)
    )
    inner_sum = jnp.sum(attn_probs * grad_probs, axis=3, keepdims=True)
    logit_grad = (attn_probs * (grad_probs - inner_sum)).astype(BF)
    grad_query_rot = (
        jnp.einsum("xkfq,qxb->fxkb", logit_grad, key_rotated, preferred_element_type=F32).reshape(
            length, HEADS, HEAD
        )
        * score_scale
    )
    grad_key_rot = (
        jnp.einsum("fxyq,yfxk->qfk", logit_grad, query_rotated, preferred_element_type=F32)
        * score_scale
    )
    grad_query = rotate_back(grad_query_rot, cosine_table, sine_table).astype(BF)
    grad_key = rotate_back(grad_key_rot, cosine_table, sine_table).astype(BF)
    grad_mix = jnp.concatenate(
        [grad_query.reshape(length, width), grad_key.reshape(length, kvd), grad_value], axis=1
    )
    grad_mix_w = dot_tn(normed, grad_mix)
    grad_normed = dot_nt(grad_mix, front[:, : width + 2 * kvd])
    scaled_one = grad_normed * gain_one
    input_grad = (
        grad_resid
        + inv_one * scaled_one
        - inputs * inv_one**3 * jnp.mean(scaled_one * inputs, axis=1, keepdims=True)
    )
    grad_gain_one = jnp.sum(grad_normed * inputs * inv_one, axis=0)
    out_shard = scatter_rows(grad_out_w.astype(BF))
    front_grad = jnp.concatenate(
        [
            grad_mix_w.astype(BF),
            grad_gain_one.astype(BF)[:, None],
            grad_gain_two.astype(BF)[:, None],
            jnp.zeros((width, 254), BF),
        ],
        axis=1,
    )
    front_shard = scatter_rows(front_grad)
    return (
        output,
        input_grad,
        front_shard[:, width + 2 * kvd],
        front_shard[:, :width],
        front_shard[:, width : width + kvd],
        front_shard[:, width + kvd : width + 2 * kvd],
        out_shard,
        front_shard[:, width + 2 * kvd + 1],
        in_shards[..., :hid],
        in_shards[..., hid:],
        down_shards,
    )


def solution(mesh):
    reps, group = mesh.shape["rep"], mesh.shape["fsdp"]
    both, one = P(AXES, None), P("fsdp")
    flat, deep = P("fsdp", None), P("fsdp", None, None)

    def whole(*args):
        return shards(reps, group, *args)

    return jax.shard_map(
        whole,
        mesh=mesh,
        in_specs=(both, both, both, both, P(AXES), one, flat, flat, flat, flat, one, deep, deep, deep),
        out_specs=(both, both, one, flat, flat, flat, flat, one, deep, deep, deep),
        check_vma=False,
    )
```

time: 1990 us -> 1060 us (0.53)
  waiting for transfers between devices: 1320 us -> 434 us
  starting transfers between devices: 0.62 us -> 116 us
  blocking collectives: 74.2 us -> 0 us
  other arithmetic: 112 us -> 59.1 us
  local copies, waits for them, and re-layouts: 205 us -> 163 us
  Pallas kernels: 0 us -> 31.3 us
    reduce_scatter x7 -> x0, waiting for transfers between devices: 836 us -> none  [the longest x1 247 us: shards(): lax.psum_scatter(grad_gate_w.astype(jnp.bfloat16), 'fsdp', scatter_dimens...]
    ppermute x0 -> x161, waiting for transfers between devices: none -> 434 us  [pp(): return lax.ppermute(value, AXES, perm(to))]
    all_gather x7 -> x0, waiting for transfers between devices: 396 us -> none  [the longest x1 112 us: shards(): lax.all_gather(w_gate.astype(jnp.bfloat16), 'fsdp', axis=0, tiled=True)]
    ppermute x0 -> x161, starting transfers between devices: none -> 116 us  [pp(): return lax.ppermute(value, AXES, perm(to))]
    convert_element_type x5 -> x4, local copies, waits for them, and re-layouts: 99.2 us -> 3.12 us  [the longest x1 1.7 us: shards(): dot_nt(grad_mixed, out_w).astype(BF)]
    psum x1 -> x0, waiting for transfers between devices: 83 us -> none  [shards(): lax.psum(query_slice.astype(jnp.bfloat16), 'rep').astype(jnp.float32)]
    gather x3 -> x0, local copies, waits for them, and re-layouts: 70.5 us -> none  [the longest x1 28.4 us: shards(): jnp.take(grad_rows, target, axis=0).reshape(length, top_k, model_width)]
    unnamed x2 -> x0, blocking collectives: 68.6 us -> none
  transfers between devices with their start and end apart: 15 -> 161, of which waited for: 11 -> 47; matrix products, arithmetic and copies ran while one was open for 18% -> 34% of each run, Pallas kernels for 0% -> 3%
where the time goes in v1:
time: 1060 us; the launch traced here: 1050 us
  waiting for transfers between devices  434 us (41%)
  matrix products  240 us (23%)
  local copies, waits for them, and re-layouts  163 us (15%)
  starting transfers between devices  116 us (11%)
  other arithmetic  59.1 us (6%)
  Pallas kernels  31.3 us (3%)
    ppermute x161, waiting for transfers between devices, pp(): return lax.ppermute(value, AXES, perm(to))  434 us
    ppermute x161, starting transfers between devices, pp(): return lax.ppermute(value, AXES, perm(to))  116 us
    unnamed x331, local copies, waits for them, and re-layouts  78.4 us
    dot_general x6, matrix products, dot_nt(): lax.dot_general(a, b, (((1,), (1,)), ((), ())), preferred_element_type=F32)  77.8 us
    dot_general x6, matrix products, dot(): return jnp.dot(a, b, preferred_element_type=F32)  61.6 us
    dot_general x6, matrix products, dot_tn(): lax.dot_general(a, b, (((0,), (0,)), ((), ())), preferred_element_type=F32)  55.5 us
    pallas_call x12, Pallas kernels, place(): pl.pallas_call(kernel, out_shape=out_shape, in_specs=[pl.BlockSpec(memory...  31.3 us
  transfers between devices with their start and end apart: 161, of which 47 were waited for; matrix products, arithmetic and copies ran while one was open for 34% of the time, Pallas kernels for 3%

profile of v1, /device:TPU:0, one launch (start us, length us, event | category | flops | bytes accessed | tf_op | source)
XLA Modules:
  0.0 1047.7 jit_solution(5526123402643502439)
XLA Ops:
  45.6 7.3 collective-permute-done.63.refs_3_
  75.4 6.2 collective-permute-done.28.refs_10_
  107.2 11.0 %collective-permute-done.87 = bf16[192,1536]{1,0:T(8,128)(2,1)} collective-permute-done((bf16[192,1536]{1,0:T(8,128)(2,1)}, bf16[192,1536]{1,0:T(8,128)(2,1)}, u32[]{:S(2)}, u32[]{:S(2)}) %collective-permute-start.87) | collective-permute-done | bytes 589856 | tf_op jit(solution)/shard_map/ppermute | solution.py:142
  121.3 7.0 collective-permute-done.91
  142.4 7.2 collective-permute-done.13.refs_12_
  150.1 11.7 %collective-permute-done.4.refs_2_ = bf16[384,768]{1,0:T(8,128)(2,1)S(1)} collective-permute-done((bf16[384,768]{1,0:T(8,128)(2,1)S(1)}, bf16[384,768]{1,0:T(8,128)(2,1)S(1)}, u32[]{:S(2)}, u32[]{:S(2)}) %collective-permute-start.4) | collective-permute-done | bytes 589856 | tf_op jit(solution)/shard_map/ppermute | solution.py:142
  176.0 35.0 %collective-permute-done.77.refs_2_ = bf16[128,1536]{1,0:T(8,128)(2,1)} collective-permute-done((bf16[128,1536]{1,0:T(8,128)(2,1)S(1)}, bf16[128,1536]{1,0:T(8,128)(2,1)}, u32[]{:S(2)}, u32[]{:S(2)}) %collective-permute-start.77) | collective-permute-done | bytes 393248 | tf_op jit(solution)/shard_map/ppermute | solution.py:142
  216.4 10.7 %collective-permute-done.94 = bf16[192,1536]{1,0:T(8,128)(2,1)S(1)} collective-permute-done((bf16[192,1536]{1,0:T(8,128)(2,1)S(1)}, bf16[192,1536]{1,0:T(8,128)(2,1)S(1)}, u32[]{:S(2)}, u32[]{:S(2)}) %collective-permute-start.94) | collective-permute-done | bytes 589856 | tf_op jit(solution)/shard_map/ppermute | solution.py:142
  227.8 10.8 %collective-permute-done.8.refs_6_ = bf16[384,768]{1,0:T(8,128)(2,1)S(1)} collective-permute-done((bf16[384,768]{1,0:T(8,128)(2,1)S(1)}, bf16[384,768]{1,0:T(8,128)(2,1)S(1)}, u32[]{:S(2)}, u32[]{:S(2)}) %collective-permute-start.8) | collective-permute-done | bytes 589856 | tf_op jit(solution)/shard_map/ppermute | solution.py:142
  246.8 6.1 shard_map.221
  273.2 10.8 %fusion.120 = (f32[8,3,384]{2,1,0:T(4,128)S(1)}, f32[8,3,384,384]{2,3,1,0:T(8,128)}) fusion(pred[384,384]{0,1:T(8,128)(4,1)} %fusion.52, bf16[384,8,3,32]{0,3,2,1:T(8,128)(2,1)} %bitcast.382, bf16[384,8,3,32]{0,3,2,1:T(8,128)(2,1)} %bitcast.378, bf16[384,8,32]{0,2,1:T(8,128)(2,1)} %get-tuple-element.132, bf16[384,8,32]{0,2,1:T(8,128)(2,1)S(1)} %get-tuple-element.131), kind=kOutput, calls=%fused_computation.364 | convolution fusion | flops 470286720 | bytes 15912960 | tf_op jit(solution)/shard_map/sub | solution.py:325
  284.0 8.4 fusion.35
  300.8 45.1 %collective-permute-done.66.refs_3_ = bf16[128,1536]{1,0:T(8,128)(2,1)S(1)} collective-permute-done((bf16[128,1536]{1,0:T(8,128)(2,1)}, bf16[128,1536]{1,0:T(8,128)(2,1)S(1)}, u32[]{:S(2)}, u32[]{:S(2)}) %collective-permute-start.66) | collective-permute-done | bytes 393248 | tf_op jit(solution)/shard_map/ppermute | solution.py:142
  363.6 6.0 collective-permute-done.43
  369.6 12.6 %collective-permute-done.44 = bf16[192,1536]{1,0:T(8,128)(2,1)S(1)} collective-permute-done((bf16[192,1536]{1,0:T(8,128)(2,1)S(1)}, bf16[192,1536]{1,0:T(8,128)(2,1)S(1)}, u32[]{:S(2)}, u32[]{:S(2)}) %collective-permute-start.44) | collective-permute-done | bytes 589856 | tf_op jit(solution)/shard_map/ppermute | solution.py:142
  388.2 6.0 collective-permute-done.51
  394.2 6.4 collective-permute-done.52
  406.6 15.2 %fusion.122 = f32[3072,1024]{0,1:T(8,128)} fusion(bf16[3072,1536]{1,0:T(8,128)(2,1)} %constant_dynamic-update-slice_fusion.8, bf16[1536,1024]{1,0:T(8,128)(2,1)S(1)} %shard_map.228), kind=kOutput, calls=%fused_computation.366 | convolution fusion | flops 9663676416 | bytes 25165824 | tf_op jit(solution)/shard_map/dot_general | solution.py:58
  421.9 15.1 %multiply_convert_fusion.1 = (bf16[3072,512]{0,1:T(8,128)(2,1)}, bf16[3072,512]{0,1:T(8,128)(2,1)}, bf16[3072,512]{0,1:T(8,128)(2,1)}) fusion(f32[3072,1024]{0,1:T(8,128)} %fusion.122, f32[3072]{0:T(1024)S(1)} %bitcast.400, bf16[3072,1536]{1,0:T(8,128)(2,1)} %constant_dynamic-update-slice_fusion.23, bf16[512,1536]{1,0:T(8,128)(2,1)S(1)} %shard_map.230), kind=kOutput, calls=%fused_computation.25 | convolution fusion | flops 4858576896 | bytes 33042432 | tf_op jit(solution)/shard_map/dot_general | solution.py:62
  437.0 9.5 convolution_convert_fusion.2
  446.5 9.5 fusion.123
  456.0 14.2 %fusion.20 = bf16[1536,1024]{1,0:T(8,128)(2,1)S(1)} fusion(bf16[3072,1536]{1,0:T(8,128)(2,1)} %constant_dynamic-update-slice_fusion.8, bf16[3072,512]{0,1:T(8,128)(2,1)} %get-tuple-element.79, bf16[3072,512]{0,1:T(8,128)(2,1)} %get-tuple-element.78), kind=kOutput, calls=%fused_computation.68 | convolution fusion | flops 9677832192 | bytes 18874368 | tf_op jit(solution)/shard_map/dot_general | solution.py:66
  470.3 16.9 %fusion.17 = f32[3072,1536]{1,0:T(8,128)} fusion(bf16[1536,1024]{1,0:T(8,128)(2,1)S(1)} %shard_map.228, bf16[3072,512]{0,1:T(8,128)(2,1)} %get-tuple-element.79, bf16[3072,512]{0,1:T(8,128)(2,1)} %get-tuple-element.78), kind=kOutput, calls=%fused_computation.65 | convolution fusion | flops 9676259328 | bytes 28311552 | tf_op jit(solution)/shard_map/dot_general | solution.py:62
  487.3 15.5 %fusion.121 = f32[3072,1024]{0,1:T(8,128)} fusion(bf16[3072,1536]{1,0:T(8,128)(2,1)} %constant_dynamic-update-slice_fusion.8, bf16[1536,1024]{1,0:T(8,128)(2,1)S(1)} %shard_map.224), kind=kOutput, calls=%fused_computation.365 | convolution fusion | flops 9663676416 | bytes 25165824 | tf_op jit(solution)/shard_map/dot_general | solution.py:58
  502.9 14.9 %multiply_convert_fusion.3 = (bf16[3072,512]{0,1:T(8,128)(2,1)}, bf16[3072,512]{0,1:T(8,128)(2,1)}, bf16[3072,512]{0,1:T(8,128)(2,1)}) fusion(f32[3072,1024]{0,1:T(8,128)} %fusion.121, f32[3072]{0:T(1024)S(1)} %bitcast.399, bf16[3072,1536]{1,0:T(8,128)(2,1)} %constant_dynamic-update-slice_fusion.23, bf16[512,1536]{1,0:T(8,128)(2,1)S(1)} %shard_map.226), kind=kOutput, calls=%fused_computation.27 | convolution fusion | flops 4858576896 | bytes 33042432 | tf_op jit(solution)/shard_map/dot_general | solution.py:62
  517.8 6.6 convolution_convert_fusion.3
  527.0 14.2 %fusion.19 = bf16[1536,1024]{1,0:T(8,128)(2,1)S(1)} fusion(bf16[3072,1536]{1,0:T(8,128)(2,1)} %constant_dynamic-update-slice_fusion.8, bf16[3072,512]{0,1:T(8,128)(2,1)} %get-tuple-element.77, bf16[3072,512]{0,1:T(8,128)(2,1)} %get-tuple-element.76), kind=kOutput, calls=%fused_computation.67 | convolution fusion | flops 9677832192 | bytes 18874368 | tf_op jit(solution)/shard_map/dot_general | solution.py:66
  547.3 10.2 add_convert_fusion.1
  562.5 19.0 %add_convert_fusion = bf16[3072,1536]{1,0:T(8,128)(2,1)} fusion(f32[3072,1536]{1,0:T(8,128)} %fusion.17, bf16[1536,1024]{1,0:T(8,128)(2,1)} %copy-done.3, bf16[3072,512]{0,1:T(8,128)(2,1)} %get-tuple-element.77, bf16[3072,512]{0,1:T(8,128)(2,1)} %get-tuple-element.76), kind=kOutput, calls=%fused_computation.1 | convolution fusion | flops 9685696512 | bytes 37748736 | tf_op jit(solution)/shard_map/dot_general | solution.py:62
  591.6 9.4 collective-permute-done.152
  601.1 8.3 collective-permute-done.142
  609.5 41.1 %collective-permute-done.153 = bf16[128,1536]{1,0:T(8,128)(2,1)S(1)} collective-permute-done((bf16[128,1536]{1,0:T(8,128)(2,1)S(1)}, bf16[128,1536]{1,0:T(8,128)(2,1)S(1)}, u32[]{:S(2)}, u32[]{:S(2)}) %collective-permute-start.153) | collective-permute-done | bytes 393248 | tf_op jit(solution)/shard_map/ppermute | solution.py:142
  651.8 10.8 %collective-permute-done.143 = bf16[128,1536]{1,0:T(8,128)(2,1)S(1)} collective-permute-done((bf16[128,1536]{1,0:T(8,128)(2,1)S(1)}, bf16[128,1536]{1,0:T(8,128)(2,1)S(1)}, u32[]{:S(2)}, u32[]{:S(2)}) %collective-permute-start.143) | collective-permute-done | bytes 393248 | tf_op jit(solution)/shard_map/ppermute | solution.py:142
  665.0 17.5 %collective-permute-done.133 = bf16[384,1024]{1,0:T(8,128)(2,1)S(1)} collective-permute-done((bf16[384,1024]{1,0:T(8,128)(2,1)S(1)}, bf16[384,1024]{1,0:T(8,128)(2,1)S(1)}, u32[]{:S(2)}, u32[]{:S(2)}) %collective-permute-start.133) | collective-permute-done | bytes 786464 | tf_op jit(solution)/shard_map/ppermute | solution.py:142
  695.5 19.3 %collective-permute-done.80 = bf16[2,192,1536]{2,1,0:T(8,128)(2,1)S(1)} collective-permute-done((bf16[2,192,1536]{2,1,0:T(8,128)(2,1)S(1)}, bf16[2,192,1536]{2,1,0:T(8,128)(2,1)S(1)}, u32[]{:S(2)}, u32[]{:S(2)}) %collective-permute-start.80) | collective-permute-done | bytes 1179680 | tf_op jit(solution)/shard_map/ppermute | solution.py:142
  715.9 21.7 %collective-permute-done.101 = bf16[2,192,1536]{2,1,0:T(8,128)(2,1)S(1)} collective-permute-done((bf16[2,192,1536]{2,1,0:T(8,128)(2,1)S(1)}, bf16[2,192,1536]{2,1,0:T(8,128)(2,1)S(1)}, u32[]{:S(2)}, u32[]{:S(2)}) %collective-permute-start.101) | collective-permute-done | bytes 1179680 | tf_op jit(solution)/shard_map/ppermute | solution.py:142
  740.9 14.3 %collective-permute-done.100 = bf16[192,1536]{1,0:T(8,128)(2,1)S(1)} collective-permute-done((bf16[192,1536]{1,0:T(8,128)(2,1)S(1)}, bf16[192,1536]{1,0:T(8,128)(2,1)S(1)}, u32[]{:S(2)}, u32[]{:S(2)}) %collective-permute-start.100) | collective-permute-done | bytes 589856 | tf_op jit(solution)/shard_map/ppermute | solution.py:142
  756.3 9.9 collective-permute-done.81
  775.0 12.7 %fusion.1 = (f32[8,3,384]{2,1,0:T(4,128)S(1)}, f32[8,384,384,3]{2,1,3,0:T(8,128)}) fusion(f32[8,3,384,384]{2,3,1,0:T(8,128)} %get-tuple-element.172, f32[8,3,384]{2,1,0:T(4,128)S(1)} %copy-done.106, bf16[384,8,64,1]{0,2,3,1:T(8,128)(2,1)S(1)} %bitcast.394, bf16[384,8,3,64]{0,3,2,1:T(8,128)(2,1)S(1)} %bitcast.387), kind=kOutput, calls=%fused_computation.5 | convolution fusion | flops 463592448 | bytes 29958144 | tf_op jit(solution)/shard_map/voua,zoa->ouvz/dot_general | solution.py:407
  789.3 6.8 fusion.3
  801.4 8.1 fusion.43
  812.0 8.9 fusion.32
  820.9 8.1 convolution_convert_fusion
  830.5 13.2 %concatenate.102 = bf16[4,2,2,96,2816]{4,3,2,1,0:T(8,128)(2,1)} concatenate(bf16[4,2,2,96,2560]{4,3,2,1,0:T(8,128)(2,1)} %bitcast.370, bf16[4,2,2,96,1]{4,3,2,1,0:T(8,128)(2,1)S(1)} %convert_element_type.343, bf16[4,2,2,96,1]{4,3,2,1,0:T(8,128)(2,1)S(1)} %convert_element_type.344, bf16[4,2,2,96,254]{4,3,2,1,0:T(8,128)(2,1)S(1)} %broadcast_in_dim.35), dimensions={4} | concatenate | bytes 17301504 | tf_op jit(solution)/shard_map/concatenate | solution.py:440
  954.1 7.0 reshape.277
  974.8 28.9 %collective-permute-done.116 = bf16[4,96,384]{2,1,0:T(8,128)(2,1)S(1)} collective-permute-done((bf16[4,96,384]{2,1,0:T(8,128)(2,1)S(1)}, bf16[4,96,384]{2,1,0:T(8,128)(2,1)S(1)}, u32[]{:S(2)}, u32[]{:S(2)}) %collective-permute-start.116) | collective-permute-done | bytes 294944 | tf_op jit(solution)/shard_map/ppermute | solution.py:142
  1022.6 6.3 collective-permute-done.108
  1028.9 9.1 collective-permute-done.109
  (792 shorter events, 412.7 us)
Async XLA Ops:
  70.7 29.0 %collective-permute-start.84 = (bf16[192,1536]{1,0:T(8,128)(2,1)}, bf16[192,1536]{1,0:T(8,128)(2,1)}, u32[]{:S(2)}, u32[]{:S(2)}) collective-permute-start(bf16[192,1536]{1,0:T(8,128)(2,1)} %get-tuple-element.121), channel_id=1, source_target_pairs={{0,1},{1,0},{2,3},{3,2},{4,5},{5,4},{6,7},{7,6},{8,9},{9,8},{10,11... | collective-permute-start | bytes 1769480 | tf_op jit(solution)/shard_map/ppermute | solution.py:142
  90.3 27.9 %collective-permute-start.87 = (bf16[192,1536]{1,0:T(8,128)(2,1)}, bf16[192,1536]{1,0:T(8,128)(2,1)}, u32[]{:S(2)}, u32[]{:S(2)}) collective-permute-start(bf16[192,1536]{1,0:T(8,128)(2,1)} %get-tuple-element.120), channel_id=1, source_target_pairs={{0,2},{1,3},{2,0},{3,1},{4,6},{5,7},{6,4},{7,5},{8,10},{9,11},{10,... | collective-permute-start | bytes 1769480 | tf_op jit(solution)/shard_map/ppermute | solution.py:142
  99.7 28.6 %collective-permute-start.91 = (bf16[192,1536]{1,0:T(8,128)(2,1)}, bf16[192,1536]{1,0:T(8,128)(2,1)S(1)}, u32[]{:S(2)}, u32[]{:S(2)}) collective-permute-start(bf16[192,1536]{1,0:T(8,128)(2,1)} %get-tuple-element.120), channel_id=1, source_target_pairs={{0,16},{1,17},{2,18},{3,19},{4,20},{5,21},{6,22},{7,23},{8,24},{9,... | collective-permute-start | bytes 1769480 | tf_op jit(solution)/shard_map/ppermute | solution.py:142
  105.6 27.3 %collective-permute-start.32 = (bf16[384,384]{1,0:T(8,128)(2,1)S(1)}, bf16[384,384]{1,0:T(8,128)(2,1)S(1)}, u32[]{:S(2)}, u32[]{:S(2)}) collective-permute-start(bf16[384,384]{1,0:T(8,128)(2,1)S(1)} %collective-permute-done.28.refs_10_), channel_id=1, source_target_pairs={{0,16},{1,17},{2,18},{3,19},{4,20},{5,21},{6,22},{7,23},{8,24},{9,... | collective-permute-start | bytes 884744 | tf_op jit(solution)/shard_map/ppermute | solution.py:142
  163.8 47.6 %collective-permute-start.70 = (bf16[384,1024]{1,0:T(8,128)(2,1)S(1)}, bf16[384,1024]{1,0:T(8,128)(2,1)}, u32[]{:S(2)}, u32[]{:S(2)}) collective-permute-start(bf16[384,1024]{1,0:T(8,128)(2,1)S(1)} %shard_map.227.refs_0_), channel_id=1, source_target_pairs={{0,4},{1,5},{2,6},{3,7},{4,8},{5,9},{6,10},{7,11},{8,12},{9,13},{1... | collective-permute-start | bytes 2359304 | tf_op jit(solution)/shard_map/ppermute | solution.py:142
  163.8 47.6 %collective-permute-start.58 = (bf16[384,1024]{1,0:T(8,128)(2,1)S(1)}, bf16[384,1024]{1,0:T(8,128)(2,1)}, u32[]{:S(2)}, u32[]{:S(2)}) collective-permute-start(bf16[384,1024]{1,0:T(8,128)(2,1)S(1)} %shard_map.223.refs_0_), channel_id=1, source_target_pairs={{0,4},{1,5},{2,6},{3,7},{4,8},{5,9},{6,10},{7,11},{8,12},{9,13},{1... | collective-permute-start | bytes 2359304 | tf_op jit(solution)/shard_map/ppermute | solution.py:142
  167.2 44.9 %collective-permute-start.89 = (bf16[192,1536]{1,0:T(8,128)(2,1)}, bf16[192,1536]{1,0:T(8,128)(2,1)S(1)}, u32[]{:S(2)}, u32[]{:S(2)}) collective-permute-start(bf16[192,1536]{1,0:T(8,128)(2,1)} %collective-permute-done.87), channel_id=1, source_target_pairs={{0,1},{1,0},{2,3},{3,2},{4,5},{5,4},{6,7},{7,6},{8,9},{9,8},{10,11... | collective-permute-start | bytes 1769480 | tf_op jit(solution)/shard_map/ppermute | solution.py:142
  167.2 45.0 %collective-permute-start.92 = (bf16[192,1536]{1,0:T(8,128)(2,1)S(1)}, bf16[192,1536]{1,0:T(8,128)(2,1)S(1)}, u32[]{:S(2)}, u32[]{:S(2)}) collective-permute-start(bf16[192,1536]{1,0:T(8,128)(2,1)S(1)} %collective-permute-done.90), channel_id=1, source_target_pairs={{0,1},{1,0},{2,3},{3,2},{4,5},{5,4},{6,7},{7,6},{8,9},{9,8},{10,11... | collective-permute-start | bytes 1769480 | tf_op jit(solution)/shard_map/ppermute | solution.py:142
  169.7 41.3 %collective-permute-start.77 = (bf16[128,1536]{1,0:T(8,128)(2,1)S(1)}, bf16[128,1536]{1,0:T(8,128)(2,1)}, u32[]{:S(2)}, u32[]{:S(2)}) collective-permute-start(bf16[128,1536]{1,0:T(8,128)(2,1)S(1)} %copy-done.6), channel_id=1, source_target_pairs={{0,4},{1,5},{2,6},{3,7},{4,8},{5,9},{6,10},{7,11},{8,12},{9,13},{1... | collective-permute-start | bytes 1179656 | tf_op jit(solution)/shard_map/ppermute | solution.py:142
  241.2 57.4 %collective-permute-start.65 = (bf16[128,1536]{1,0:T(8,128)(2,1)S(1)}, bf16[128,1536]{1,0:T(8,128)(2,1)}, u32[]{:S(2)}, u32[]{:S(2)}) collective-permute-start(bf16[128,1536]{1,0:T(8,128)(2,1)S(1)} %copy-done.9), channel_id=1, source_target_pairs={{0,4},{1,5},{2,6},{3,7},{4,8},{5,9},{6,10},{7,11},{8,12},{9,13},{1... | collective-permute-start | bytes 1179656 | tf_op jit(solution)/shard_map/ppermute | solution.py:142
  241.3 59.0 %collective-permute-start.95 = (bf16[192,1536]{1,0:T(8,128)(2,1)}, bf16[192,1536]{1,0:T(8,128)(2,1)}, u32[]{:S(2)}, u32[]{:S(2)}) collective-permute-start(bf16[192,1536]{1,0:T(8,128)(2,1)} %collective-permute-done.87), channel_id=1, source_target_pairs={{0,16},{1,17},{2,18},{3,19},{4,20},{5,21},{6,22},{7,23},{8,24},{9,... | collective-permute-start | bytes 1769480 | tf_op jit(solution)/shard_map/ppermute | solution.py:142
  241.9 58.8 %collective-permute-start.78 = (bf16[128,1536]{1,0:T(8,128)(2,1)}, bf16[128,1536]{1,0:T(8,128)(2,1)}, u32[]{:S(2)}, u32[]{:S(2)}) collective-permute-start(bf16[128,1536]{1,0:T(8,128)(2,1)} %collective-permute-done.77.refs_2_), channel_id=1, source_target_pairs={{0,4},{1,5},{2,6},{3,7},{4,8},{5,9},{6,10},{7,11},{8,12},{9,13},{1... | collective-permute-start | bytes 1179656 | tf_op jit(solution)/shard_map/ppermute | solution.py:142
  241.9 56.8 %collective-permute-start.71 = (bf16[384,1024]{1,0:T(8,128)(2,1)}, bf16[384,1024]{1,0:T(8,128)(2,1)}, u32[]{:S(2)}, u32[]{:S(2)}) collective-permute-start(bf16[384,1024]{1,0:T(8,128)(2,1)} %collective-permute-done.70.refs_1_), channel_id=1, source_target_pairs={{0,4},{1,5},{2,6},{3,7},{4,8},{5,9},{6,10},{7,11},{8,12},{9,13},{1... | collective-permute-start | bytes 2359304 | tf_op jit(solution)/shard_map/ppermute | solution.py:142
  242.4 56.4 %collective-permute-start.59 = (bf16[384,1024]{1,0:T(8,128)(2,1)}, bf16[384,1024]{1,0:T(8,128)(2,1)}, u32[]{:S(2)}, u32[]{:S(2)}) collective-permute-start(bf16[384,1024]{1,0:T(8,128)(2,1)} %collective-permute-done.58.refs_1_), channel_id=1, source_target_pairs={{0,4},{1,5},{2,6},{3,7},{4,8},{5,9},{6,10},{7,11},{8,12},{9,13},{1... | collective-permute-start | bytes 2359304 | tf_op jit(solution)/shard_map/ppermute | solution.py:142
  298.6 47.3 %collective-permute-start.96 = (bf16[192,1536]{1,0:T(8,128)(2,1)S(1)}, bf16[192,1536]{1,0:T(8,128)(2,1)S(1)}, u32[]{:S(2)}, u32[]{:S(2)}) collective-permute-start(bf16[192,1536]{1,0:T(8,128)(2,1)S(1)} %copy-done.92), channel_id=1, source_target_pairs={{0,1},{1,0},{2,3},{3,2},{4,5},{5,4},{6,7},{7,6},{8,9},{9,8},{10,11... | collective-permute-start | bytes 1769480 | tf_op jit(solution)/shard_map/ppermute | solution.py:142
  298.7 55.3 %collective-permute-start.72 = (bf16[384,1024]{1,0:T(8,128)(2,1)}, bf16[384,1024]{1,0:T(8,128)(2,1)S(1)}, u32[]{:S(2)}, u32[]{:S(2)}) collective-permute-start(bf16[384,1024]{1,0:T(8,128)(2,1)} %collective-permute-done.71.refs_2_), channel_id=1, source_target_pairs={{0,4},{1,5},{2,6},{3,7},{4,8},{5,9},{6,10},{7,11},{8,12},{9,13},{1... | collective-permute-start | bytes 2359304 | tf_op jit(solution)/shard_map/ppermute | solution.py:142
  298.8 55.1 %collective-permute-start.60 = (bf16[384,1024]{1,0:T(8,128)(2,1)}, bf16[384,1024]{1,0:T(8,128)(2,1)S(1)}, u32[]{:S(2)}, u32[]{:S(2)}) collective-permute-start(bf16[384,1024]{1,0:T(8,128)(2,1)} %collective-permute-done.59.refs_2_), channel_id=1, source_target_pairs={{0,4},{1,5},{2,6},{3,7},{4,8},{5,9},{6,10},{7,11},{8,12},{9,13},{1... | collective-permute-start | bytes 2359304 | tf_op jit(solution)/shard_map/ppermute | solution.py:142
  300.3 45.6 %collective-permute-start.66 = (bf16[128,1536]{1,0:T(8,128)(2,1)}, bf16[128,1536]{1,0:T(8,128)(2,1)S(1)}, u32[]{:S(2)}, u32[]{:S(2)}) collective-permute-start(bf16[128,1536]{1,0:T(8,128)(2,1)} %collective-permute-done.65.refs_2_), channel_id=1, source_target_pairs={{0,4},{1,5},{2,6},{3,7},{4,8},{5,9},{6,10},{7,11},{8,12},{9,13},{1... | collective-permute-start | bytes 1179656 | tf_op jit(solution)/shard_map/ppermute | solution.py:142
  300.7 52.7 %collective-permute-start.97 = (bf16[192,1536]{1,0:T(8,128)(2,1)}, bf16[192,1536]{1,0:T(8,128)(2,1)S(1)}, u32[]{:S(2)}, u32[]{:S(2)}) collective-permute-start(bf16[192,1536]{1,0:T(8,128)(2,1)} %collective-permute-done.95), channel_id=1, source_target_pairs={{0,1},{1,0},{2,3},{3,2},{4,5},{5,4},{6,7},{7,6},{8,9},{9,8},{10,11... | collective-permute-start | bytes 1769480 | tf_op jit(solution)/shard_map/ppermute | solution.py:142
  354.0 28.3 %collective-permute-start.44 = (bf16[192,1536]{1,0:T(8,128)(2,1)S(1)}, bf16[192,1536]{1,0:T(8,128)(2,1)S(1)}, u32[]{:S(2)}, u32[]{:S(2)}) collective-permute-start(bf16[192,1536]{1,0:T(8,128)(2,1)S(1)} %get-tuple-element.122), channel_id=1, source_target_pairs={{0,2},{1,3},{2,0},{3,1},{4,6},{5,7},{6,4},{7,5},{8,10},{9,11},{10,... | collective-permute-start | bytes 1769480 | tf_op jit(solution)/shard_map/ppermute | solution.py:142
  361.9 39.5 %collective-permute-start.49 = (bf16[192,1536]{1,0:T(8,128)(2,1)S(1)}, bf16[192,1536]{1,0:T(8,128)(2,1)S(1)}, u32[]{:S(2)}, u32[]{:S(2)}) collective-permute-start(bf16[192,1536]{1,0:T(8,128)(2,1)S(1)} %collective-permute-done.47), channel_id=1, source_target_pairs={{0,1},{1,0},{2,3},{3,2},{4,5},{5,4},{6,7},{7,6},{8,9},{9,8},{10,11... | collective-permute-start | bytes 1769480 | tf_op jit(solution)/shard_map/ppermute | solution.py:142
  363.1 31.1 %collective-permute-start.51 = (bf16[192,1536]{1,0:T(8,128)(2,1)S(1)}, bf16[192,1536]{1,0:T(8,128)(2,1)S(1)}, u32[]{:S(2)}, u32[]{:S(2)}) collective-permute-start(bf16[192,1536]{1,0:T(8,128)(2,1)S(1)} %collective-permute-done.47), channel_id=1, source_target_pairs={{0,2},{1,3},{2,0},{3,1},{4,6},{5,7},{6,4},{7,5},{8,10},{9,11},{10,... | collective-permute-start | bytes 1769480 | tf_op jit(solution)/shard_map/ppermute | solution.py:142
  487.2 99.3 %collective-permute-start.151 = (bf16[128,1536]{1,0:T(8,128)(2,1)S(1)}, bf16[128,1536]{1,0:T(8,128)(2,1)S(1)}, u32[]{:S(2)}, u32[]{:S(2)}) collective-permute-start(bf16[128,1536]{1,0:T(8,128)(2,1)S(1)} %constant_dynamic-slice_fusion.4), channel_id=1, source_target_pairs={{0,4},{1,5},{2,6},{3,7},{4,8},{5,9},{6,10},{7,11},{8,12},{9,13},{1... | collective-permute-start | bytes 1179656 | tf_op jit(solution)/shard_map/ppermute | solution.py:142
  525.3 61.9 %collective-permute-start.141 = (bf16[128,1536]{1,0:T(8,128)(2,1)}, bf16[128,1536]{1,0:T(8,128)(2,1)}, u32[]{:S(2)}, u32[]{:S(2)}) collective-permute-start(bf16[128,1536]{1,0:T(8,128)(2,1)} %constant_dynamic-slice_fusion.9), channel_id=1, source_target_pairs={{0,4},{1,5},{2,6},{3,7},{4,8},{5,9},{6,10},{7,11},{8,12},{9,13},{1... | collective-permute-start | bytes 1179656 | tf_op jit(solution)/shard_map/ppermute | solution.py:142
  526.2 62.4 %collective-permute-start.131 = (bf16[384,1024]{1,0:T(8,128)(2,1)}, bf16[384,1024]{1,0:T(8,128)(2,1)}, u32[]{:S(2)}, u32[]{:S(2)}) collective-permute-start(bf16[384,1024]{1,0:T(8,128)(2,1)} %constant_dynamic-slice_fusion.14), channel_id=1, source_target_pairs={{0,4},{1,5},{2,6},{3,7},{4,8},{5,9},{6,10},{7,11},{8,12},{9,13},{1... | collective-permute-start | bytes 2359304 | tf_op jit(solution)/shard_map/ppermute | solution.py:142
  543.1 47.1 %collective-permute-start.121 = (bf16[384,1024]{1,0:T(8,128)(2,1)}, bf16[384,1024]{1,0:T(8,128)(2,1)S(1)}, u32[]{:S(2)}, u32[]{:S(2)}) collective-permute-start(bf16[384,1024]{1,0:T(8,128)(2,1)} %constant_dynamic-slice_fusion.19), channel_id=1, source_target_pairs={{0,4},{1,5},{2,6},{3,7},{4,8},{5,9},{6,10},{7,11},{8,12},{9,13},{1... | collective-permute-start | bytes 2359304 | tf_op jit(solution)/shard_map/ppermute | solution.py:142
  562.5 120.3 %collective-permute-start.79 = (bf16[2,2,384,1536]{3,2,1,0:T(8,128)(2,1)}, bf16[2,2,384,1536]{3,2,1,0:T(8,128)(2,1)}, u32[]{:S(2)}, u32[]{:S(2)}) collective-permute-start(bf16[2,2,384,1536]{3,2,1,0:T(8,128)(2,1)} %slice_bitcast_fusion.2), channel_id=1, source_target_pairs={{0,1},{1,0},{2,3},{3,2},{4,5},{5,4},{6,7},{7,6},{8,9},{9,8},{10,11... | collective-permute-start | bytes 14155784 | tf_op jit(solution)/shard_map/ppermute | solution.py:142
  586.5 100.7 %collective-permute-start.98 = (bf16[2,2,384,1536]{3,2,1,0:T(8,128)(2,1)}, bf16[2,2,384,1536]{3,2,1,0:T(8,128)(2,1)}, u32[]{:S(2)}, u32[]{:S(2)}) collective-permute-start(bf16[2,2,384,1536]{3,2,1,0:T(8,128)(2,1)} %slice_bitcast_fusion), channel_id=1, source_target_pairs={{0,1},{1,0},{2,3},{3,2},{4,5},{5,4},{6,7},{7,6},{8,9},{9,8},{10,11... | collective-permute-start | bytes 14155784 | tf_op jit(solution)/shard_map/ppermute | solution.py:142
  590.2 61.3 %collective-permute-start.132 = (bf16[384,1024]{1,0:T(8,128)(2,1)S(1)}, bf16[384,1024]{1,0:T(8,128)(2,1)S(1)}, u32[]{:S(2)}, u32[]{:S(2)}) collective-permute-start(bf16[384,1024]{1,0:T(8,128)(2,1)S(1)} %dynamic-slice_add_fusion.2), channel_id=1, source_target_pairs={{0,4},{1,5},{2,6},{3,7},{4,8},{5,9},{6,10},{7,11},{8,12},{9,13},{1... | collective-permute-start | bytes 2359304 | tf_op jit(solution)/shard_map/ppermute | solution.py:142
  601.0 62.8 %collective-permute-start.122 = (bf16[384,1024]{1,0:T(8,128)(2,1)S(1)}, bf16[384,1024]{1,0:T(8,128)(2,1)S(1)}, u32[]{:S(2)}, u32[]{:S(2)}) collective-permute-start(bf16[384,1024]{1,0:T(8,128)(2,1)S(1)} %dynamic-slice_add_fusion.5), channel_id=1, source_target_pairs={{0,4},{1,5},{2,6},{3,7},{4,8},{5,9},{6,10},{7,11},{8,12},{9,13},{1... | collective-permute-start | bytes 2359304 | tf_op jit(solution)/shard_map/ppermute | solution.py:142
  609.4 41.2 %collective-permute-start.153 = (bf16[128,1536]{1,0:T(8,128)(2,1)S(1)}, bf16[128,1536]{1,0:T(8,128)(2,1)S(1)}, u32[]{:S(2)}, u32[]{:S(2)}) collective-permute-start(bf16[128,1536]{1,0:T(8,128)(2,1)S(1)} %dynamic-slice_add_fusion.7), channel_id=1, source_target_pairs={{0,4},{1,5},{2,6},{3,7},{4,8},{5,9},{6,10},{7,11},{8,12},{9,13},{1... | collective-permute-start | bytes 1179656 | tf_op jit(solution)/shard_map/ppermute | solution.py:142
  651.5 192.3 %collective-permute-start.154 = (bf16[32,1536]{1,0:T(8,128)(2,1)}, bf16[32,1536]{1,0:T(8,128)(2,1)S(1)}, u32[]{:S(2)}, u32[]{:S(2)}) collective-permute-start(bf16[32,1536]{1,0:T(8,128)(2,1)} %get-tuple-element.148), channel_id=1, source_target_pairs={{0,1},{1,0},{2,3},{3,2},{4,5},{5,4},{6,7},{7,6},{8,9},{9,8},{10,11... | collective-permute-start | bytes 294920 | tf_op jit(solution)/shard_map/ppermute | solution.py:142
  685.9 29.0 %collective-permute-start.80 = (bf16[2,192,1536]{2,1,0:T(8,128)(2,1)S(1)}, bf16[2,192,1536]{2,1,0:T(8,128)(2,1)S(1)}, u32[]{:S(2)}, u32[]{:S(2)}) collective-permute-start(bf16[2,192,1536]{2,1,0:T(8,128)(2,1)S(1)} %slice_bitcast_fusion.10), channel_id=1, source_target_pairs={{0,2},{1,3},{2,0},{3,1},{4,6},{5,7},{6,4},{7,5},{8,10},{9,11},{10,... | collective-permute-start | bytes 3538952 | tf_op jit(solution)/shard_map/ppermute | solution.py:142
  686.6 29.0 %collective-permute-start.82 = (bf16[2,192,1536]{2,1,0:T(8,128)(2,1)S(1)}, bf16[2,192,1536]{2,1,0:T(8,128)(2,1)S(1)}, u32[]{:S(2)}, u32[]{:S(2)}) collective-permute-start(bf16[2,192,1536]{2,1,0:T(8,128)(2,1)S(1)} %slice_bitcast_fusion.8), channel_id=1, source_target_pairs={{0,16},{1,17},{2,18},{3,19},{4,20},{5,21},{6,22},{7,23},{8,24},{9,... | collective-permute-start | bytes 3538952 | tf_op jit(solution)/shard_map/ppermute | solution.py:142
  691.5 46.1 %collective-permute-start.101 = (bf16[2,192,1536]{2,1,0:T(8,128)(2,1)S(1)}, bf16[2,192,1536]{2,1,0:T(8,128)(2,1)S(1)}, u32[]{:S(2)}, u32[]{:S(2)}) collective-permute-start(bf16[2,192,1536]{2,1,0:T(8,128)(2,1)S(1)} %slice_bitcast_fusion.4), channel_id=1, source_target_pairs={{0,16},{1,17},{2,18},{3,19},{4,20},{5,21},{6,22},{7,23},{8,24},{9,... | collective-permute-start | bytes 3538952 | tf_op jit(solution)/shard_map/ppermute | solution.py:142
  693.1 47.0 %collective-permute-start.99 = (bf16[2,192,1536]{2,1,0:T(8,128)(2,1)S(1)}, bf16[2,192,1536]{2,1,0:T(8,128)(2,1)S(1)}, u32[]{:S(2)}, u32[]{:S(2)}) collective-permute-start(bf16[2,192,1536]{2,1,0:T(8,128)(2,1)S(1)} %slice_bitcast_fusion.6), channel_id=1, source_target_pairs={{0,2},{1,3},{2,0},{3,1},{4,6},{5,7},{6,4},{7,5},{8,10},{9,11},{10,... | collective-permute-start | bytes 3538952 | tf_op jit(solution)/shard_map/ppermute | solution.py:142
  714.9 129.0 %collective-permute-start.155 = (bf16[32,1536]{1,0:T(8,128)(2,1)}, bf16[32,1536]{1,0:T(8,128)(2,1)S(1)}, u32[]{:S(2)}, u32[]{:S(2)}) collective-permute-start(bf16[32,1536]{1,0:T(8,128)(2,1)} %get-tuple-element.147), channel_id=1, source_target_pairs={{0,2},{1,3},{2,0},{3,1},{4,6},{5,7},{6,4},{7,5},{8,10},{9,11},{10,... | collective-permute-start | bytes 294920 | tf_op jit(solution)/shard_map/ppermute | solution.py:142
  715.5 133.1 %collective-permute-start.156 = (bf16[32,1536]{1,0:T(8,128)(2,1)}, bf16[32,1536]{1,0:T(8,128)(2,1)S(1)}, u32[]{:S(2)}, u32[]{:S(2)}) collective-permute-start(bf16[32,1536]{1,0:T(8,128)(2,1)} %get-tuple-element.146), channel_id=1, source_target_pairs={{0,3},{1,2},{2,1},{3,0},{4,7},{5,6},{6,5},{7,4},{8,11},{9,10},{10,... | collective-permute-start | bytes 294920 | tf_op jit(solution)/shard_map/ppermute | solution.py:142
  766.1 84.1 %collective-permute-start.157 = (bf16[32,1536]{1,0:T(8,128)(2,1)S(1)}, bf16[32,1536]{1,0:T(8,128)(2,1)S(1)}, u32[]{:S(2)}, u32[]{:S(2)}) collective-permute-start(bf16[32,1536]{1,0:T(8,128)(2,1)S(1)} %get-tuple-element.149.refs_8_), channel_id=1, source_target_pairs={{0,16},{1,17},{2,18},{3,19},{4,20},{5,21},{6,22},{7,23},{8,24},{9,... | collective-permute-start | bytes 294920 | tf_op jit(solution)/shard_map/ppermute | solution.py:142
  766.3 86.0 %collective-permute-start.144 = (bf16[32,1536]{1,0:T(8,128)(2,1)}, bf16[32,1536]{1,0:T(8,128)(2,1)S(1)}, u32[]{:S(2)}, u32[]{:S(2)}) collective-permute-start(bf16[32,1536]{1,0:T(8,128)(2,1)} %get-tuple-element.152), channel_id=1, source_target_pairs={{0,1},{1,0},{2,3},{3,2},{4,5},{5,4},{6,7},{7,6},{8,9},{9,8},{10,11... | collective-permute-start | bytes 294920 | tf_op jit(solution)/shard_map/ppermute | solution.py:142
  852.4 95.7 %collective-permute-start.103 = (bf16[4,2,96,2816]{3,2,1,0:T(8,128)(2,1)}, bf16[4,2,96,2816]{3,2,1,0:T(8,128)(2,1)}, u32[]{:S(2)}, u32[]{:S(2)}) collective-permute-start(bf16[4,2,96,2816]{3,2,1,0:T(8,128)(2,1)} %dynamic-slice_bitcast_fusion), channel_id=1, source_target_pairs={{0,1},{1,0},{2,3},{3,2},{4,5},{5,4},{6,7},{7,6},{8,9},{9,8},{10,11... | collective-permute-start | bytes 12976136 | tf_op jit(solution)/shard_map/ppermute | solution.py:142
  866.5 66.4 %collective-permute-start.112 = (bf16[4,2,96,1536]{3,2,1,0:T(8,128)(2,1)}, bf16[4,2,96,1536]{3,2,1,0:T(8,128)(2,1)}, u32[]{:S(2)}, u32[]{:S(2)}) collective-permute-start(bf16[4,2,96,1536]{3,2,1,0:T(8,128)(2,1)} %dynamic-slice_bitcast_fusion.1), channel_id=1, source_target_pairs={{0,1},{1,0},{2,3},{3,2},{4,5},{5,4},{6,7},{7,6},{8,9},{9,8},{10,11... | collective-permute-start | bytes 7077896 | tf_op jit(solution)/shard_map/ppermute | solution.py:142
  943.4 28.0 %collective-permute-start.115 = (bf16[4,2,96,384]{3,2,1,0:T(8,128)(2,1)S(1)}, bf16[4,2,96,384]{3,2,1,0:T(8,128)(2,1)}, u32[]{:S(2)}, u32[]{:S(2)}) collective-permute-start(bf16[4,2,96,384]{3,2,1,0:T(8,128)(2,1)S(1)} %bitcast.392), channel_id=1, source_target_pairs={{0,16},{1,17},{2,18},{3,19},{4,20},{5,21},{6,22},{7,23},{8,24},{9,... | collective-permute-start | bytes 1769480 | tf_op jit(solution)/shard_map/ppermute | solution.py:142
  946.8 27.2 %collective-permute-start.113 = (bf16[4,96,2,384]{3,1,2,0:T(8,128)(2,1)}, bf16[4,96,2,384]{3,1,2,0:T(8,128)(2,1)S(1)}, u32[]{:S(2)}, u32[]{:S(2)}) collective-permute-start(bf16[4,96,2,384]{3,1,2,0:T(8,128)(2,1)} %bitcast.355), channel_id=1, source_target_pairs={{0,2},{1,3},{2,0},{3,1},{4,6},{5,7},{6,4},{7,5},{8,10},{9,11},{10,... | collective-permute-start | bytes 1769480 | tf_op jit(solution)/shard_map/ppermute | solution.py:142
  967.3 36.4 %collective-permute-start.106 = (bf16[4,2,96,640]{3,2,1,0:T(8,128)(2,1)S(1)}, bf16[4,2,96,640]{3,2,1,0:T(8,128)(2,1)S(1)}, u32[]{:S(2)}, u32[]{:S(2)}) collective-permute-start(bf16[4,2,96,640]{3,2,1,0:T(8,128)(2,1)S(1)} %bitcast.391), channel_id=1, source_target_pairs={{0,16},{1,17},{2,18},{3,19},{4,20},{5,21},{6,22},{7,23},{8,24},{9,... | collective-permute-start | bytes 2949128 | tf_op jit(solution)/shard_map/ppermute | solution.py:142
  970.6 34.0 %collective-permute-start.104 = (bf16[4,96,2,768]{3,1,2,0:T(8,128)(2,1)S(1)}, bf16[4,96,2,768]{3,1,2,0:T(8,128)(2,1)S(1)}, u32[]{:S(2)}, u32[]{:S(2)}) collective-permute-start(bf16[4,96,2,768]{3,1,2,0:T(8,128)(2,1)S(1)} %bitcast.386), channel_id=1, source_target_pairs={{0,2},{1,3},{2,0},{3,1},{4,6},{5,7},{6,4},{7,5},{8,10},{9,11},{10,... | collective-permute-start | bytes 3538952 | tf_op jit(solution)/shard_map/ppermute | solution.py:142
  972.6 31.1 %collective-permute-start.116 = (bf16[4,96,384]{2,1,0:T(8,128)(2,1)S(1)}, bf16[4,96,384]{2,1,0:T(8,128)(2,1)S(1)}, u32[]{:S(2)}, u32[]{:S(2)}) collective-permute-start(bf16[4,96,384]{2,1,0:T(8,128)(2,1)S(1)} %dynamic-slice_bitcast_fusion.4), channel_id=1, source_target_pairs={{0,2},{1,3},{2,0},{3,1},{4,6},{5,7},{6,4},{7,5},{8,10},{9,11},{10,... | collective-permute-start | bytes 884744 | tf_op jit(solution)/shard_map/ppermute | solution.py:142
  974.1 31.2 %collective-permute-start.114 = (bf16[4,96,384]{2,1,0:T(8,128)(2,1)S(1)}, bf16[4,96,384]{2,1,0:T(8,128)(2,1)S(1)}, u32[]{:S(2)}, u32[]{:S(2)}) collective-permute-start(bf16[4,96,384]{2,1,0:T(8,128)(2,1)S(1)} %dynamic-slice_bitcast_fusion.5), channel_id=1, source_target_pairs={{0,16},{1,17},{2,18},{3,19},{4,20},{5,21},{6,22},{7,23},{8,24},{9,... | collective-permute-start | bytes 884744 | tf_op jit(solution)/shard_map/ppermute | solution.py:142
  (260 other events, 4188.1 us)

commit v2 on v1

--- a/solution.py
+++ b/solution.py
@@ -106,6 +106,435 @@
         scratch_shapes=[pltpu.SemaphoreType.DMA((len(plan),))],
         compiler_params=pltpu.CompilerParams(vmem_limit_bytes=40 * 2**20),
     )(jnp.stack(scalars), *pieces)
+
+
+def add_rows(store, terms, rows, step=32):
+    step = min(step, rows)
+
+    @pl.loop(0, rows // step)
+    def _(n):
+        chunk = pl.ds(pl.multiple_of(n * step, 16), step)
+        total = terms[0](chunk).astype(F32)
+        for term in terms[1:]:
+            total = total + term(chunk).astype(F32)
+        store(chunk, total)
+
+
+class Links:
+    def __init__(self, planes, group, send_sems, recv_sems):
+        r, f = lax.axis_index("rep"), lax.axis_index("fsdp")
+        self.xb, self.yb, self.c, self.z = r % 2, (f // 2) % 2, f % 2, f // 4
+        self.x = (r + 1 - 2 * self.xb, f)
+        self.y = (r, f + 2 - 4 * self.yb)
+        self.core = (r, f + 1 - 2 * self.c)
+        self.along = [None] + [(r, (f + 4 * k) % group) for k in range(1, planes)]
+        self.planes, self.send_sems, self.recv_sems, self.copies = planes, send_sems, recv_sems, []
+
+    def barrier(self, devices):
+        semaphore = pltpu.get_barrier_semaphore()
+        for device in devices:
+            pl.semaphore_signal(
+                semaphore, inc=1, device_id=device, device_id_type=pl.DeviceIdType.MESH
+            )
+        pl.semaphore_wait(semaphore, len(devices))
+
+    def send(self, src, dst, device):
+        n = len(self.copies)
+        copy = pltpu.make_async_remote_copy(
+            src_ref=src,
+            dst_ref=dst,
+            send_sem=self.send_sems.at[n],
+            recv_sem=self.recv_sems.at[n],
+            device_id=device,
+            device_id_type=pl.DeviceIdType.MESH,
+        )
+        copy.start()
+        self.copies.append(copy)
+        return copy
+
+    def finish(self):
+        for copy in self.copies:
+            copy.wait_send()
+
+
+def comm_params(number):
+    return pltpu.CompilerParams(
+        collective_id=number, has_side_effects=True, vmem_limit_bytes=56 * 2**20
+    )
+
+
+def dma_pairs(count):
+    return [pltpu.SemaphoreType.DMA((count,)), pltpu.SemaphoreType.DMA((count,))]
+
+
+def whole_vmem():
+    return pl.BlockSpec(memory_space=pltpu.VMEM)
+
+
+def anywhere():
+    return pl.BlockSpec(memory_space=pl.ANY)
+
+
+def split_half(half):
+    return (half // 128 + 1) // 2 * 128
+
+
+def gather_front(own, planes, group):
+    ds, half = own.shape
+    part = split_half(half)
+    first, second, every = (0, part), (part, half - part), (0, half)
+
+    def kernel(own_ref, out_ref, send_sems, recv_sems, local_sem):
+        at = Links(planes, group, send_sems, recv_sems)
+
+        def region(k, dx, dy, span):
+            row = (((at.z + planes - k) % planes) * 4 + (at.yb + dy) % 2 * 2 + at.c) * ds
+            col = (at.xb + dx) % 2 * half + span[0]
+            return out_ref.at[
+                pl.ds(pl.multiple_of(row, 16), ds), pl.ds(pl.multiple_of(col, 128), span[1])
+            ]
+
+        def pass_on(k, dx, dy, span, device):
+            here = region(k, dx, dy, span)
+            return at.send(here, here, device)
+
+        at.barrier([at.x, at.y, at.core] + at.along[1:])
+        local = pltpu.make_async_copy(own_ref, region(0, 0, 0, every), local_sem)
+        local.start()
+        arrive = [None] + [
+            at.send(own_ref, region(0, 0, 0, every), at.along[k]) for k in range(1, planes)
+        ]
+        to_core = [at.send(own_ref, region(0, 0, 0, every), at.core)]
+        x_first, x_second, y_first, y_second, diagonal = [], [], [], [], []
+
+        def spread(k):
+            for device, span, copies in (
+                (at.x, first, x_first),
+                (at.y, second, y_second),
+                (at.x, second, x_second),
+                (at.y, first, y_first),
+            ):
+                here = region(k, 0, 0, span)
+                src = own_ref.at[:, pl.ds(span[0], span[1])] if k == 0 else here
+                copies.append(at.send(src, here, device))
+            if k > 0:
+                to_core.append(pass_on(k, 0, 0, every, at.core))
+
+        def forward(k):
+            x_first[k].wait_recv()
+            diagonal.append((k, first, pass_on(k, 1, 0, first, at.y)))
+            y_second[k].wait_recv()
+            diagonal.append((k, second, pass_on(k, 0, 1, second, at.x)))
+            x_second[k].wait_recv()
+            to_core.append(pass_on(k, 1, 0, every, at.core))
+            y_first[k].wait_recv()
+            to_core.append(pass_on(k, 0, 1, every, at.core))
+
+        for k in range(planes):
+            if k > 0:
+                arrive[k].wait_recv()
+            spread(k)
+            if k > 0:
+                forward(k - 1)
+        forward(planes - 1)
+        for k, span, copy in diagonal:
+            copy.wait_recv()
+            to_core.append(pass_on(k, 1, 1, span, at.core))
+        for copy in to_core:
+            copy.wait_recv()
+        local.wait()
+        at.finish()
+
+    count = planes - 1 + planes * 4 + planes * 2 + planes * 5
+    return pl.pallas_call(
+        kernel,
+        out_shape=jax.ShapeDtypeStruct((planes * 4 * ds, 2 * half), BF),
+        in_specs=[whole_vmem()],
+        out_specs=anywhere(),
+        scratch_shapes=dma_pairs(count) + [pltpu.SemaphoreType.DMA],
+        compiler_params=comm_params(0),
+        cost_estimate=pl.CostEstimate(
+            flops=50_000_000_000, bytes_accessed=20_000_000, transcendentals=0
+        ),
+    )(own)
+
+
+def gather_plane(own, planes, group):
+    length, width = own.shape
+    half = length // 2
+    first, second = pl.ds(0, half), pl.ds(half, half)
+
+    def kernel(own_ref, out_ref, send_sems, recv_sems, local_sem):
+        at = Links(planes, group, send_sems, recv_sems)
+        at.barrier([at.x, at.y, at.core])
+
+        def slot(j, rows=pl.ds(0, length)):
+            return out_ref.at[j, rows]
+
+        x_first = at.send(own_ref.at[first], slot(4, first), at.x)
+        y_second = at.send(own_ref.at[second], slot(2, second), at.y)
+        x_second = at.send(own_ref.at[second], slot(4, second), at.x)
+        y_first = at.send(own_ref.at[first], slot(2, first), at.y)
+        cores = [at.send(own_ref, slot(1), at.core)]
+        local = pltpu.make_async_copy(own_ref, slot(0), local_sem)
+        local.start()
+        x_first.wait_recv()
+        far_first = at.send(slot(4, first), slot(6, first), at.y)
+        cores.append(at.send(slot(4, first), slot(5, first), at.core))
+        y_second.wait_recv()
+        far_second = at.send(slot(2, second), slot(6, second), at.x)
+        cores.append(at.send(slot(2, second), slot(3, second), at.core))
+        x_second.wait_recv()
+        cores.append(at.send(slot(4, second), slot(5, second), at.core))
+        y_first.wait_recv()
+        cores.append(at.send(slot(2, first), slot(3, first), at.core))
+        far_first.wait_recv()
+        cores.append(at.send(slot(6, first), slot(7, first), at.core))
+        far_second.wait_recv()
+        cores.append(at.send(slot(6, second), slot(7, second), at.core))
+        for copy in cores:
+            copy.wait_recv()
+        local.wait()
+        at.finish()
+
+    return pl.pallas_call(
+        kernel,
+        out_shape=jax.ShapeDtypeStruct((PLANE, length, width), BF),
+        in_specs=[whole_vmem()],
+        out_specs=anywhere(),
+        scratch_shapes=dma_pairs(13) + [pltpu.SemaphoreType.DMA],
+        compiler_params=comm_params(1),
+        cost_estimate=pl.CostEstimate(
+            flops=45_000_000_000, bytes_accessed=20_000_000, transcendentals=0
+        ),
+    )(own)
+
+
+def scatter_plane(partial, planes, group):
+    slots, length, width = partial.shape
+    half = length // 2
+    first, second = pl.ds(0, half), pl.ds(half, half)
+
+    def kernel(p_ref, out_ref, from_core, kept, far, near, send_sems, recv_sems):
+        at = Links(planes, group, send_sems, recv_sems)
+        at.barrier([at.x, at.y, at.core])
+        order = (3, 2, 1, 0)
+        arrive = {
+            j: at.send(p_ref.at[2 * j + 1], from_core.at[j], at.core) for j in order
+        }
+
+        def add_core(j):
+            arrive[j].wait_recv()
+
+            def store(chunk, total):
+                kept[j, chunk] = total.astype(BF)
+
+            add_rows(store, [lambda q: p_ref[2 * j, q], lambda q: from_core[j, q]], length)
+
+        def add_far(j, n, base):
+            def store(chunk, total):
+                kept[j, pl.ds(pl.multiple_of(chunk.start + base, 16), chunk.size)] = total.astype(BF)
+
+            add_rows(
+                store,
+                [
+                    lambda q: kept[j, pl.ds(pl.multiple_of(q.start + base, 16), q.size)],
+                    lambda q: far[n, q],
+                ],
+                half,
+            )
+
+        add_core(3)
+        far_y = at.send(kept.at[3, first], far.at[0], at.y)
+        far_x = at.send(kept.at[3, second], far.at[1], at.x)
+        add_core(2)
+        x_second = at.send(kept.at[2, second], near.at[0, second], at.x)
+        add_core(1)
+        y_first = at.send(kept.at[1, first], near.at[1, first], at.y)
+        far_y.wait_recv()
+        add_far(2, 0, 0)
+        x_first = at.send(kept.at[2, first], near.at[0, first], at.x)
+        far_x.wait_recv()
+        add_far(1, 1, half)
+        y_second = at.send(kept.at[1, second], near.at[1, second], at.y)
+        arrive[0].wait_recv()
+        for copy in (x_second, y_first, x_first, y_second):
+            copy.wait_recv()
+
+        def store(chunk, total):
+            out_ref[chunk] = total
+
+        add_rows(
+            store,
+            [
+                lambda q: p_ref[0, q],
+                lambda q: from_core[0, q],
+                lambda q: near[0, q],
+                lambda q: near[1, q],
+            ],
+            length,
+        )
+        at.finish()
+
+    return pl.pallas_call(
+        kernel,
+        out_shape=jax.ShapeDtypeStruct((length, width), F32),
+        in_specs=[whole_vmem()],
+        out_specs=whole_vmem(),
+        scratch_shapes=[
+            pltpu.VMEM((4, length, width), BF),
+            pltpu.VMEM((4, length, width), BF),
+            pltpu.VMEM((2, half, width), BF),
+            pltpu.VMEM((2, length, width), BF),
+        ]
+        + dma_pairs(10),
+        compiler_params=comm_params(2),
+        cost_estimate=pl.CostEstimate(
+            flops=45_000_000_000, bytes_accessed=20_000_000, transcendentals=0
+        ),
+    )(partial)
+
+
+def scatter_front(grad, planes, group):
+    rows, columns = grad.shape
+    ds, half = rows // (4 * planes), columns // 2
+    part = split_half(half)
+    first, second = pl.ds(0, part), pl.ds(part, half - part)
+
+    def kernel(
+        g_ref, out_ref, from_core, kept, far_a, far_b, near_x, near_y, total_ref, from_z, send_sems, recv_sems
+    ):
+        at = Links(planes, group, send_sems, recv_sems)
+        at.barrier([at.x, at.y, at.core] + at.along[1:])
+
+        def row(k, dy, core):
+            owner = ((at.z + k) % planes) * 4 + (at.yb + dy) % 2 * 2 + core
+            return pl.multiple_of(owner * ds, 16)
+
+        def column(dx):
+            return pl.ds(pl.multiple_of((at.xb + dx) % 2 * half, 128), half)
+
+        order = list(range(1, planes)) + [0]
+        arrive = {}
+        for k in order:
+            for dy in (1, 0):
+                arrive[k, dy] = at.send(
+                    g_ref.at[pl.ds(row(k, dy, 1 - at.c), ds)], from_core.at[k, dy], at.core
+                )
+        step = 16
+        x_second, y_first, x_first, y_second, to_x, to_y = {}, {}, {}, {}, {}, {}
+        for k in order:
+            for dy in (1, 0):
+                arrive[k, dy].wait_recv()
+                for dx in (1, 0):
+
+                    def store(chunk, total, k=k, dx=dx, dy=dy):
+                        kept[k, dx, dy, chunk] = total.astype(BF)
+
+                    add_rows(
+                        store,
+                        [
+                            lambda q, k=k, dx=dx, dy=dy: g_ref[
+                                pl.ds(pl.multiple_of(row(k, dy, at.c) + q.start, 16), q.size),
+                                column(dx),
+                            ],
+                            lambda q, k=k, dx=dx, dy=dy: from_core[k, dy, q, column(dx)],
+                        ],
+                        ds,
+                        step,
+                    )
+                    if (dx, dy) == (1, 1):
+                        to_y[k] = at.send(kept.at[k, 1, 1, :, first], far_a.at[k], at.y)
+                        to_x[k] = at.send(kept.at[k, 1, 1, :, second], far_b.at[k], at.x)
+                    elif (dx, dy) == (0, 1):
+                        y_first[k] = at.send(
+                            kept.at[k, 0, 1, :, first], near_y.at[k, :, first], at.y
+                        )
+                    elif (dx, dy) == (1, 0):
+                        x_second[k] = at.send(
+                            kept.at[k, 1, 0, :, second], near_x.at[k, :, second], at.x
+                        )
+        for k in order:
+            to_y[k].wait_recv()
+
+            def store(chunk, total, k=k):
+                kept[k, 1, 0, chunk, first] = total.astype(BF)
+
+            add_rows(
+                store,
+                [lambda q, k=k: kept[k, 1, 0, q, first], lambda q, k=k: far_a[k, q]],
+                ds,
+                step,
+            )
+            x_first[k] = at.send(kept.at[k, 1, 0, :, first], near_x.at[k, :, first], at.x)
+            to_x[k].wait_recv()
+
+            def store(chunk, total, k=k):
+                kept[k, 0, 1, chunk, second] = total.astype(BF)
+
+            add_rows(
+                store,
+                [lambda q, k=k: kept[k, 0, 1, q, second], lambda q, k=k: far_b[k, q]],
+                ds,
+                step,
+            )
+            y_second[k] = at.send(kept.at[k, 0, 1, :, second], near_y.at[k, :, second], at.y)
+        arrive_z = {}
+        for k in order:
+            for copies in (x_second, y_first, x_first, y_second):
+                copies[k].wait_recv()
+
+            def store(chunk, total, k=k):
+                total_ref[k, chunk] = total.astype(BF)
+
+            add_rows(
+                store,
+                [
+                    lambda q, k=k: kept[k, 0, 0, q],
+                    lambda q, k=k: near_x[k, q],
+                    lambda q, k=k: near_y[k, q],
+                ],
+                ds,
+                step,
+            )
+            if k > 0:
+                arrive_z[k] = at.send(total_ref.at[k], from_z.at[k], at.along[k])
+        for k in range(1, planes):
+            arrive_z[k].wait_recv()
+
+        def store(chunk, total):
+            out_ref[chunk] = total.astype(BF)
+
+        add_rows(
+            store,
+            [lambda q: total_ref[0, q]]
+            + [lambda q, k=k: from_z[k, q] for k in range(1, planes)],
+            ds,
+            step,
+        )
+        at.finish()
+
+    return pl.pallas_call(
+        kernel,
+        out_shape=jax.ShapeDtypeStruct((ds, half), BF),
+        in_specs=[whole_vmem()],
+        out_specs=whole_vmem(),
+        scratch_shapes=[
+            pltpu.VMEM((planes, 2, ds, columns), BF),
+            pltpu.VMEM((planes, 2, 2, ds, half), BF),
+            pltpu.VMEM((planes, ds, part), BF),
+            pltpu.VMEM((planes, ds, half - part), BF),
+            pltpu.VMEM((planes, ds, half), BF),
+            pltpu.VMEM((planes, ds, half), BF),
+            pltpu.VMEM((planes, ds, half), BF),
+            pltpu.VMEM((planes, ds, half), BF),
+        ]
+        + dma_pairs(planes * 8 + planes - 1),
+        compiler_params=comm_params(3),
+        cost_estimate=pl.CostEstimate(
+            flops=50_000_000_000, bytes_accessed=20_000_000, transcendentals=0
+        ),
+    )(grad)
 
 
 def shards(
@@ -163,76 +592,13 @@
     score_scale = 1.0 / math.sqrt(HEAD)
     half_rows = length // 2
 
-    def split_axes(columns):
-        half = columns // 2
-        part = (half // 128 + 1) // 2 * 128
-        return half, part
-
-    def gather_rows(own):
-        columns = own.shape[1]
-        half, part = split_axes(columns)
-        send = lax.dynamic_slice(own, (0, xb * half), (ds, half))
-        stack = jnp.concatenate([send] + [along(send, k) for k in range(1, planes)], axis=0)
-        a, b = stack[:, :part], stack[:, part:]
-        ax, by = go(a, 1, 0, 0), go(b, 0, 1, 0)
-        a_all = {(0, 0): a, (1, 0): ax, (0, 1): go(a, 0, 1, 0), (1, 1): go(ax, 0, 1, 0)}
-        b_all = {(0, 0): b, (0, 1): by, (1, 0): go(b, 1, 0, 0), (1, 1): go(by, 1, 0, 0)}
-        pieces, moves = [], []
-        for held, col, cols in ((a_all, 0, part), (b_all, part, half - part)):
-            for (dx, dy), piece in held.items():
-                for dc in range(2):
-                    pieces.append(piece if dc == 0 else go(piece, 0, 0, 1))
-                    for k in range(planes):
-                        owner = ((z - k) % planes) * 4 + (yb ^ dy) * 2 + (c ^ dc)
-                        moves.append(
-                            (
-                                len(pieces) - 1,
-                                (pl.ds(k * ds, ds),),
-                                (None, owner * ds, ds, (xb ^ dx) * half + col, cols),
-                            )
-                        )
-        return place(pieces, moves, jax.ShapeDtypeStruct((width, columns), BF))
-
-    def scatter_rows(grad):
-        columns = grad.shape[1]
-        half, part = split_axes(columns)
-        by_core = grad.reshape(planes, 2, 2, ds, columns)
-
-        def pick(value, index, axis):
-            return lax.dynamic_index_in_dim(value, index, axis, keepdims=False)
-
-        kept = pick(by_core, c, 2) + go(pick(by_core, 1 - c, 2), 0, 0, 1)
-        kept = kept.reshape(planes, 2, ds, 2, half)
-        a, b = kept[..., :part], kept[..., part:]
-        a = pick(a, yb, 1) + go(pick(a, 1 - yb, 1), 0, 1, 0)
-        b = pick(b, xb, 3) + go(pick(b, 1 - xb, 3), 1, 0, 0)
-        a = pick(a, xb, 2) + go(pick(a, 1 - xb, 2), 1, 0, 0)
-        b = pick(b, yb, 1) + go(pick(b, 1 - yb, 1), 0, 1, 0)
-        both = jnp.concatenate([a, b], axis=2)
-        total = pick(both, z, 0).astype(F32)
-        for k in range(1, planes):
-            total = total + along(pick(both, (z + k) % planes, 0), k).astype(F32)
-        total = all_reps(total.astype(BF))
-        other = go(total, 1, 0, 0)
-        return jnp.where(
-            xb == 0,
-            jnp.concatenate([total, other], axis=1),
-            jnp.concatenate([other, total], axis=1),
-        ).astype(F32)
-
     def gather_tokens(own):
-        a, b = own[:half_rows], own[half_rows:]
-        ax, by = go(a, 1, 0, 0), go(b, 0, 1, 0)
-        a_all = {(0, 0): a, (1, 0): ax, (0, 1): go(a, 0, 1, 0), (1, 1): go(ax, 0, 1, 0)}
-        b_all = {(0, 0): b, (0, 1): by, (1, 0): go(b, 1, 0, 0), (1, 1): go(by, 1, 0, 0)}
-        parts = []
-        for dx in range(2):
-            for dy in range(2):
-                for dc in range(2):
-                    for held in (a_all, b_all):
-                        piece = held[(dx, dy)]
-                        parts.append(piece if dc == 0 else go(piece, 0, 0, 1))
-        return jnp.concatenate(parts, axis=0)
+        a, b = slice(0, half_rows), slice(half_rows, length)
+        x, y = go(own, 1, 0, 0), go(own, 0, 1, 0)
+        far_a, far_b = go(x[a], 0, 1, 0), go(y[b], 1, 0, 0)
+        slots = [own, go(own, 0, 0, 1), y, go(y, 0, 0, 1), x, go(x, 0, 0, 1)]
+        slots += [far_a, far_b, go(far_a, 0, 0, 1), go(far_b, 0, 0, 1)]
+        return jnp.concatenate(slots, axis=0)
 
     def scatter_tokens(partial):
         slots = partial.reshape(2, 2, 2, length, width)
@@ -244,50 +610,77 @@
         b = b[0].astype(F32) + go(b[1], 0, 1, 0).astype(F32)
         return jnp.concatenate([a, b], axis=0)
 
-    pad = jnp.zeros((ds, 254), BF)
-    front = jnp.concatenate(
+    mix = width + 2 * kvd
+    columns = mix + width + 256
+    half = columns // 2
+    gains = jnp.stack([norm1_gain.astype(BF), norm2_gain.astype(BF)], axis=1)
+    front_own = jnp.concatenate(
         [
             w_query.astype(BF),
             w_key.astype(BF),
             w_value.astype(BF),
-            norm1_gain.astype(BF)[:, None],
-            norm2_gain.astype(BF)[:, None],
-            pad,
+            w_out.astype(BF),
+            gains,
+            jnp.zeros((ds, 254), BF),
         ],
         axis=1,
     )
-    front = gather_rows(front)
-    out_w = gather_rows(w_out.astype(BF))
-
-    gate_up = jnp.concatenate([w_gate.astype(BF), w_up.astype(BF)], axis=2).transpose(1, 0, 2)
-    down = w_down.astype(BF).transpose(1, 0, 2)
-
-    def expert_weights(source, e, rows):
-        columns = source.shape[2]
-        pieces, moves = [], []
-        for dy in range(2):
-            for dc in range(2):
-                target = (mine ^ (dy * 2 + dc)) * EPD + e
-                block = lax.dynamic_index_in_dim(source, target, 0, keepdims=False)
-                pieces.append(block if dy + dc == 0 else go(block, 0, dy, dc))
-                moves.append(
-                    (
-                        len(pieces) - 1,
-                        (),
-                        (None, ((yb ^ dy) * 2 + (c ^ dc)) * rows, rows, 0, columns),
-                    )
-                )
-        piece = place(pieces, moves, jax.ShapeDtypeStruct((4 * rows, columns), BF))
-        ring, moves = [piece], [(0, (), (None, z * 4 * rows, 4 * rows, 0, columns))]
+    front = gather_front(lax.dynamic_slice(front_own, (0, xb * half), (ds, half)), planes, group)
+    out_w = front[:, mix : mix + width]
+
+    blocks = width // hid
+    packed = jnp.concatenate(
+        [
+            w_gate.astype(BF).transpose(1, 0, 2),
+            w_up.astype(BF).transpose(1, 0, 2),
+            w_down.astype(BF)
+            .reshape(hs, EXP, blocks, hid)
+            .transpose(1, 2, 0, 3)
+            .reshape(EXP, ds, hid),
+        ],
+        axis=2,
+    )
+    packs = []
+    for dy in range(2):
+        for dc in range(2):
+            block = lax.dynamic_slice(
+                packed, ((mine ^ (dy * 2 + dc)) * EPD, 0, 0), (EPD, ds, 3 * hid)
+            )
+            packs.append(block if dy + dc == 0 else go(block, 0, dy, dc))
+
+    def expert_weights(e):
+        moves = []
+        for i in range(4):
+            moves.append(
+                (i, (e,), (None, ((yb ^ (i // 2)) * 2 + (c ^ (i % 2))) * ds, ds, 0, 3 * hid))
+            )
+        ring = [place(packs, moves, jax.ShapeDtypeStruct((4 * ds, 3 * hid), BF))]
         for k in range(1, planes):
             ring.append(along(ring[-1], 1))
+        moves, down_moves = [], []
+        for k in range(planes):
             moves.append(
-                (k, (), (None, ((z - k) % planes) * 4 * rows, 4 * rows, 0, columns))
-            )
-        return place(ring, moves, jax.ShapeDtypeStruct((planes * 4 * rows, columns), BF))
-
-    expert_in = [expert_weights(gate_up, e, ds) for e in range(EPD)]
-    expert_down = [expert_weights(down, e, hs) for e in range(EPD)]
+                (
+                    k,
+                    (slice(None), pl.ds(0, 2 * hid)),
+                    (None, ((z - k) % planes) * 4 * ds, 4 * ds, 0, 2 * hid),
+                )
+            )
+            for i in range(4):
+                for n in range(blocks):
+                    down_moves.append(
+                        (
+                            k,
+                            (pl.ds(i * ds + n * hs, hs), pl.ds(2 * hid, hid)),
+                            (None, (((z - k) % planes) * 4 + i) * hs, hs, n * hid, hid),
+                        )
+                    )
+        return (
+            place(ring, moves, jax.ShapeDtypeStruct((width, 2 * hid), BF)),
+            place(ring, down_moves, jax.ShapeDtypeStruct((hid, width), BF)),
+        )
+
+    weights = [expert_weights(e) for e in range(EPD)]
 
     experts = jnp.arange(EXP, dtype=jnp.int32)[:, None, None]
     share = jnp.sum(jnp.where(routes[None] == experts, gates[None], 0.0), axis=2)
@@ -300,11 +693,11 @@
     grads_all = gather_tokens(cotangent)
 
     inputs = tokens.astype(F32)
-    gain_one = front[:, 2560].astype(F32)[None, :]
-    gain_two = front[:, 2561].astype(F32)[None, :]
+    gain_one = front[:, mix + width].astype(F32)[None, :]
+    gain_two = front[:, mix + width + 1].astype(F32)[None, :]
     inv_one = lax.rsqrt(jnp.mean(inputs * inputs, axis=1, keepdims=True) + EPSILON)
     normed = (inputs * inv_one * gain_one).astype(BF)
-    mixed = dot(normed, front[:, : width + 2 * kvd])
+    mixed = dot(normed, front[:, :mix])
     query_raw = mixed[:, :width].reshape(length, HEADS, HEAD)
     key_raw = mixed[:, width : width + kvd].reshape(length, KV_HEADS, HEAD)
     value = mixed[:, width + kvd :].astype(BF).reshape(length, KV_HEADS, HEAD)
@@ -334,11 +727,11 @@
     inv_two = lax.rsqrt(jnp.mean(residual * residual, axis=1, keepdims=True) + EPSILON)
     normed_two = (residual * inv_two * gain_two).astype(BF)
 
-    rows_all = gather_tokens(normed_two)
+    rows_all = gather_plane(normed_two, planes, group).reshape(PLANE * length, width)
     out_sum, row_sum = None, None
-    in_grads, down_grads = [], []
+    pack_grads = []
     for e in range(EPD):
-        weight_in, weight_down = expert_in[e], expert_down[e]
+        weight_in, weight_down = weights[e]
         part = shares[e][:, None]
         pre = dot(rows_all, weight_in)
         gate_pre, up_pre = pre[:, :hid], pre[:, hid:]
@@ -353,17 +746,22 @@
         row_part = dot_nt(grad_pre, weight_in)
         out_sum = out_part if e == 0 else out_sum + out_part
         row_sum = row_part if e == 0 else row_sum + row_part
-        down_grads.append(dot_tn(act, grads_all).astype(BF))
-        in_grads.append(dot_tn(rows_all, grad_pre).astype(BF))
-    grad_normed_two = scatter_tokens(row_sum.astype(BF))
+        down_grad = dot_tn(act, grads_all).astype(BF)
+        in_grad = dot_tn(rows_all, grad_pre).astype(BF)
+        down_grad = (
+            down_grad.reshape(group, hs, blocks, hid).transpose(0, 2, 1, 3).reshape(width, hid)
+        )
+        pack_grads.append(jnp.concatenate([in_grad, down_grad], axis=1))
+    grad_normed_two = scatter_plane(
+        row_sum.astype(BF).reshape(PLANE, length, width), planes, group
+    )
     output = residual + scatter_tokens(out_sum.astype(BF))
 
-    def expert_grads(grad, rows):
-        columns = grad.shape[1]
-        block = 4 * rows
+    def expert_grads(grad):
+        block = 4 * ds
 
         def own(k):
-            return lax.dynamic_slice(grad, (((z - k) % planes) * block, 0), (block, columns))
+            return lax.dynamic_slice(grad, (((z - k) % planes) * block, 0), (block, 3 * hid))
 
         total = own(1)
         for k in range(2, planes + 1):
@@ -373,25 +771,34 @@
         for dy in range(2):
             for dc in range(2):
                 shard = lax.dynamic_slice(
-                    total, (((yb ^ dy) * 2 + (c ^ dc)) * rows, 0), (rows, columns)
+                    total, (((yb ^ dy) * 2 + (c ^ dc)) * ds, 0), (ds, 3 * hid)
                 )
                 held.append(shard if dy + dc == 0 else go(shard, 0, dy, dc))
-        return held + [go(shard, 1, 0, 0) for shard in held]
-
-    def expert_shards(grads, rows):
-        columns = grads[0].shape[1]
-        pieces, moves = [], []
-        for e in range(EPD):
-            for j, shard in enumerate(expert_grads(grads[e], rows)):
-                pieces.append(shard)
-                moves.append(
-                    (len(pieces) - 1, (), ((mine ^ j) * EPD + e, 0, rows, 0, columns))
+        other = go(jnp.stack(held), 1, 0, 0)
+        return held, other
+
+    pieces, moves = [], []
+    for e in range(EPD):
+        held, other = expert_grads(pack_grads[e])
+        pieces += held + [other]
+        for j in range(PLANE):
+            moves.append(
+                (
+                    e * 5 + min(j, 4),
+                    () if j < 4 else (j - 4,),
+                    ((mine ^ j) * EPD + e, 0, ds, 0, 3 * hid),
                 )
-        whole = place(pieces, moves, jax.ShapeDtypeStruct((EXP, rows, columns), BF))
-        return whole.transpose(1, 0, 2).astype(F32)
-
-    in_shards = expert_shards(in_grads, ds)
-    down_shards = expert_shards(down_grads, hs)
+            )
+    shard_pack = place(pieces, moves, jax.ShapeDtypeStruct((EXP, ds, 3 * hid), BF))
+    gate_shard = shard_pack[..., :hid].transpose(1, 0, 2).astype(F32)
+    up_shard = shard_pack[..., hid : 2 * hid].transpose(1, 0, 2).astype(F32)
+    down_shard = (
+        shard_pack[..., 2 * hid :]
+        .reshape(EXP, blocks, hs, hid)
+        .transpose(2, 0, 1, 3)
+        .reshape(hs, EXP, width)
+        .astype(F32)
+    )
 
     grad_out = cotangent.astype(F32)
     scaled_two = grad_normed_two * gain_two
@@ -428,7 +835,7 @@
         [grad_query.reshape(length, width), grad_key.reshape(length, kvd), grad_value], axis=1
     )
     grad_mix_w = dot_tn(normed, grad_mix)
-    grad_normed = dot_nt(grad_mix, front[:, : width + 2 * kvd])
+    grad_normed = dot_nt(grad_mix, front[:, :mix])
     scaled_one = grad_normed * gain_one
     input_grad = (
         grad_resid
@@ -436,29 +843,35 @@
         - inputs * inv_one**3 * jnp.mean(scaled_one * inputs, axis=1, keepdims=True)
     )
     grad_gain_one = jnp.sum(grad_normed * inputs * inv_one, axis=0)
-    out_shard = scatter_rows(grad_out_w.astype(BF))
     front_grad = jnp.concatenate(
         [
             grad_mix_w.astype(BF),
+            grad_out_w.astype(BF),
             grad_gain_one.astype(BF)[:, None],
             grad_gain_two.astype(BF)[:, None],
             jnp.zeros((width, 254), BF),
         ],
         axis=1,
     )
-    front_shard = scatter_rows(front_grad)
+    total = all_reps(scatter_front(front_grad, planes, group))
+    other = go(total, 1, 0, 0)
+    front_shard = jnp.where(
+        xb == 0,
+        jnp.concatenate([total, other], axis=1),
+        jnp.concatenate([other, total], axis=1),
+    ).astype(F32)
     return (
         output,
         input_grad,
-        front_shard[:, width + 2 * kvd],
+        front_shard[:, mix + width],
         front_shard[:, :width],
         front_shard[:, width : width + kvd],
-        front_shard[:, width + kvd : width + 2 * kvd],
-        out_shard,
-        front_shard[:, width + 2 * kvd + 1],
-        in_shards[..., :hid],
-        in_shards[..., hid:],
-        down_shards,
+        front_shard[:, width + kvd : mix],
+        front_shard[:, mix : mix + width],
+        front_shard[:, mix + width + 1],
+        gate_shard,
+        up_shard,
+        down_shard,
     )
 
 

time: 1060 us -> 1020 us (0.962)
  Pallas kernels: 31.3 us -> 348 us
  waiting for transfers between devices: 434 us -> 190 us
  starting transfers between devices: 116 us -> 33.5 us
  local copies, waits for them, and re-layouts: 163 us -> 130 us
    pallas_call x0 -> x4, Pallas kernels: none -> 335 us  [the longest x1 106 us: scatter_plane(): pl.pallas_call(kernel, out_shape=jax.ShapeDtypeStruct((length, width), F3...]
    ppermute x161 -> x45, waiting for transfers between devices: 434 us -> 190 us  [pp(): return lax.ppermute(value, AXES, perm(to))]
    ppermute x161 -> x45, starting transfers between devices: 116 us -> 33.5 us  [pp(): return lax.ppermute(value, AXES, perm(to))]
    unnamed x331 -> x191, local copies, waits for them, and re-layouts: 78.4 us -> 39.8 us
    pallas_call x12 -> x7, Pallas kernels: 31.3 us -> 13 us  [place(): pl.pallas_call(kernel, out_shape=out_shape, in_specs=[pl.BlockSpec(memory...]
    transpose x0 -> x4, local copies, waits for them, and re-layouts: none -> 13 us  [the longest x1 6.3 us: shards(): w_gate.astype(BF).transpose(1, 0, 2)]
    dynamic_slice x15 -> x4, local copies, waits for them, and re-layouts: 15.9 us -> 3.89 us  [the longest x2 1.84 us: expert_grads(): lax.dynamic_slice(total, (((yb ^ dy) * 2 + (c ^ dc)) * ds, 0), (ds, 3 * h...]
  transfers between devices with their start and end apart: 161 -> 45, of which waited for: 47 -> 15; matrix products, arithmetic and copies ran while one was open for 34% -> 33% of each run, Pallas kernels for 3% -> 26%
where the time goes in v2:
time: 1020 us; the launch traced here: 1000 us
  Pallas kernels  348 us (34%)
  matrix products  237 us (23%)
  waiting for transfers between devices  190 us (19%)
  local copies, waits for them, and re-layouts  130 us (13%)
  other arithmetic  62.3 us (6%)
  starting transfers between devices  33.5 us (3%)
    ppermute x45, waiting for transfers between devices, pp(): return lax.ppermute(value, AXES, perm(to))  190 us
    pallas_call x1, Pallas kernels, scatter_plane(): pl.pallas_call(kernel, out_shape=jax.ShapeDtypeStruct((length, width), F3...  106 us
    pallas_call x1, Pallas kernels, scatter_front(): pl.pallas_call(kernel, out_shape=jax.ShapeDtypeStruct((ds, half), BF), in...  83.4 us
    pallas_call x1, Pallas kernels, gather_front(): pl.pallas_call(kernel, out_shape=jax.ShapeDtypeStruct((planes * 4 * ds, 2...  81.2 us
    dot_general x6, matrix products, dot_nt(): lax.dot_general(a, b, (((1,), (1,)), ((), ())), preferred_element_type=F32)  73.9 us
    dot_general x6, matrix products, dot(): return jnp.dot(a, b, preferred_element_type=F32)  66.7 us
    pallas_call x1, Pallas kernels, gather_plane(): pl.pallas_call(kernel, out_shape=jax.ShapeDtypeStruct((PLANE, length, wid...  64.4 us
    dot_general x6, matrix products, dot_tn(): lax.dot_general(a, b, (((0,), (0,)), ((), ())), preferred_element_type=F32)  51.4 us
  transfers between devices with their start and end apart: 45, of which 15 were waited for; matrix products, arithmetic and copies ran while one was open for 33% of the time, Pallas kernels for 26%

profile of v2, /device:TPU:0, one launch (start us, length us, event | category | flops | bytes accessed | tf_op | source)
XLA Modules:
  0.0 1003.8 jit_solution(1642478237134539448)
XLA Ops:
  6.9 4.6 reshape.239
  13.8 6.3 fusion.43
  31.4 81.2 %shard_map.221 = bf16[1536,4352]{1,0:T(8,128)(2,1)} custom-call(bf16[96,2176]{1,0:T(8,128)(2,1)} %constant_dynamic-slice_fusion.20.own_ref), custom_call_target="tpu_custom_call" | custom-call | flops 49999998976 | bytes 20000000 | tf_op jit(solution)/shard_map/pallas_call | solution.py:249
  115.1 5.6 fusion.10
  138.0 11.5 %fusion.100 = (f32[8,3,384]{2,1,0:T(4,128)}, f32[8,3,384,384]{2,3,1,0:T(8,128)}) fusion(pred[384,384]{0,1:T(8,128)(4,1)} %fusion.75, bf16[384,8,3,32]{0,3,2,1:T(8,128)(2,1)} %bitcast.251, bf16[384,8,3,32]{0,3,2,1:T(8,128)(2,1)} %bitcast.247, bf16[384,8,32]{0,2,1:T(8,128)(2,1)} %get-tuple-element.88, bf16[384,8,32]{0,2,1:T(8,128)(2,1)} %get-tuple-element.87), kind=kOutput, calls=%fused_computation.230 | convolution fusion | flops 470286720 | bytes 15912960 | tf_op jit(solution)/shard_map/sub | solution.py:718
  149.6 8.5 fusion.45
  158.0 6.4 multiply_reduce_fusion.2
  173.9 64.4 %shard_map.222 = bf16[8,384,1536]{2,1,0:T(8,128)(2,1)} custom-call(bf16[384,1536]{1,0:T(8,128)(2,1)} %multiply_convert_fusion.6.own_ref), custom_call_target="tpu_custom_call" | custom-call | flops 44999999488 | bytes 20000000 | tf_op jit(solution)/shard_map/pallas_call | solution.py:300
  279.1 4.2 collective-permute-done.27
  283.3 14.0 %collective-permute-done.10.refs_1_ = bf16[384,1536]{1,0:T(8,128)(2,1)S(1)} collective-permute-done((bf16[384,1536]{1,0:T(8,128)(2,1)S(1)}, bf16[384,1536]{1,0:T(8,128)(2,1)S(1)}, u32[]{:S(2)}, u32[]{:S(2)}) %collective-permute-start.10) | collective-permute-done | bytes 1179680 | tf_op jit(solution)/shard_map/ppermute | solution.py:571
  300.9 21.7 %collective-permute-done.14.refs_2_ = bf16[384,1536]{1,0:T(8,128)(2,1)S(1)} collective-permute-done((bf16[384,1536]{1,0:T(8,128)(2,1)}, bf16[384,1536]{1,0:T(8,128)(2,1)S(1)}, u32[]{:S(2)}, u32[]{:S(2)}) %collective-permute-start.14) | collective-permute-done | bytes 1179680 | tf_op jit(solution)/shard_map/ppermute | solution.py:571
  327.2 20.8 %collective-permute-done.11.refs_2_ = bf16[384,1536]{1,0:T(8,128)(2,1)} collective-permute-done((bf16[384,1536]{1,0:T(8,128)(2,1)S(1)}, bf16[384,1536]{1,0:T(8,128)(2,1)}, u32[]{:S(2)}, u32[]{:S(2)}) %collective-permute-start.11) | collective-permute-done | bytes 1179680 | tf_op jit(solution)/shard_map/ppermute | solution.py:571
  348.0 25.2 %collective-permute-done.15.refs_3_ = bf16[384,1536]{1,0:T(8,128)(2,1)S(1)} collective-permute-done((bf16[384,1536]{1,0:T(8,128)(2,1)S(1)}, bf16[384,1536]{1,0:T(8,128)(2,1)S(1)}, u32[]{:S(2)}, u32[]{:S(2)}) %collective-permute-start.15) | collective-permute-done | bytes 1179680 | tf_op jit(solution)/shard_map/ppermute | solution.py:571
  374.9 16.5 %fusion.102 = f32[3072,1024]{0,1:T(8,128)} fusion(bf16[3072,1536]{1,0:T(8,128)(2,1)} %bitcast.269, bf16[1536,1024]{1,0:T(8,128)(2,1)S(1)} %shard_map.227), kind=kOutput, calls=%fused_computation.232 | convolution fusion | flops 9663676416 | bytes 25165824 | tf_op jit(solution)/shard_map/dot_general | solution.py:58
  393.7 15.1 %multiply_convert_fusion.1 = (bf16[3072,512]{0,1:T(8,128)(2,1)}, bf16[3072,512]{0,1:T(8,128)(2,1)}, bf16[3072,512]{0,1:T(8,128)(2,1)S(1)}) fusion(f32[3072,1024]{0,1:T(8,128)} %fusion.102, f32[3072]{0:T(1024)S(1)} %bitcast.268, bf16[3072,1536]{1,0:T(8,128)(2,1)} %constant_dynamic-update-slice_fusion.8, bf16[512,1536]{1,0:T(8,128)(2,1)S(1)} %shard_map.228), kind=kOutput, calls=%fused_computation.32 | convolution fusion | flops 4858576896 | bytes 33042432 | tf_op jit(solution)/shard_map/dot_general | solution.py:62
  410.5 6.2 convolution_convert_fusion.2
  416.7 5.6 reshape.247
  424.8 13.8 %fusion.23 = bf16[1536,1024]{1,0:T(8,128)(2,1)S(1)} fusion(bf16[3072,1536]{1,0:T(8,128)(2,1)} %bitcast.270, bf16[3072,512]{0,1:T(8,128)(2,1)} %get-tuple-element.55, bf16[3072,512]{0,1:T(8,128)(2,1)S(1)} %copy-done.74), kind=kOutput, calls=%fused_computation.68 | convolution fusion | flops 9677832192 | bytes 18874368 | tf_op jit(solution)/shard_map/dot_general | solution.py:66
  442.6 9.0 fusion.103
  454.0 16.6 %fusion.101 = f32[3072,1024]{0,1:T(8,128)} fusion(bf16[3072,1536]{1,0:T(8,128)(2,1)} %bitcast.271, bf16[1536,1024]{1,0:T(8,128)(2,1)S(1)} %shard_map.224), kind=kOutput, calls=%fused_computation.231 | convolution fusion | flops 9663676416 | bytes 25165824 | tf_op jit(solution)/shard_map/dot_general | solution.py:58
  473.2 12.9 %multiply_convert_fusion.3 = (bf16[3072,512]{0,1:T(8,128)(2,1)}, bf16[3072,512]{0,1:T(8,128)(2,1)}, bf16[3072,512]{0,1:T(8,128)(2,1)S(1)}) fusion(f32[3072,1024]{0,1:T(8,128)} %fusion.101, f32[3072]{0:T(1024)S(1)} %bitcast.267, bf16[3072,1536]{1,0:T(8,128)(2,1)S(1)} %bitcast.266, bf16[512,1536]{1,0:T(8,128)(2,1)S(1)} %shard_map.225), kind=kOutput, calls=%fused_computation.34 | convolution fusion | flops 4858576896 | bytes 33042432 | tf_op jit(solution)/shard_map/dot_general | solution.py:62
  487.8 5.1 convolution_convert_fusion.3
  497.8 13.7 %fusion.22 = bf16[1536,1024]{1,0:T(8,128)(2,1)S(1)} fusion(bf16[3072,1536]{1,0:T(8,128)(2,1)} %bitcast.272, bf16[3072,512]{0,1:T(8,128)(2,1)} %get-tuple-element.53, bf16[3072,512]{0,1:T(8,128)(2,1)S(1)} %copy-done.73), kind=kOutput, calls=%fused_computation.67 | convolution fusion | flops 9677832192 | bytes 18874368 | tf_op jit(solution)/shard_map/dot_general | solution.py:66
  513.4 12.6 %add_convert_fusion.1 = bf16[3072,1536]{1,0:T(8,128)(2,1)} fusion(f32[3072,1536]{1,0:T(8,128)} %fusion.103, bf16[3072,512]{0,1:T(8,128)(2,1)} %copy-done.72, bf16[512,1536]{1,0:T(8,128)(2,1)S(1)} %copy-done.10), kind=kOutput, calls=%fused_computation.2 | convolution fusion | flops 4841275392 | bytes 33030144 | tf_op jit(solution)/shard_map/dot_general | solution.py:58
  528.2 15.4 %collective-permute-done.31 = bf16[384,1536]{1,0:T(8,128)(2,1)} collective-permute-done((bf16[384,1536]{1,0:T(8,128)(2,1)}, bf16[384,1536]{1,0:T(8,128)(2,1)}, u32[]{:S(2)}, u32[]{:S(2)}) %collective-permute-start.31) | collective-permute-done | bytes 1179680 | tf_op jit(solution)/shard_map/ppermute | solution.py:571
  547.8 21.0 %collective-permute-done.39 = bf16[384,1536]{1,0:T(8,128)(2,1)S(1)} collective-permute-done((bf16[384,1536]{1,0:T(8,128)(2,1)S(1)}, bf16[384,1536]{1,0:T(8,128)(2,1)S(1)}, u32[]{:S(2)}, u32[]{:S(2)}) %collective-permute-start.39) | collective-permute-done | bytes 1179680 | tf_op jit(solution)/shard_map/ppermute | solution.py:571
  570.4 23.7 %collective-permute-done.32 = bf16[384,1536]{1,0:T(8,128)(2,1)S(1)} collective-permute-done((bf16[384,1536]{1,0:T(8,128)(2,1)S(1)}, bf16[384,1536]{1,0:T(8,128)(2,1)S(1)}, u32[]{:S(2)}, u32[]{:S(2)}) %collective-permute-start.32) | collective-permute-done | bytes 1179680 | tf_op jit(solution)/shard_map/ppermute | solution.py:571
  594.5 15.8 %fusion.20 = f32[3072,1536]{1,0:T(8,128)} fusion(bf16[1536,1024]{1,0:T(8,128)(2,1)S(1)} %copy-done.3, bf16[3072,512]{0,1:T(8,128)(2,1)} %get-tuple-element.55, bf16[3072,512]{0,1:T(8,128)(2,1)} %get-tuple-element.54), kind=kOutput, calls=%fused_computation.65 | convolution fusion | flops 9676259328 | bytes 28311552 | tf_op jit(solution)/shard_map/dot_general | solution.py:62
  610.3 9.2 collective-permute-done.40
  623.7 16.1 %collective-permute-done.33 = bf16[384,1536]{1,0:T(8,128)(2,1)S(1)} collective-permute-done((bf16[384,1536]{1,0:T(8,128)(2,1)S(1)}, bf16[384,1536]{1,0:T(8,128)(2,1)S(1)}, u32[]{:S(2)}, u32[]{:S(2)}) %collective-permute-start.33) | collective-permute-done | bytes 1179680 | tf_op jit(solution)/shard_map/ppermute | solution.py:571
  644.4 17.3 %add_convert_fusion = bf16[3072,1536]{1,0:T(8,128)(2,1)} fusion(f32[3072,1536]{1,0:T(8,128)} %fusion.20, bf16[1536,1024]{1,0:T(8,128)(2,1)S(1)} %copy-done.1, bf16[3072,512]{0,1:T(8,128)(2,1)} %get-tuple-element.53, bf16[3072,512]{0,1:T(8,128)(2,1)} %get-tuple-element.52), kind=kOutput, calls=%fused_computation.1 | convolution fusion | flops 9685696512 | bytes 37748736 | tf_op jit(solution)/shard_map/dot_general | solution.py:62
  668.5 4.2 fusion.14
  677.2 106.2 %shard_map.229 = f32[384,1536]{1,0:T(8,128)} custom-call(bf16[8,384,1536]{2,1,0:T(8,128)(2,1)} %bitcast.273), custom_call_target="tpu_custom_call" | custom-call | flops 44999999488 | bytes 20000000 | tf_op jit(solution)/shard_map/pallas_call | solution.py:379
  795.7 3.7 fusion.96
  802.8 6.1 reshape.253
  808.9 5.5 copy.112
  814.4 3.5 copy.113
  820.6 3.5 multiply_subtract_fusion
  824.1 4.4 convolution_convert_fusion.1
  828.5 4.4 fusion.30
  833.9 13.1 %fusion.1 = (f32[8,3,384]{2,1,0:T(4,128)S(1)}, f32[8,384,384,3]{2,1,3,0:T(8,128)}) fusion(f32[8,3,384,384]{2,3,1,0:T(8,128)} %get-tuple-element.107, f32[8,3,384]{2,1,0:T(4,128)S(1)} %copy-done.49, bf16[384,8,64,1]{0,2,3,1:T(8,128)(2,1)S(1)} %bitcast.260, bf16[384,8,3,64]{0,3,2,1:T(8,128)(2,1)S(1)} %bitcast.255), kind=kOutput, calls=%fused_computation.5 | convolution fusion | flops 463592448 | bytes 29958144 | tf_op jit(solution)/shard_map/voua,zoa->ouvz/dot_general | solution.py:814
  848.1 6.6 fusion.3
  858.6 8.6 fusion.53
  868.8 8.2 convolution_convert_fusion
  877.1 8.4 fusion.40
  885.8 19.6 %concatenate.74.g_ref = bf16[1536,4352]{1,0:T(8,128)(2,1)} concatenate(bf16[1536,2560]{1,0:T(8,128)(2,1)} %convolution_convert_fusion, bf16[1536,1536]{1,0:T(8,128)(2,1)} %convolution_convert_fusion.1, bf16[1536,1]{1,0:T(8,128)(2,1)S(1)} %convert_element_type.280, bf16[1536,1]{1,0:T(8,128)(2,1)S(1)} %copy-done.35, bf16[1536,254]{1,0:T(8,128)(2,1)S(1)} %broadcast_in_dim.29), dimensions={1} | concatenate | bytes 26738688 | tf_op jit(solution)/shard_map/concatenate | solution.py:846
  905.4 83.4 %shard_map.230 = bf16[96,2176]{1,0:T(8,128)(2,1)} custom-call(bf16[1536,4352]{1,0:T(8,128)(2,1)} %concatenate.74.g_ref), custom_call_target="tpu_custom_call" | custom-call | flops 49999998976 | bytes 20000000 | tf_op jit(solution)/shard_map/pallas_call | solution.py:517
  991.9 8.9 collective-permute-done.30
  (365 shorter events, 182.5 us)
Async XLA Ops:
  0.6 267.6 %collective-permute-start.22 = (bf16[384,1536]{1,0:T(8,128)(2,1)}, bf16[384,1536]{1,0:T(8,128)(2,1)}, u32[]{:S(2)}, u32[]{:S(2)}) collective-permute-start(bf16[384,1536]{1,0:T(8,128)(2,1)} %param.15), channel_id=1, source_target_pairs={{0,2},{1,3},{2,0},{3,1},{4,6},{5,7},{6,4},{7,5},{8,10},{9,11},{10,... | collective-permute-start | bytes 3538952 | tf_op jit(solution)/shard_map/ppermute | solution.py:571
  3.7 267.2 %collective-permute-start.21 = (bf16[384,1536]{1,0:T(8,128)(2,1)}, bf16[384,1536]{1,0:T(8,128)(2,1)}, u32[]{:S(2)}, u32[]{:S(2)}) collective-permute-start(bf16[384,1536]{1,0:T(8,128)(2,1)} %param.15), channel_id=1, source_target_pairs={{0,1},{1,0},{2,3},{3,2},{4,5},{5,4},{6,7},{7,6},{8,9},{9,8},{10,11... | collective-permute-start | bytes 3538952 | tf_op jit(solution)/shard_map/ppermute | solution.py:571
  21.9 147.6 %collective-permute-start.7 = (bf16[2,96,1536]{2,1,0:T(8,128)(2,1)}, bf16[2,96,1536]{2,1,0:T(8,128)(2,1)S(1)}, u32[]{:S(2)}, u32[]{:S(2)}) collective-permute-start(bf16[2,96,1536]{2,1,0:T(8,128)(2,1)} %get-tuple-element.65), channel_id=1, source_target_pairs={{0,1},{1,0},{2,3},{3,2},{4,5},{5,4},{6,7},{7,6},{8,9},{9,8},{10,11... | collective-permute-start | bytes 1769480 | tf_op jit(solution)/shard_map/ppermute | solution.py:571
  22.4 148.8 %collective-permute-start.8 = (bf16[2,96,1536]{2,1,0:T(8,128)(2,1)}, bf16[2,96,1536]{2,1,0:T(8,128)(2,1)S(1)}, u32[]{:S(2)}, u32[]{:S(2)}) collective-permute-start(bf16[2,96,1536]{2,1,0:T(8,128)(2,1)} %get-tuple-element.64), channel_id=1, source_target_pairs={{0,2},{1,3},{2,0},{3,1},{4,6},{5,7},{6,4},{7,5},{8,10},{9,11},{10,... | collective-permute-start | bytes 1769480 | tf_op jit(solution)/shard_map/ppermute | solution.py:571
  22.5 148.9 %collective-permute-start.9 = (bf16[2,96,1536]{2,1,0:T(8,128)(2,1)}, bf16[2,96,1536]{2,1,0:T(8,128)(2,1)S(1)}, u32[]{:S(2)}, u32[]{:S(2)}) collective-permute-start(bf16[2,96,1536]{2,1,0:T(8,128)(2,1)} %get-tuple-element.63), channel_id=1, source_target_pairs={{0,3},{1,2},{2,1},{3,0},{4,7},{5,6},{6,5},{7,4},{8,11},{9,10},{10,... | collective-permute-start | bytes 1769480 | tf_op jit(solution)/shard_map/ppermute | solution.py:571
  169.5 74.9 %collective-permute-start.24 = (bf16[384,1536]{1,0:T(8,128)(2,1)}, bf16[384,1536]{1,0:T(8,128)(2,1)}, u32[]{:S(2)}, u32[]{:S(2)}) collective-permute-start(bf16[384,1536]{1,0:T(8,128)(2,1)} %param.15), channel_id=1, source_target_pairs={{0,16},{1,17},{2,18},{3,19},{4,20},{5,21},{6,22},{7,23},{8,24},{9,... | collective-permute-start | bytes 3538952 | tf_op jit(solution)/shard_map/ppermute | solution.py:571
  171.2 70.0 %collective-permute-start = (f32[2,384]{1,0:T(2,128)}, f32[2,384]{1,0:T(2,128)}, u32[]{:S(2)}, u32[]{:S(2)}) collective-permute-start(f32[2,384]{1,0:T(2,128)} %get-tuple-element.97), channel_id=1, source_target_pairs={{0,1},{1,0},{2,3},{3,2},{4,5},{5,4},{6,7},{7,6},{8,9},{9,8},{10,11... | collective-permute-start | bytes 9224 | tf_op jit(solution)/shard_map/ppermute | solution.py:571
  172.2 98.6 %collective-permute-start.13 = (bf16[384,1536]{1,0:T(8,128)(2,1)S(1)}, bf16[384,1536]{1,0:T(8,128)(2,1)}, u32[]{:S(2)}, u32[]{:S(2)}) collective-permute-start(bf16[384,1536]{1,0:T(8,128)(2,1)S(1)} %shard_map.226.refs_0_), channel_id=1, source_target_pairs={{0,4},{1,5},{2,6},{3,7},{4,8},{5,9},{6,10},{7,11},{8,12},{9,13},{1... | collective-permute-start | bytes 3538952 | tf_op jit(solution)/shard_map/ppermute | solution.py:571
  241.3 4.2 collective-permute-start.1
  244.4 3.5 collective-permute-start.2
  245.5 25.9 %collective-permute-start.26 = (bf16[192,1536]{1,0:T(8,128)(2,1)S(1)}, bf16[192,1536]{1,0:T(8,128)(2,1)S(1)}, u32[]{:S(2)}, u32[]{:S(2)}) collective-permute-start(bf16[192,1536]{1,0:T(8,128)(2,1)S(1)} %slice.199), channel_id=1, source_target_pairs={{0,2},{1,3},{2,0},{3,1},{4,6},{5,7},{6,4},{7,5},{8,10},{9,11},{10,... | collective-permute-start | bytes 1769480 | tf_op jit(solution)/shard_map/ppermute | solution.py:571
  247.9 3.6 collective-permute-start.3
  251.5 3.0 collective-permute-start.4
  254.5 4.6 collective-permute-start.5
  259.1 3.9 collective-permute-start.6
  266.6 30.8 %collective-permute-start.10 = (bf16[384,1536]{1,0:T(8,128)(2,1)S(1)}, bf16[384,1536]{1,0:T(8,128)(2,1)S(1)}, u32[]{:S(2)}, u32[]{:S(2)}) collective-permute-start(bf16[384,1536]{1,0:T(8,128)(2,1)S(1)} %shard_map.223.refs_0_), channel_id=1, source_target_pairs={{0,4},{1,5},{2,6},{3,7},{4,8},{5,9},{6,10},{7,11},{8,12},{9,13},{1... | collective-permute-start | bytes 3538952 | tf_op jit(solution)/shard_map/ppermute | solution.py:571
  269.3 14.0 %collective-permute-start.27 = (bf16[192,1536]{1,0:T(8,128)(2,1)S(1)}, bf16[192,1536]{1,0:T(8,128)(2,1)S(1)}, u32[]{:S(2)}, u32[]{:S(2)}) collective-permute-start(bf16[192,1536]{1,0:T(8,128)(2,1)S(1)} %slice.200), channel_id=1, source_target_pairs={{0,16},{1,17},{2,18},{3,19},{4,20},{5,21},{6,22},{7,23},{8,24},{9,... | collective-permute-start | bytes 1769480 | tf_op jit(solution)/shard_map/ppermute | solution.py:571
  270.9 26.5 %collective-permute-start.23 = (bf16[384,1536]{1,0:T(8,128)(2,1)}, bf16[384,1536]{1,0:T(8,128)(2,1)S(1)}, u32[]{:S(2)}, u32[]{:S(2)}) collective-permute-start(bf16[384,1536]{1,0:T(8,128)(2,1)} %collective-permute-done.22), channel_id=1, source_target_pairs={{0,1},{1,0},{2,3},{3,2},{4,5},{5,4},{6,7},{7,6},{8,9},{9,8},{10,11... | collective-permute-start | bytes 3538952 | tf_op jit(solution)/shard_map/ppermute | solution.py:571
  270.9 51.7 %collective-permute-start.25 = (bf16[384,1536]{1,0:T(8,128)(2,1)}, bf16[384,1536]{1,0:T(8,128)(2,1)S(1)}, u32[]{:S(2)}, u32[]{:S(2)}) collective-permute-start(bf16[384,1536]{1,0:T(8,128)(2,1)} %collective-permute-done.24), channel_id=1, source_target_pairs={{0,1},{1,0},{2,3},{3,2},{4,5},{5,4},{6,7},{7,6},{8,9},{9,8},{10,11... | collective-permute-start | bytes 3538952 | tf_op jit(solution)/shard_map/ppermute | solution.py:571
  271.4 51.2 %collective-permute-start.14 = (bf16[384,1536]{1,0:T(8,128)(2,1)}, bf16[384,1536]{1,0:T(8,128)(2,1)S(1)}, u32[]{:S(2)}, u32[]{:S(2)}) collective-permute-start(bf16[384,1536]{1,0:T(8,128)(2,1)} %collective-permute-done.13.refs_1_), channel_id=1, source_target_pairs={{0,4},{1,5},{2,6},{3,7},{4,8},{5,9},{6,10},{7,11},{8,12},{9,13},{1... | collective-permute-start | bytes 3538952 | tf_op jit(solution)/shard_map/ppermute | solution.py:571
  283.3 42.1 %collective-permute-start.28 = (bf16[192,1536]{1,0:T(8,128)(2,1)S(1)}, bf16[192,1536]{1,0:T(8,128)(2,1)S(1)}, u32[]{:S(2)}, u32[]{:S(2)}) collective-permute-start(bf16[192,1536]{1,0:T(8,128)(2,1)S(1)} %collective-permute-done.26), channel_id=1, source_target_pairs={{0,1},{1,0},{2,3},{3,2},{4,5},{5,4},{6,7},{7,6},{8,9},{9,8},{10,11... | collective-permute-start | bytes 1769480 | tf_op jit(solution)/shard_map/ppermute | solution.py:571
  297.3 29.0 %collective-permute-start.29 = (bf16[192,1536]{1,0:T(8,128)(2,1)S(1)}, bf16[192,1536]{1,0:T(8,128)(2,1)S(1)}, u32[]{:S(2)}, u32[]{:S(2)}) collective-permute-start(bf16[192,1536]{1,0:T(8,128)(2,1)S(1)} %collective-permute-done.27), channel_id=1, source_target_pairs={{0,1},{1,0},{2,3},{3,2},{4,5},{5,4},{6,7},{7,6},{8,9},{9,8},{10,11... | collective-permute-start | bytes 1769480 | tf_op jit(solution)/shard_map/ppermute | solution.py:571
  297.3 50.7 %collective-permute-start.11 = (bf16[384,1536]{1,0:T(8,128)(2,1)S(1)}, bf16[384,1536]{1,0:T(8,128)(2,1)}, u32[]{:S(2)}, u32[]{:S(2)}) collective-permute-start(bf16[384,1536]{1,0:T(8,128)(2,1)S(1)} %collective-permute-done.10.refs_1_), channel_id=1, source_target_pairs={{0,4},{1,5},{2,6},{3,7},{4,8},{5,9},{6,10},{7,11},{8,12},{9,13},{1... | collective-permute-start | bytes 3538952 | tf_op jit(solution)/shard_map/ppermute | solution.py:571
  322.6 50.6 %collective-permute-start.15 = (bf16[384,1536]{1,0:T(8,128)(2,1)S(1)}, bf16[384,1536]{1,0:T(8,128)(2,1)S(1)}, u32[]{:S(2)}, u32[]{:S(2)}) collective-permute-start(bf16[384,1536]{1,0:T(8,128)(2,1)S(1)} %collective-permute-done.14.refs_2_), channel_id=1, source_target_pairs={{0,4},{1,5},{2,6},{3,7},{4,8},{5,9},{6,10},{7,11},{8,12},{9,13},{1... | collective-permute-start | bytes 3538952 | tf_op jit(solution)/shard_map/ppermute | solution.py:571
  348.0 103.6 %collective-permute-start.12 = (bf16[384,1536]{1,0:T(8,128)(2,1)}, bf16[384,1536]{1,0:T(8,128)(2,1)}, u32[]{:S(2)}, u32[]{:S(2)}) collective-permute-start(bf16[384,1536]{1,0:T(8,128)(2,1)} %collective-permute-done.11.refs_2_), channel_id=1, source_target_pairs={{0,4},{1,5},{2,6},{3,7},{4,8},{5,9},{6,10},{7,11},{8,12},{9,13},{1... | collective-permute-start | bytes 3538952 | tf_op jit(solution)/shard_map/ppermute | solution.py:571
  440.8 85.1 %collective-permute-start.38 = (bf16[384,1536]{1,0:T(8,128)(2,1)}, bf16[384,1536]{1,0:T(8,128)(2,1)}, u32[]{:S(2)}, u32[]{:S(2)}) collective-permute-start(bf16[384,1536]{1,0:T(8,128)(2,1)} %fusion.58), channel_id=1, source_target_pairs={{0,4},{1,5},{2,6},{3,7},{4,8},{5,9},{6,10},{7,11},{8,12},{9,13},{1... | collective-permute-start | bytes 3538952 | tf_op jit(solution)/shard_map/ppermute | solution.py:571
  512.6 31.0 %collective-permute-start.31 = (bf16[384,1536]{1,0:T(8,128)(2,1)}, bf16[384,1536]{1,0:T(8,128)(2,1)}, u32[]{:S(2)}, u32[]{:S(2)}) collective-permute-start(bf16[384,1536]{1,0:T(8,128)(2,1)} %fusion.65), channel_id=1, source_target_pairs={{0,4},{1,5},{2,6},{3,7},{4,8},{5,9},{6,10},{7,11},{8,12},{9,13},{1... | collective-permute-start | bytes 3538952 | tf_op jit(solution)/shard_map/ppermute | solution.py:571
  527.7 41.1 %collective-permute-start.39 = (bf16[384,1536]{1,0:T(8,128)(2,1)S(1)}, bf16[384,1536]{1,0:T(8,128)(2,1)S(1)}, u32[]{:S(2)}, u32[]{:S(2)}) collective-permute-start(bf16[384,1536]{1,0:T(8,128)(2,1)S(1)} %fusion.60), channel_id=1, source_target_pairs={{0,4},{1,5},{2,6},{3,7},{4,8},{5,9},{6,10},{7,11},{8,12},{9,13},{1... | collective-permute-start | bytes 3538952 | tf_op jit(solution)/shard_map/ppermute | solution.py:571
  545.2 48.9 %collective-permute-start.32 = (bf16[384,1536]{1,0:T(8,128)(2,1)S(1)}, bf16[384,1536]{1,0:T(8,128)(2,1)S(1)}, u32[]{:S(2)}, u32[]{:S(2)}) collective-permute-start(bf16[384,1536]{1,0:T(8,128)(2,1)S(1)} %fusion.67), channel_id=1, source_target_pairs={{0,4},{1,5},{2,6},{3,7},{4,8},{5,9},{6,10},{7,11},{8,12},{9,13},{1... | collective-permute-start | bytes 3538952 | tf_op jit(solution)/shard_map/ppermute | solution.py:571
  547.8 120.7 %collective-permute-start.16 = (bf16[2,2,384,1536]{3,2,1,0:T(8,128)(2,1)}, bf16[2,2,384,1536]{3,2,1,0:T(8,128)(2,1)}, u32[]{:S(2)}, u32[]{:S(2)}) collective-permute-start(bf16[2,2,384,1536]{3,2,1,0:T(8,128)(2,1)} %slice_bitcast_fusion), channel_id=1, source_target_pairs={{0,1},{1,0},{2,3},{3,2},{4,5},{5,4},{6,7},{7,6},{8,9},{9,8},{10,11... | collective-permute-start | bytes 14155784 | tf_op jit(solution)/shard_map/ppermute | solution.py:571
  570.2 49.3 %collective-permute-start.40 = (bf16[384,1536]{1,0:T(8,128)(2,1)}, bf16[384,1536]{1,0:T(8,128)(2,1)}, u32[]{:S(2)}, u32[]{:S(2)}) collective-permute-start(bf16[384,1536]{1,0:T(8,128)(2,1)} %fusion.62), channel_id=1, source_target_pairs={{0,4},{1,5},{2,6},{3,7},{4,8},{5,9},{6,10},{7,11},{8,12},{9,13},{1... | collective-permute-start | bytes 3538952 | tf_op jit(solution)/shard_map/ppermute | solution.py:571
  594.4 45.4 %collective-permute-start.33 = (bf16[384,1536]{1,0:T(8,128)(2,1)S(1)}, bf16[384,1536]{1,0:T(8,128)(2,1)S(1)}, u32[]{:S(2)}, u32[]{:S(2)}) collective-permute-start(bf16[384,1536]{1,0:T(8,128)(2,1)S(1)} %fusion.69), channel_id=1, source_target_pairs={{0,4},{1,5},{2,6},{3,7},{4,8},{5,9},{6,10},{7,11},{8,12},{9,13},{1... | collective-permute-start | bytes 3538952 | tf_op jit(solution)/shard_map/ppermute | solution.py:571
  621.9 19.3 %collective-permute-start.41 = (bf16[96,1536]{1,0:T(8,128)(2,1)S(1)}, bf16[96,1536]{1,0:T(8,128)(2,1)}, u32[]{:S(2)}, u32[]{:S(2)}) collective-permute-start(bf16[96,1536]{1,0:T(8,128)(2,1)S(1)} %get-tuple-element.79), channel_id=1, source_target_pairs={{0,1},{1,0},{2,3},{3,2},{4,5},{5,4},{6,7},{7,6},{8,9},{9,8},{10,11... | collective-permute-start | bytes 884744 | tf_op jit(solution)/shard_map/ppermute | solution.py:571
  621.9 22.4 %collective-permute-start.42 = (bf16[96,1536]{1,0:T(8,128)(2,1)S(1)}, bf16[96,1536]{1,0:T(8,128)(2,1)}, u32[]{:S(2)}, u32[]{:S(2)}) collective-permute-start(bf16[96,1536]{1,0:T(8,128)(2,1)S(1)} %get-tuple-element.78), channel_id=1, source_target_pairs={{0,2},{1,3},{2,0},{3,1},{4,6},{5,7},{6,4},{7,5},{8,10},{9,11},{10,... | collective-permute-start | bytes 884744 | tf_op jit(solution)/shard_map/ppermute | solution.py:571
  622.1 39.7 %collective-permute-start.43 = (bf16[96,1536]{1,0:T(8,128)(2,1)}, bf16[96,1536]{1,0:T(8,128)(2,1)}, u32[]{:S(2)}, u32[]{:S(2)}) collective-permute-start(bf16[96,1536]{1,0:T(8,128)(2,1)} %get-tuple-element.77), channel_id=1, source_target_pairs={{0,3},{1,2},{2,1},{3,0},{4,7},{5,6},{6,5},{7,4},{8,11},{9,10},{10,... | collective-permute-start | bytes 884744 | tf_op jit(solution)/shard_map/ppermute | solution.py:571
  641.2 22.9 %collective-permute-start.34 = (bf16[96,1536]{1,0:T(8,128)(2,1)}, bf16[96,1536]{1,0:T(8,128)(2,1)}, u32[]{:S(2)}, u32[]{:S(2)}) collective-permute-start(bf16[96,1536]{1,0:T(8,128)(2,1)} %get-tuple-element.83), channel_id=1, source_target_pairs={{0,1},{1,0},{2,3},{3,2},{4,5},{5,4},{6,7},{7,6},{8,9},{9,8},{10,11... | collective-permute-start | bytes 884744 | tf_op jit(solution)/shard_map/ppermute | solution.py:571
  641.2 22.9 %collective-permute-start.35 = (bf16[96,1536]{1,0:T(8,128)(2,1)}, bf16[96,1536]{1,0:T(8,128)(2,1)}, u32[]{:S(2)}, u32[]{:S(2)}) collective-permute-start(bf16[96,1536]{1,0:T(8,128)(2,1)} %get-tuple-element.82), channel_id=1, source_target_pairs={{0,2},{1,3},{2,0},{3,1},{4,6},{5,7},{6,4},{7,5},{8,10},{9,11},{10,... | collective-permute-start | bytes 884744 | tf_op jit(solution)/shard_map/ppermute | solution.py:571
  644.3 19.8 %collective-permute-start.36 = (bf16[96,1536]{1,0:T(8,128)(2,1)}, bf16[96,1536]{1,0:T(8,128)(2,1)}, u32[]{:S(2)}, u32[]{:S(2)}) collective-permute-start(bf16[96,1536]{1,0:T(8,128)(2,1)} %get-tuple-element.81), channel_id=1, source_target_pairs={{0,3},{1,2},{2,1},{3,0},{4,7},{5,6},{6,5},{7,4},{8,11},{9,10},{10,... | collective-permute-start | bytes 884744 | tf_op jit(solution)/shard_map/ppermute | solution.py:571
  664.1 123.1 %collective-permute-start.44 = (bf16[4,96,1536]{2,1,0:T(8,128)(2,1)}, bf16[4,96,1536]{2,1,0:T(8,128)(2,1)S(1)}, u32[]{:S(2)}, u32[]{:S(2)}) collective-permute-start(bf16[4,96,1536]{2,1,0:T(8,128)(2,1)} %pad_maximum_fusion.15), channel_id=1, source_target_pairs={{0,16},{1,17},{2,18},{3,19},{4,20},{5,21},{6,22},{7,23},{8,24},{9,... | collective-permute-start | bytes 3538952 | tf_op jit(solution)/shard_map/ppermute | solution.py:571
  666.4 120.8 %collective-permute-start.37 = (bf16[4,96,1536]{2,1,0:T(8,128)(2,1)}, bf16[4,96,1536]{2,1,0:T(8,128)(2,1)S(1)}, u32[]{:S(2)}, u32[]{:S(2)}) collective-permute-start(bf16[4,96,1536]{2,1,0:T(8,128)(2,1)} %pad_maximum_fusion.14), channel_id=1, source_target_pairs={{0,16},{1,17},{2,18},{3,19},{4,20},{5,21},{6,22},{7,23},{8,24},{9,... | collective-permute-start | bytes 3538952 | tf_op jit(solution)/shard_map/ppermute | solution.py:571
  675.5 114.3 %collective-permute-start.17 = (bf16[2,192,1536]{2,1,0:T(8,128)(2,1)}, bf16[2,192,1536]{2,1,0:T(8,128)(2,1)}, u32[]{:S(2)}, u32[]{:S(2)}) collective-permute-start(bf16[2,192,1536]{2,1,0:T(8,128)(2,1)} %slice_bitcast_fusion.4), channel_id=1, source_target_pairs={{0,2},{1,3},{2,0},{3,1},{4,6},{5,7},{6,4},{7,5},{8,10},{9,11},{10,... | collective-permute-start | bytes 3538952 | tf_op jit(solution)/shard_map/ppermute | solution.py:571
  677.1 112.6 %collective-permute-start.19 = (bf16[2,192,1536]{2,1,0:T(8,128)(2,1)}, bf16[2,192,1536]{2,1,0:T(8,128)(2,1)}, u32[]{:S(2)}, u32[]{:S(2)}) collective-permute-start(bf16[2,192,1536]{2,1,0:T(8,128)(2,1)} %slice_bitcast_fusion.2), channel_id=1, source_target_pairs={{0,16},{1,17},{2,18},{3,19},{4,20},{5,21},{6,22},{7,23},{8,24},{9,... | collective-permute-start | bytes 3538952 | tf_op jit(solution)/shard_map/ppermute | solution.py:571
  677.1 106.3 %copy-start.19 = (f32[384,1536]{1,0:T(8,128)S(1)}, f32[384,1536]{1,0:T(8,128)}, u32[]{:S(2)}) copy-start(f32[384,1536]{1,0:T(8,128)} %get-tuple-element.109) | copy-start | bytes 7077892
  677.1 106.3 %copy-start.48 = (f32[1536]{0:T(1024)S(1)}, f32[1536]{0:T(1024)}, u32[]{:S(2)}) copy-start(f32[1536]{0:T(1024)} %copy-done.47) | copy-start | bytes 18436
  677.1 106.3 %copy-start.53 = (f32[384]{0:T(512)S(1)}, f32[384]{0:T(512)}, u32[]{:S(2)}) copy-start(f32[384]{0:T(512)} %copy-done.52) | copy-start | bytes 4612
  792.6 25.3 %collective-permute-start.18 = (bf16[192,1536]{1,0:T(8,128)(2,1)}, bf16[192,1536]{1,0:T(8,128)(2,1)}, u32[]{:S(2)}, u32[]{:S(2)}) collective-permute-start(bf16[192,1536]{1,0:T(8,128)(2,1)} %slice_bitcast_fusion.8), channel_id=1, source_target_pairs={{0,16},{1,17},{2,18},{3,19},{4,20},{5,21},{6,22},{7,23},{8,24},{9,... | collective-permute-start | bytes 1769480 | tf_op jit(solution)/shard_map/ppermute | solution.py:571
  793.8 25.6 %collective-permute-start.20 = (bf16[192,1536]{1,0:T(8,128)(2,1)}, bf16[192,1536]{1,0:T(8,128)(2,1)}, u32[]{:S(2)}, u32[]{:S(2)}) collective-permute-start(bf16[192,1536]{1,0:T(8,128)(2,1)} %slice_bitcast_fusion.6), channel_id=1, source_target_pairs={{0,2},{1,3},{2,0},{3,1},{4,6},{5,7},{6,4},{7,5},{8,10},{9,11},{10,... | collective-permute-start | bytes 1769480 | tf_op jit(solution)/shard_map/ppermute | solution.py:571
  988.8 11.9 %collective-permute-start.30 = (bf16[96,2176]{1,0:T(8,128)(2,1)}, bf16[96,2176]{1,0:T(8,128)(2,1)S(1)}, u32[]{:S(2)}, u32[]{:S(2)}) collective-permute-start(bf16[96,2176]{1,0:T(8,128)(2,1)} %shard_map.230), channel_id=1, source_target_pairs={{0,16},{1,17},{2,18},{3,19},{4,20},{5,21},{6,22},{7,23},{8,24},{9,... | collective-permute-start | bytes 1253384 | tf_op jit(solution)/shard_map/ppermute | solution.py:571
  (84 other events, 1220.4 us)

commit v3 on v2

v3 whole, which is shorter than its diff:
```python
import math

import jax
import jax.numpy as jnp
from jax import lax
from jax.experimental import pallas as pl
from jax.experimental.pallas import tpu as pltpu
from jax.sharding import PartitionSpec as P

HEADS = 24
KV_HEADS = 8
HEAD = 64
EXP = 16
PIECE = 256
AXES = ("rep", "fsdp")
EPSILON = 1e-05
NEG_FILL = -1e30
BF = jnp.bfloat16
F32 = jnp.float32
PLANE = 8
EPD = EXP // PLANE


def turn_tables(length):
    positions = jnp.arange(length, dtype=F32)[:, None]
    lanes = jnp.arange(2 * HEAD)
    rates = jnp.exp((lanes % (HEAD // 2)).astype(F32) * (-2.0 * math.log(10000.0) / HEAD))
    angles = positions * rates[None, :]
    low = (lanes % HEAD < HEAD // 2)[None, :]
    sines = jnp.sin(angles)
    return jnp.stack([jnp.cos(angles), jnp.where(low, -sines, 0.0), jnp.where(low, 0.0, sines)])


def turned(values, tables, sign):
    ahead = pltpu.roll(values, 2 * HEAD - HEAD // 2, 1)
    back = pltpu.roll(values, HEAD // 2, 1)
    return values * tables[0] + sign * (ahead * tables[1] + back * tables[2])


def row_loop(rows, step, body):
    @pl.loop(0, rows // step)
    def _(n):
        body(pl.ds(pl.multiple_of(n * step, step), step))


def dot(a, b):
    return jnp.dot(a, b, preferred_element_type=F32)


def dot_nt(a, b):
    return lax.dot_general(a, b, (((1,), (1,)), ((), ())), preferred_element_type=F32)


def dot_tn(a, b):
    return lax.dot_general(a, b, (((0,), (0,)), ((), ())), preferred_element_type=F32)


def add_rows(store, terms, rows, step=32):
    step = min(step, rows)

    @pl.loop(0, rows // step)
    def _(n):
        chunk = pl.ds(pl.multiple_of(n * step, 16), step)
        total = terms[0](chunk).astype(F32)
        for term in terms[1:]:
            total = total + term(chunk).astype(F32)
        store(chunk, total)


class Links:
    def __init__(self, planes, group, send_sems, recv_sems):
        r, f = lax.axis_index("rep"), lax.axis_index("fsdp")
        self.xb, self.yb, self.c, self.z = r % 2, (f // 2) % 2, f % 2, f // 4
        self.x = (r + 1 - 2 * self.xb, f)
        self.y = (r, f + 2 - 4 * self.yb)
        self.core = (r, f + 1 - 2 * self.c)
        self.diagonal = (r, f + 3 - 4 * self.yb - 2 * self.c)
        self.along = [None] + [(r, (f + 4 * k) % group) for k in range(1, planes)]
        self.planes, self.send_sems, self.recv_sems, self.copies = planes, send_sems, recv_sems, []

    def barrier(self, devices):
        semaphore = pltpu.get_barrier_semaphore()
        for device in devices:
            pl.semaphore_signal(
                semaphore, inc=1, device_id=device, device_id_type=pl.DeviceIdType.MESH
            )
        pl.semaphore_wait(semaphore, len(devices))

    def send(self, src, dst, device):
        n = len(self.copies)
        copy = pltpu.make_async_remote_copy(
            src_ref=src,
            dst_ref=dst,
            send_sem=self.send_sems.at[n],
            recv_sem=self.recv_sems.at[n],
            device_id=device,
            device_id_type=pl.DeviceIdType.MESH,
        )
        copy.start()
        self.copies.append(copy)
        return copy

    def finish(self):
        for copy in self.copies:
            copy.wait_send()


def comm_params(number):
    return pltpu.CompilerParams(
        collective_id=number, has_side_effects=True, vmem_limit_bytes=56 * 2**20
    )


def dma_pairs(count):
    return [pltpu.SemaphoreType.DMA((count,)), pltpu.SemaphoreType.DMA((count,))]


def whole_vmem():
    return pl.BlockSpec(memory_space=pltpu.VMEM)


def anywhere():
    return pl.BlockSpec(memory_space=pl.ANY)


def share_of(half, share):
    return int(half * share) // 128 * 128


def both_sides(values, store, pair):
    low = lax.broadcasted_iota(jnp.int32, values.shape, 1) < HEAD
    swapped = pltpu.roll(values, HEAD, 1)
    store(0, 2 * pair, jnp.where(low, values, 0.0).astype(BF))
    store(1, 2 * pair, jnp.where(low, 0.0, swapped).astype(BF))
    store(0, 2 * pair + 1, jnp.where(low, swapped, 0.0).astype(BF))
    store(1, 2 * pair + 1, jnp.where(low, 0.0, values).astype(BF))


def fill_bias(bias, start):
    length = bias.shape[0]

    def body(chunk):
        shape = (chunk.size, length)
        i = lax.broadcasted_iota(jnp.int32, shape, 0) + chunk.start
        j = lax.broadcasted_iota(jnp.int32, shape, 1)
        in_i = (i >= start) & (i < start + PIECE)
        in_j = (j >= start) & (j < start + PIECE)
        bias[chunk] = jnp.where((j <= i) | (in_i & in_j), 0.0, NEG_FILL)

    row_loop(length, 64, body)


def softmax_rows(query, key, bias):
    scores = dot_nt(query, key) + bias
    exponent = jnp.exp(scores - jnp.max(scores, axis=1, keepdims=True))
    return exponent * (1.0 / jnp.sum(exponent, axis=1, keepdims=True))


PAIRS = HEADS // 2
GROUP = HEADS // KV_HEADS
LANES = 2 * HEAD


def forward(starts, tokens, cotangent, own, w_gate, w_up, w_down, planes, group):
    length, width = tokens.shape
    ds, half = own.shape
    hid, hs = w_gate.shape[2], w_down.shape[0]
    wide = 3 * hid
    part = share_of(half, 0.25)
    first, second, every = (0, part), (part, half - part), (0, half)
    kvd = KV_HEADS * HEAD
    mix = width + 2 * kvd
    row_half = length // 2
    low_rows, high_rows = pl.ds(0, row_half), pl.ds(row_half, row_half)
    tables = turn_tables(length)

    def kernel(
        starts_ref,
        x_ref,
        cot_ref,
        own_ref,
        gate_hbm,
        up_hbm,
        down_hbm,
        tab_ref,
        front_out,
        wall_a,
        wall_b,
        grads_out,
        rows_out,
        gain_ref,
        q_ref,
        kk_ref,
        vv_ref,
        att_ref,
        res_ref,
        n1_ref,
        front,
        bias,
        n2_ref,
        packed,
        raw_in,
        raw_down,
        send_sems,
        recv_sems,
        local_sems,
        load_sems,
    ):
        at = Links(planes, group, send_sems, recv_sems)
        at.barrier([at.x, at.y, at.core, at.diagonal] + at.along[1:])
        walls = (wall_a, wall_b)
        shard = at.yb * 2 + at.c

        order = [(s, e) for e in range(EPD) for s in range(4)]

        def load(n):
            s, e = order[n]
            index = (at.xb * 4 + s) * EPD + e
            copies = [
                pltpu.make_async_copy(src, dst, load_sems.at[n % 2, i])
                for i, (src, dst) in enumerate(
                    (
                        (gate_hbm.at[:, index], raw_in.at[n % 2, 0]),
                        (up_hbm.at[:, index], raw_in.at[n % 2, 1]),
                        (down_hbm.at[:, index], raw_down.at[n % 2]),
                    )
                )
            ]
            for copy in copies:
                copy.start()
            return copies

        loads = {n: load(n) for n in range(2)}

        def pack(e):
            for n in range(4 * e, 4 * e + 4):
                s = order[n][0]
                for copy in loads[n]:
                    copy.wait()

                def cast(chunk, n=n, s=s):
                    packed[s, e, chunk, :hid] = raw_in[n % 2, 0, chunk].astype(BF)
                    packed[s, e, chunk, hid : 2 * hid] = raw_in[n % 2, 1, chunk].astype(BF)

                row_loop(ds, 16, cast)
                for i in range(width // hid):
                    packed[s, e, i * hs : (i + 1) * hs, 2 * hid :] = raw_down[
                        n % 2, :, i * hid : (i + 1) * hid
                    ].astype(BF)
                if n + 2 < len(order):
                    loads[n + 2] = load(n + 2)
            copy = pltpu.make_async_copy(
                packed.at[shard, e], walls[e].at[at.z, shard], local_sems.at[e]
            )
            copy.start()
            locals_.append(copy)

        locals_ = []

        def exchange(e):
            copies = []
            for dy, dc, device in ((1, 0, at.y), (1, 1, at.diagonal), (0, 1, at.core)):
                target = (at.yb + dy) % 2 * 2 + (at.c + dc) % 2
                copies.append(
                    at.send(packed.at[target, e], walls[e].at[at.z, shard], device)
                )
            return copies

        ring = {}

        def ring_first(e, copies):
            sent = [
                at.send(packed.at[shard, e], walls[e].at[at.z, shard], at.along[1])
            ]
            for copy, (dy, dc) in zip(copies, ((1, 0), (1, 1), (0, 1))):
                copy.wait_recv()
                piece = walls[e].at[at.z, (at.yb + dy) % 2 * 2 + (at.c + dc) % 2]
                sent.append(at.send(piece, piece, at.along[1]))
            ring[e] = (1, sent)

        def ring_next(e):
            step, sent = ring[e]
            for copy in sent:
                copy.wait_recv()
            if step < planes - 1:
                piece = walls[e].at[(at.z + planes - step) % planes]
                ring[e] = (step + 1, [at.send(piece, piece, at.along[1])])
            else:
                ring[e] = (planes, [])

        def region(k, dx, dy, span):
            row = (((at.z + planes - k) % planes) * 4 + (at.yb + dy) % 2 * 2 + at.c) * ds
            col = (at.xb + dx) % 2 * half + span[0]
            return front.at[
                pl.ds(pl.multiple_of(row, 16), ds), pl.ds(pl.multiple_of(col, 128), span[1])
            ]

        def pass_on(k, dx, dy, span, device):
            here = region(k, dx, dy, span)
            return at.send(here, here, device)

        x_first, x_second, y_first, y_second, far = [], [], [], [], []

        def spread(k):
            for device, span, copies in (
                (at.x, first, x_first),
                (at.y, second, y_second),
                (at.x, second, x_second),
                (at.y, first, y_first),
            ):
                here = region(k, 0, 0, span)
                src = own_ref.at[:, pl.ds(span[0], span[1])] if k == 0 else here
                copies.append(at.send(src, here, device))
            if k > 0:
                to_core.append(pass_on(k, 0, 0, every, at.core))

        def onward(k):
            x_first[k].wait_recv()
            far.append((k, first, pass_on(k, 1, 0, first, at.y)))
            y_second[k].wait_recv()
            far.append((k, second, pass_on(k, 0, 1, second, at.x)))
            x_second[k].wait_recv()
            to_core.append(pass_on(k, 1, 0, every, at.core))
            y_first[k].wait_recv()
            to_core.append(pass_on(k, 0, 1, every, at.core))

        own_copy = pltpu.make_async_copy(own_ref, region(0, 0, 0, every), local_sems.at[2])
        own_copy.start()
        arrive = [None] + [
            at.send(own_ref, region(0, 0, 0, every), at.along[k]) for k in range(1, planes)
        ]
        to_core = [at.send(own_ref, region(0, 0, 0, every), at.core)]
        spread(0)
        pack(0)
        first_exchange = exchange(0)
        pack(1)
        second_exchange = exchange(1)
        fill_bias(bias, starts_ref[0])
        for k in range(1, planes):
            arrive[k].wait_recv()
            spread(k)
            onward(k - 1)
        ring_first(0, first_exchange)
        ring_first(1, second_exchange)
        onward(planes - 1)
        for k, span, copy in far:
            copy.wait_recv()
            to_core.append(pass_on(k, 1, 1, span, at.core))
        for copy in to_core:
            copy.wait_recv()
        own_copy.wait()
        front_copy = pltpu.make_async_copy(front, front_out, local_sems.at[3])
        front_copy.start()

        def gather_start(src, out):
            def slot(j, rows=pl.ds(0, length)):
                return out.at[j, rows]

            got = {
                "x_low": at.send(src.at[low_rows], slot(4, low_rows), at.x),
                "y_high": at.send(src.at[high_rows], slot(2, high_rows), at.y),
                "x_high": at.send(src.at[high_rows], slot(4, high_rows), at.x),
                "y_low": at.send(src.at[low_rows], slot(2, low_rows), at.y),
                "core": [at.send(src, slot(1), at.core)],
            }
            return slot, got

        def gather_middle(slot, got):
            got["x_low"].wait_recv()
            got["far_low"] = at.send(slot(4, low_rows), slot(6, low_rows), at.y)
            got["core"].append(at.send(slot(4, low_rows), slot(5, low_rows), at.core))
            got["y_high"].wait_recv()
            got["far_high"] = at.send(slot(2, high_rows), slot(6, high_rows), at.x)
            got["core"].append(at.send(slot(2, high_rows), slot(3, high_rows), at.core))

        def gather_last(slot, got):
            got["x_high"].wait_recv()
            got["core"].append(at.send(slot(4, high_rows), slot(5, high_rows), at.core))
            got["y_low"].wait_recv()
            got["core"].append(at.send(slot(2, low_rows), slot(3, low_rows), at.core))
            got["far_low"].wait_recv()
            got["core"].append(at.send(slot(6, low_rows), slot(7, low_rows), at.core))
            got["far_high"].wait_recv()
            got["core"].append(at.send(slot(6, high_rows), slot(7, high_rows), at.core))

        grads = gather_start(cot_ref, grads_out)
        cot_copy = pltpu.make_async_copy(cot_ref, grads_out.at[0], local_sems.at[4])
        cot_copy.start()

        gain_ref[...] = front[:, mix + width : mix + width + 128].astype(F32).T[:8]

        def norm(chunk):
            x = x_ref[chunk].astype(F32)
            inv = lax.rsqrt(jnp.mean(x * x, axis=1, keepdims=True) + EPSILON)
            n1_ref[chunk] = (x * inv * gain_ref[0:1, :]).astype(BF)

        row_loop(length, 64, norm)
        block = 4 * LANES
        for n in range(mix // block):
            raw = dot(n1_ref[...], front[:, n * block : (n + 1) * block])
            for j in range(4):
                col = n * block + j * LANES
                values = raw[:, j * LANES : (j + 1) * LANES]
                if col < width:
                    turned_low = turned(values, tab_ref, 1.0).astype(BF).astype(F32)
                    q_ref[:, col : col + LANES] = (turned_low * (1.0 / math.sqrt(HEAD))).astype(BF)
                else:
                    target, base = (kk_ref, width) if col < width + kvd else (vv_ref, width + kvd)
                    if col < width + kvd:
                        values = turned(values, tab_ref, 1.0)

                    def store(side, head, side_values, target=target):
                        target[side, head] = side_values

                    both_sides(values, store, (col - base) // LANES)
        ring_next(0)

        def attend(pairs):
            @pl.loop(*pairs)
            def _(p):
                cols = pl.ds(pl.multiple_of(p * LANES, LANES), LANES)
                for n in range(length // 128):
                    rows = slice(n * 128, (n + 1) * 128)
                    total = None
                    for side in range(2):
                        head = (2 * p + side) // GROUP
                        probs = softmax_rows(q_ref[rows, cols], kk_ref[side, head], bias[rows])
                        term = dot(probs.astype(BF), vv_ref[side, head])
                        total = term if total is None else total + term
                    att_ref[rows, cols] = total.astype(BF)

        attend((0, PAIRS // 2))
        gather_middle(*grads)
        ring_next(1)
        attend((PAIRS // 2, PAIRS))
        for n in range(width // block):
            cols = slice(n * block, (n + 1) * block)
            res_ref[:, cols] = x_ref[:, cols].astype(F32) + dot(
                att_ref[...], front[:, mix + n * block : mix + (n + 1) * block]
            )

        def norm_two(chunk):
            r = res_ref[chunk]
            inv = lax.rsqrt(jnp.mean(r * r, axis=1, keepdims=True) + EPSILON)
            n2_ref[chunk] = (r * inv * gain_ref[1:2, :]).astype(BF)

        row_loop(length, 64, norm_two)
        rows = gather_start(n2_ref, rows_out)
        rows_copy = pltpu.make_async_copy(n2_ref, rows_out.at[0], local_sems.at[5])
        rows_copy.start()
        gather_last(*grads)
        gather_middle(*rows)
        ring_next(0)
        gather_last(*rows)
        for e in (1, 0):
            while ring[e][0] < planes:
                ring_next(e)
        for copy in grads[1]["core"] + rows[1]["core"]:
            copy.wait_recv()
        for copy in locals_ + [front_copy, cot_copy, rows_copy]:
            copy.wait()
        at.finish()

    shape = jax.ShapeDtypeStruct
    count = planes - 1 + planes * 11 + 2 * 3 + 2 * (4 + planes - 2) + 2 * 13
    return pl.pallas_call(
        kernel,
        out_shape=[
            shape((width, 2 * half), BF),
            shape((planes, 4, ds, wide), BF),
            shape((planes, 4, ds, wide), BF),
            shape((PLANE, length, width), BF),
            shape((PLANE, length, width), BF),
            shape((8, width), F32),
            shape((length, width), BF),
            shape((2, KV_HEADS, length, LANES), BF),
            shape((2, KV_HEADS, length, LANES), BF),
            shape((length, width), BF),
            shape((length, width), F32),
            shape((length, width), BF),
        ],
        in_specs=[pl.BlockSpec(memory_space=pltpu.SMEM)]
        + [whole_vmem()] * 3
        + [anywhere()] * 3
        + [whole_vmem()],
        out_specs=[anywhere()] * 5 + [whole_vmem()] * 7,
        scratch_shapes=[
            pltpu.VMEM((width, 2 * half), BF),
            pltpu.VMEM((length, length), F32),
            pltpu.VMEM((length, width), BF),
            pltpu.VMEM((4, EPD, ds, wide), BF),
            pltpu.VMEM((2, 2, ds, hid), F32),
            pltpu.VMEM((2, hs, width), F32),
        ]
        + dma_pairs(count)
        + [pltpu.SemaphoreType.DMA((6,)), pltpu.SemaphoreType.DMA((2, 3))],
        compiler_params=comm_params(0),
        cost_estimate=pl.CostEstimate(
            flops=150_000_000_000, bytes_accessed=20_000_000, transcendentals=0
        ),
    )(starts, tokens, cotangent, own, w_gate, w_up, w_down, tables)


def expert(rows, grads, share, pack, before, group):
    count, width = rows.shape
    hid = width // 3
    tile = 512
    ds, hs, blocks = width // group, hid // group, width // hid

    def kernel(*refs):
        x_ref, g_ref, s_ref, w_ref = refs[:4]
        old = refs[4:6] if before else None
        o_ref, dx_ref, dw_ref, down, in_sum, down_sum, pre, act = refs[6 if before else 4 :]
        step = pl.program_id(0)

        @pl.when(step == 0)
        def _():
            for s in range(group):
                for b in range(blocks):
                    down[s * hs : (s + 1) * hs, b * hid : (b + 1) * hid] = w_ref[
                        s * ds + b * hs : s * ds + (b + 1) * hs, 2 * hid :
                    ]
            in_sum[...] = jnp.zeros_like(in_sum)
            down_sum[...] = jnp.zeros_like(down_sum)

        half = hid // 2
        for n in range(2):
            cols = slice(n * half, (n + 1) * half)
            up_cols = slice(hid + n * half, hid + (n + 1) * half)
            gate = dot(x_ref[...], w_ref[:, cols])
            up = dot(x_ref[...], w_ref[:, up_cols])
            inner = dot_nt(g_ref[...], down[cols, :]) * s_ref[...]
            sig = jax.nn.sigmoid(gate)
            swish = gate * sig
            act[:, cols] = (s_ref[...] * (swish * up)).astype(BF)
            pre[:, cols] = (inner * up * sig * (1.0 + gate * (1.0 - sig))).astype(BF)
            pre[:, up_cols] = (inner * swish).astype(BF)
        for n in range(width // hid):
            cols = slice(n * hid, (n + 1) * hid)
            out = dot(act[...], down[:, cols])
            dx = dot_nt(pre[...], w_ref[cols, : 2 * hid])
            if before:
                out = out + old[0][:, cols].astype(F32)
                dx = dx + old[1][:, cols].astype(F32)
            o_ref[:, cols] = out.astype(BF)
            dx_ref[:, cols] = dx.astype(BF)
            in_sum[cols, :] += dot_tn(x_ref[:, cols], pre[...])
            down_sum[:, cols] += dot_tn(act[...], g_ref[:, cols])

        @pl.when(step == count // tile - 1)
        def _():
            dw_ref[:, : 2 * hid] = in_sum[...].astype(BF)
            for s in range(group):
                for b in range(blocks):
                    dw_ref[s * ds + b * hs : s * ds + (b + 1) * hs, 2 * hid :] = down_sum[
                        s * hs : (s + 1) * hs, b * hid : (b + 1) * hid
                    ].astype(BF)

    tiles = pl.BlockSpec((tile, width), lambda i: (i, 0))
    whole = pl.BlockSpec((width, width), lambda i: (0, 0))
    shape = jax.ShapeDtypeStruct
    return pl.pallas_call(
        kernel,
        grid=(count // tile,),
        in_specs=[tiles, tiles, pl.BlockSpec((tile, 1), lambda i: (i, 0)), whole]
        + [tiles] * len(before),
        out_specs=[tiles, tiles, whole],
        out_shape=[shape((count, width), BF), shape((count, width), BF), shape((width, width), BF)],
        scratch_shapes=[
            pltpu.VMEM((hid, width), BF),
            pltpu.VMEM((width, 2 * hid), F32),
            pltpu.VMEM((hid, width), F32),
            pltpu.VMEM((tile, 2 * hid), BF),
            pltpu.VMEM((tile, hid), BF),
        ],
        compiler_params=pltpu.CompilerParams(vmem_limit_bytes=58 * 2**20),
        cost_estimate=pl.CostEstimate(
            flops=44_000_000_000, bytes_accessed=50_000_000, transcendentals=0
        ),
    )(rows, grads, share, pack, *before)


class PlaneSum:
    def __init__(self, at, odd, even, from_core, far, near):
        self.at, self.odd, self.even, self.core = at, odd, even, from_core
        self.far, self.near = far, near
        self.length = from_core.shape[1]
        self.half = self.length // 2
        self.low, self.high = pl.ds(0, self.half), pl.ds(self.half, self.half)

    def start(self):
        self.arrive = {
            j: self.at.send(self.odd(j), self.core.at[j], self.at.core) for j in (3, 2, 1, 0)
        }

    def add_core(self, j):
        self.arrive[j].wait_recv()
        core = self.core

        def store(chunk, total):
            core[j, chunk] = total.astype(BF)

        add_rows(store, [lambda q: self.even(j, q), lambda q: core[j, q]], self.length)

    def add_far(self, j, n, base):
        core, far = self.core, self.far

        def moved(chunk):
            return pl.ds(pl.multiple_of(chunk.start + base, 16), chunk.size)

        def store(chunk, total):
            core[j, moved(chunk)] = total.astype(BF)

        add_rows(store, [lambda q: core[j, moved(q)], lambda q: far[n, q]], self.half)

    def neighbours(self):
        at, core, far, near, low, high = self.at, self.core, self.far, self.near, self.low, self.high
        self.add_core(3)
        self.far_y = at.send(core.at[3, low], far.at[0], at.y)
        self.far_x = at.send(core.at[3, high], far.at[1], at.x)
        self.add_core(2)
        self.last = [at.send(core.at[2, high], near.at[0, high], at.x)]
        self.add_core(1)
        self.last.append(at.send(core.at[1, low], near.at[1, low], at.y))

    def onward(self):
        at, core, near, low, high = self.at, self.core, self.near, self.low, self.high
        self.far_y.wait_recv()
        self.add_far(2, 0, 0)
        self.last.append(at.send(core.at[2, low], near.at[0, low], at.x))
        self.far_x.wait_recv()
        self.add_far(1, 1, self.half)
        self.last.append(at.send(core.at[1, high], near.at[1, high], at.y))

    def end(self, store):
        self.arrive[0].wait_recv()
        for copy in self.last:
            copy.wait_recv()
        core, near = self.core, self.near
        terms = [lambda q: self.even(0, q), lambda q: core[0, q]]
        terms += [lambda q: near[0, q], lambda q: near[1, q]]
        add_rows(store, terms, self.length)

    copies = 10


class RingSum:
    def __init__(self, at, pack, own, own_sem):
        self.at, self.pack, self.own, self.own_sem = at, pack, own, own_sem

    def block(self, k):
        return self.pack.at[(self.at.z + self.at.planes - k) % self.at.planes]

    def fetch(self, k):
        self.fetched = pltpu.make_async_copy(self.block(k), self.own, self.own_sem)
        self.fetched.start()

    def add(self, source, target):
        self.fetched.wait()

        def store(chunk, total):
            target[chunk] = total.astype(BF)

        add_rows(store, [lambda q: source[q], lambda q: self.own[q]], self.own.shape[0], 16)

    def first(self, slots):
        self.slots, self.step = slots, 1
        self.copy = self.at.send(self.block(1), slots[0], self.at.along[1])
        self.fetch(2)

    def next(self):
        if self.step < len(self.slots):
            here = self.slots[self.step - 1]
            self.copy.wait_recv()
            self.add(here, here)
            self.copy = self.at.send(here, self.slots[self.step], self.at.along[1])
            self.step += 1
            if self.step < len(self.slots):
                self.fetch(self.step + 1)

    def rest(self):
        while self.step < len(self.slots):
            self.next()
        self.copy.wait_recv()

    def last(self, before, sent, landing):
        self.add(before, sent)
        self.landing = landing
        self.copy = self.at.send(sent, landing, self.at.along[1])
        self.fetch(0)

    def total(self):
        self.copy.wait_recv()
        self.add(self.landing, self.landing)
        return self.landing


class Exchange:
    def __init__(self, at, total, out, ds):
        self.at, self.total, self.out, self.ds = at, total, out, ds
        self.shard = at.yb * 2 + at.c

    def place(self, dx, dy, dc):
        at = self.at
        return (at.xb + dx) % 2 * 4 + (at.yb + dy) % 2 * 2 + (at.c + dc) % 2

    def rows(self, dy, dc):
        at = self.at
        shard = (at.yb + dy) % 2 * 2 + (at.c + dc) % 2
        return self.total.at[pl.ds(pl.multiple_of(shard * self.ds, 16), self.ds)]

    def start(self, sem):
        at = self.at
        here = self.out.at[self.place(0, 0, 0)]
        self.local = pltpu.make_async_copy(self.rows(0, 0), here, sem)
        self.local.start()
        self.got = [
            (dy, dc, at.send(self.rows(dy, dc), here, device))
            for dy, dc, device in ((1, 0, at.y), (1, 1, at.diagonal), (0, 1, at.core))
        ]
        self.across = [at.send(self.rows(0, 0), here, at.x)]

    def onward(self):
        at = self.at
        for dy, dc, copy in self.got:
            copy.wait_recv()
            piece = self.out.at[self.place(0, dy, dc)]
            self.across.append(at.send(piece, piece, at.x))

    def end(self):
        for copy in self.across:
            copy.wait_recv()
        self.local.wait()

    copies = 7


def backward(
    starts,
    grad_two,
    cotangent,
    tokens,
    residual,
    front,
    gains,
    q,
    kk,
    vv,
    att,
    n1,
    outs,
    pack_a,
    before_a,
    pack_b,
    planes,
    group,
):
    length, width = tokens.shape
    columns = front.shape[1]
    kvd = KV_HEADS * HEAD
    mix = width + 2 * kvd
    block = 4 * LANES
    tables = turn_tables(length)
    piece, wide = pack_a.shape[1:]
    ds = piece // 4
    extra = columns - mix - width

    def kernel(
        starts_ref,
        d_ref,
        cot_ref,
        tab_ref,
        gain_ref,
        q_ref,
        kk_ref,
        vv_ref,
        att_ref,
        before_ref,
        x_hbm,
        n1_hbm,
        res_hbm,
        w_hbm,
        outs_ref,
        pack_a_ref,
        pack_b_ref,
        in_ref,
        sum_ref,
        passed_b,
        grad_hbm,
        shards_ref,
        bias,
        gain_sum,
        mixed,
        context,
        grad_mix,
        key_sum,
        value_sum,
        w_ref,
        stage,
        even,
        from_core,
        far,
        near,
        own_a,
        sent_a,
        landing_a,
        own_b,
        slots_b,
        send_sems,
        recv_sems,
        local_sems,
    ):
        at = Links(planes, group, send_sems, recv_sems)
        at.barrier([at.x, at.y, at.core, at.diagonal] + at.along[1:])

        def local(src, dst, n):
            copy = pltpu.make_async_copy(src, dst, local_sems.at[n])
            copy.start()
            return copy

        load_res = local(res_hbm, in_ref, 0)
        load_out_w = local(
            w_hbm.at[:, pl.ds(mix, width)], w_ref.at[:, pl.ds(0, width)], 1
        )
        plane = PlaneSum(
            at, lambda j: outs_ref.at[2 * j + 1], lambda j, q: even[j, q], from_core, far, near
        )
        plane.start()
        ring_a = RingSum(at, pack_a_ref, own_a, local_sems.at[6])
        ring_b = RingSum(at, pack_b_ref, own_b, local_sems.at[7])
        ring_a.fetch(planes - 1)
        loads = [local(outs_ref.at[2 * j], even.at[j], 2 + j) for j in range(4)]
        ring_a.last(before_ref, sent_a, landing_a)
        ring_b.first([slots_b.at[n] for n in range(planes - 3)] + [passed_b])
        staged = [None, None]
        turn = [0]

        def put(values, column, count):
            n = turn[0] % 2
            turn[0] += 1
            if staged[n] is not None:
                staged[n].wait()
            stage[n, :, :count] = values
            staged[n] = local(
                stage.at[n, :, pl.ds(0, count)], grad_hbm.at[:, pl.ds(column, count)], 8 + n
            )

        fill_bias(bias, starts_ref[0])
        gain_sum[...] = jnp.zeros_like(gain_sum)

        load_res.wait()

        def residual_grad(chunk):
            d, r = d_ref[chunk], in_ref[chunk]
            inv = lax.rsqrt(jnp.mean(r * r, axis=1, keepdims=True) + EPSILON)
            scaled = d * gain_ref[1:2, :]
            grad = (
                cot_ref[chunk].astype(F32)
                + inv * scaled
                - r * (inv * inv * inv * jnp.mean(scaled * r, axis=1, keepdims=True))
            )
            sum_ref[chunk] = grad
            mixed[chunk] = grad.astype(BF)
            gain_sum[1:2, :] += jnp.sum(d * r * inv, axis=0, keepdims=True)

        row_loop(length, 32, residual_grad)
        load_out_w.wait()
        for n in range(width // block):
            cols = slice(n * block, (n + 1) * block)
            context[:, cols] = dot_nt(mixed[...], w_ref[cols, :width]).astype(BF)
        load_mix_w = local(w_hbm.at[:, pl.ds(0, mix)], w_ref, 1)
        for n in range(width // block):
            cols = slice(n * block, (n + 1) * block)
            put(dot_tn(att_ref[...], mixed[:, cols]).astype(BF), mix + n * block, block)
        load_n1 = local(n1_hbm, mixed, 0)
        for copy in loads:
            copy.wait()
        plane.neighbours()
        key_sum[...] = jnp.zeros_like(key_sum)
        value_sum[...] = jnp.zeros_like(value_sum)

        def attend(lower, upper):
            @pl.loop(lower, upper)
            def _(p):
                cols = pl.ds(pl.multiple_of(p * LANES, LANES), LANES)
                for n in range(length // 128):
                    rows = slice(n * 128, (n + 1) * 128)
                    total = None
                    for side in range(2):
                        head = (2 * p + side) // GROUP
                        query, grad = q_ref[rows, cols], context[rows, cols]
                        probs = softmax_rows(query, kk_ref[side, head], bias[rows])
                        grad_probs = dot_nt(grad, vv_ref[side, head])
                        value_sum[side, head] += dot_tn(probs.astype(BF), grad)
                        inner = jnp.sum(probs * grad_probs, axis=1, keepdims=True)
                        logit = (probs * (grad_probs - inner)).astype(BF)
                        term = dot(logit, kk_ref[side, head])
                        total = term if total is None else total + term
                        key_sum[side, head] += dot_tn(logit, query)
                    back = turned(total, tab_ref.at[:, rows], -1.0) * (1.0 / math.sqrt(HEAD))
                    grad_mix[rows, cols] = back.astype(BF)

        attend(0, PAIRS // 3)
        plane.onward()
        exchange = Exchange(at, ring_a.total(), shards_ref, ds)
        exchange.start(local_sems.at[10])
        attend(PAIRS // 3, 2 * PAIRS // 3)
        ring_b.next()
        exchange.onward()
        attend(2 * PAIRS // 3, PAIRS)
        load_x = local(x_hbm, context, 11)
        load_n1.wait()
        for pair in range(KV_HEADS // 2):
            for sums, base in ((key_sum, width), (value_sum, width + kvd)):

                def join(chunk, pair=pair, sums=sums, base=base):
                    low = lax.broadcasted_iota(jnp.int32, (chunk.size, LANES), 1) < HEAD
                    even = sums[0, 2 * pair, chunk] + pltpu.roll(sums[1, 2 * pair, chunk], HEAD, 1)
                    odd = sums[1, 2 * pair + 1, chunk] + pltpu.roll(
                        sums[0, 2 * pair + 1, chunk], HEAD, 1
                    )
                    values = jnp.where(low, even, odd)
                    if base == width:
                        values = turned(values, tab_ref.at[:, chunk], -1.0)
                    grad_mix[chunk, base + pair * LANES : base + (pair + 1) * LANES] = values.astype(BF)

                row_loop(length, 64, join)
        for n in range(mix // block):
            cols = slice(n * block, (n + 1) * block)
            put(dot_tn(mixed[...], grad_mix[:, cols]).astype(BF), n * block, block)
        load_mix_w.wait()
        for n in range(width // block):
            cols = slice(n * block, (n + 1) * block)
            in_ref[:, cols] = dot_nt(grad_mix[...], w_ref[cols, :mix])

        load_x.wait()

        def input_grad(chunk):
            d, x = in_ref[chunk], context[chunk].astype(F32)
            inv = lax.rsqrt(jnp.mean(x * x, axis=1, keepdims=True) + EPSILON)
            scaled = d * gain_ref[0:1, :]
            gain_sum[0:1, :] += jnp.sum(d * x * inv, axis=0, keepdims=True)
            in_ref[chunk] = (
                sum_ref[chunk]
                + inv * scaled
                - x * (inv * inv * inv * jnp.mean(scaled * x, axis=1, keepdims=True))
            )

        row_loop(length, 32, input_grad)
        gain_rows = jnp.concatenate([gain_sum[...].T, jnp.zeros((width, extra - 8), F32)], axis=1)
        put(gain_rows.astype(BF), mix + width, extra)

        def store(chunk, total):
            sum_ref[chunk] = total

        plane.end(store)
        ring_b.rest()
        exchange.end()
        for copy in staged:
            copy.wait()
        at.finish()

    shape = jax.ShapeDtypeStruct
    return pl.pallas_call(
        kernel,
        in_specs=[pl.BlockSpec(memory_space=pltpu.SMEM)]
        + [whole_vmem()] * 9
        + [anywhere()] * 7,
        out_specs=[whole_vmem()] * 3 + [anywhere()] * 2,
        out_shape=[
            shape((length, width), F32),
            shape((length, width), F32),
            shape((piece, wide), BF),
            shape((width, columns), BF),
            shape((PLANE, ds, wide), BF),
        ],
        scratch_shapes=[
            pltpu.VMEM((length, length), F32),
            pltpu.VMEM((8, width), F32),
            pltpu.VMEM((length, width), BF),
            pltpu.VMEM((length, width), BF),
            pltpu.VMEM((length, mix), BF),
            pltpu.VMEM((2, KV_HEADS, length, LANES), F32),
            pltpu.VMEM((2, KV_HEADS, length, LANES), F32),
            pltpu.VMEM((width, mix), BF),
            pltpu.VMEM((2, width, block), BF),
            pltpu.VMEM((4, length, width), BF),
            pltpu.VMEM((4, length, width), BF),
            pltpu.VMEM((2, length // 2, width), BF),
            pltpu.VMEM((2, length, width), BF),
            pltpu.VMEM((piece, wide), BF),
            pltpu.VMEM((piece, wide), BF),
            pltpu.VMEM((piece, wide), BF),
            pltpu.VMEM((piece, wide), BF),
            pltpu.VMEM((planes - 3, piece, wide), BF),
        ]
        + dma_pairs(PlaneSum.copies + 1 + Exchange.copies + planes - 2)
        + [pltpu.SemaphoreType.DMA((12,))],
        compiler_params=pltpu.CompilerParams(
            collective_id=1, has_side_effects=True, vmem_limit_bytes=62 * 2**20
        ),
        cost_estimate=pl.CostEstimate(
            flops=80_000_000_000, bytes_accessed=50_000_000, transcendentals=0
        ),
    )(
        starts,
        grad_two,
        cotangent,
        tables,
        gains,
        q,
        kk,
        vv,
        att,
        before_a,
        tokens,
        n1,
        residual,
        front,
        outs,
        pack_a,
        pack_b,
    )


def scatter_plane(partial, pack, planes, group):
    slots, length, width = partial.shape
    half = length // 2
    block, wide = pack.shape[1:]

    def kernel(
        p_ref, pack_ref, out_ref, passed, even, from_core, far, near, ring_slots, own, send_sems, recv_sems, local_sems
    ):
        at = Links(planes, group, send_sems, recv_sems)
        at.barrier([at.x, at.y, at.core] + at.along[1:])
        ring = RingSum(at, pack_ref, own, local_sems.at[4])
        loads = []
        for j in range(4):
            loads.append(pltpu.make_async_copy(p_ref.at[2 * j], even.at[j], local_sems.at[j]))
            loads[-1].start()
        plane = PlaneSum(
            at, lambda j: p_ref.at[2 * j + 1], lambda j, q: even[j, q], from_core, far, near
        )
        plane.start()
        ring.first([ring_slots.at[n] for n in range(planes - 3)] + [passed])
        for copy in loads:
            copy.wait()
        plane.neighbours()
        plane.onward()
        ring.next()

        def store(chunk, total):
            out_ref[chunk] = total

        plane.end(store)
        ring.rest()
        at.finish()

    return pl.pallas_call(
        kernel,
        out_shape=[
            jax.ShapeDtypeStruct((length, width), F32),
            jax.ShapeDtypeStruct((block, wide), BF),
        ],
        in_specs=[anywhere(), anywhere()],
        out_specs=[whole_vmem(), whole_vmem()],
        scratch_shapes=[
            pltpu.VMEM((4, length, width), BF),
            pltpu.VMEM((4, length, width), BF),
            pltpu.VMEM((2, half, width), BF),
            pltpu.VMEM((2, length, width), BF),
            pltpu.VMEM((planes - 3, block, wide), BF),
            pltpu.VMEM((block, wide), BF),
        ]
        + dma_pairs(PlaneSum.copies + planes - 2)
        + [pltpu.SemaphoreType.DMA((5,))],
        compiler_params=comm_params(2),
        cost_estimate=pl.CostEstimate(
            flops=45_000_000_000, bytes_accessed=20_000_000, transcendentals=0
        ),
    )(partial, pack)


def scatter_front(grad, pack, before, planes, group):
    rows, columns = grad.shape
    ds, half = rows // (4 * planes), columns // 2
    part = share_of(half, 0.6)
    first, second = pl.ds(0, part), pl.ds(part, half - part)
    block, wide = pack.shape[1:]

    def kernel(
        g_ref,
        pack_ref,
        before_ref,
        out_ref,
        shards_ref,
        from_core,
        kept,
        far_a,
        far_b,
        near_x,
        near_y,
        total_ref,
        from_z,
        own,
        passed,
        landing,
        send_sems,
        recv_sems,
        local_sems,
    ):
        at = Links(planes, group, send_sems, recv_sems)
        at.barrier([at.x, at.y, at.core, at.diagonal] + at.along[1:])
        ring = RingSum(at, pack_ref, own, local_sems.at[0])
        ring.fetch(planes - 1)

        def row(k, dy, core):
            owner = ((at.z + k) % planes) * 4 + (at.yb + dy) % 2 * 2 + core
            return pl.multiple_of(owner * ds, 16)

        def column(dx):
            return pl.ds(pl.multiple_of((at.xb + dx) % 2 * half, 128), half)

        order = list(range(1, planes)) + [0]
        arrive = {}
        for k in order:
            for dy in (1, 0):
                arrive[k, dy] = at.send(
                    g_ref.at[pl.ds(row(k, dy, 1 - at.c), ds)], from_core.at[k, dy], at.core
                )
        ring.last(before_ref, passed, landing)
        step = 16
        x_second, y_first, x_first, y_second, to_x, to_y = {}, {}, {}, {}, {}, {}
        for k in order:
            for dy in (1, 0):
                arrive[k, dy].wait_recv()
                for dx in (1, 0):

                    def store(chunk, total, k=k, dx=dx, dy=dy):
                        kept[k, dx, dy, chunk] = total.astype(BF)

                    add_rows(
                        store,
                        [
                            lambda q, k=k, dx=dx, dy=dy: g_ref[
                                pl.ds(pl.multiple_of(row(k, dy, at.c) + q.start, 16), q.size),
                                column(dx),
                            ],
                            lambda q, k=k, dx=dx, dy=dy: from_core[k, dy, q, column(dx)],
                        ],
                        ds,
                        step,
                    )
                    if (dx, dy) == (1, 1):
                        to_y[k] = at.send(kept.at[k, 1, 1, :, first], far_a.at[k], at.y)
                        to_x[k] = at.send(kept.at[k, 1, 1, :, second], far_b.at[k], at.x)
                    elif (dx, dy) == (0, 1):
                        y_first[k] = at.send(
                            kept.at[k, 0, 1, :, first], near_y.at[k, :, first], at.y
                        )
                    elif (dx, dy) == (1, 0):
                        x_second[k] = at.send(
                            kept.at[k, 1, 0, :, second], near_x.at[k, :, second], at.x
                        )
        for k in order:
            to_y[k].wait_recv()

            def store(chunk, total, k=k):
                kept[k, 1, 0, chunk, first] = total.astype(BF)

            add_rows(
                store,
                [lambda q, k=k: kept[k, 1, 0, q, first], lambda q, k=k: far_a[k, q]],
                ds,
                step,
            )
            x_first[k] = at.send(kept.at[k, 1, 0, :, first], near_x.at[k, :, first], at.x)
            to_x[k].wait_recv()

            def store(chunk, total, k=k):
                kept[k, 0, 1, chunk, second] = total.astype(BF)

            add_rows(
                store,
                [lambda q, k=k: kept[k, 0, 1, q, second], lambda q, k=k: far_b[k, q]],
                ds,
                step,
            )
            y_second[k] = at.send(kept.at[k, 0, 1, :, second], near_y.at[k, :, second], at.y)
        exchange = Exchange(at, ring.total(), shards_ref, ds)
        exchange.start(local_sems.at[1])
        arrive_z = {}
        for k in order:
            for copies in (x_second, y_first, x_first, y_second):
                copies[k].wait_recv()

            def store(chunk, total, k=k):
                total_ref[k, chunk] = total.astype(BF)

            add_rows(
                store,
                [
                    lambda q, k=k: kept[k, 0, 0, q],
                    lambda q, k=k: near_x[k, q],
                    lambda q, k=k: near_y[k, q],
                ],
                ds,
                step,
            )
            if k > 0:
                arrive_z[k] = at.send(total_ref.at[k], from_z.at[k], at.along[k])
        exchange.onward()
        for k in range(1, planes):
            arrive_z[k].wait_recv()

        def store(chunk, total):
            out_ref[chunk] = total.astype(BF)

        add_rows(
            store,
            [lambda q: total_ref[0, q]]
            + [lambda q, k=k: from_z[k, q] for k in range(1, planes)],
            ds,
            step,
        )
        exchange.end()
        at.finish()

    return pl.pallas_call(
        kernel,
        out_shape=[
            jax.ShapeDtypeStruct((ds, half), BF),
            jax.ShapeDtypeStruct((PLANE, ds, wide), BF),
        ],
        in_specs=[whole_vmem(), anywhere(), whole_vmem()],
        out_specs=[whole_vmem(), anywhere()],
        scratch_shapes=[
            pltpu.VMEM((planes, 2, ds, columns), BF),
            pltpu.VMEM((planes, 2, 2, ds, half), BF),
            pltpu.VMEM((planes, ds, part), BF),
            pltpu.VMEM((planes, ds, half - part), BF),
            pltpu.VMEM((planes, ds, half), BF),
            pltpu.VMEM((planes, ds, half), BF),
            pltpu.VMEM((planes, ds, half), BF),
            pltpu.VMEM((planes, ds, half), BF),
            pltpu.VMEM((block, wide), BF),
            pltpu.VMEM((block, wide), BF),
            pltpu.VMEM((block, wide), BF),
        ]
        + dma_pairs(planes * 8 + planes - 1 + 1 + Exchange.copies)
        + [pltpu.SemaphoreType.DMA((2,))],
        compiler_params=comm_params(3),
        cost_estimate=pl.CostEstimate(
            flops=50_000_000_000, bytes_accessed=20_000_000, transcendentals=0
        ),
    )(grad, pack, before)


def unpack(packs, hs):
    ds, wide = packs[0].shape[1:]
    hid = wide // 3
    blocks = ds // hs

    def kernel(*refs):
        ins, (gate_out, up_out, down_out, raw_in, raw_down, sems) = refs[:EPD], refs[EPD:]
        copies = {}
        for n, (p, e) in enumerate((p, e) for p in range(PLANE) for e in range(EPD)):
            slot = n % 4
            if n >= 4:
                for copy in copies[n - 4]:
                    copy.wait()

            def cast(chunk, p=p, e=e, slot=slot):
                raw_in[slot, 0, chunk] = ins[e][p, chunk, :hid].astype(F32)
                raw_in[slot, 1, chunk] = ins[e][p, chunk, hid : 2 * hid].astype(F32)

            row_loop(ds, 16, cast)
            for b in range(blocks):
                raw_down[slot, :, b * hid : (b + 1) * hid] = ins[e][
                    p, b * hs : (b + 1) * hs, 2 * hid :
                ].astype(F32)
            index = p * EPD + e
            copies[n] = [
                pltpu.make_async_copy(src, dst, sems.at[slot, i])
                for i, (src, dst) in enumerate(
                    (
                        (raw_in.at[slot, 0], gate_out.at[:, index]),
                        (raw_in.at[slot, 1], up_out.at[:, index]),
                        (raw_down.at[slot], down_out.at[:, index]),
                    )
                )
            ]
            for copy in copies[n]:
                copy.start()
        for n in range(EXP - 4, EXP):
            for copy in copies[n]:
                copy.wait()

    shape = jax.ShapeDtypeStruct
    return pl.pallas_call(
        kernel,
        in_specs=[whole_vmem()] * EPD,
        out_specs=[anywhere()] * 3,
        out_shape=[
            shape((ds, EXP, hid), F32),
            shape((ds, EXP, hid), F32),
            shape((hs, EXP, blocks * hid), F32),
        ],
        scratch_shapes=[
            pltpu.VMEM((4, 2, ds, hid), F32),
            pltpu.VMEM((4, hs, blocks * hid), F32),
            pltpu.SemaphoreType.DMA((4, 3)),
        ],
        compiler_params=pltpu.CompilerParams(vmem_limit_bytes=32 * 2**20),
    )(*packs)


def shards(
    reps,
    group,
    tokens,
    cotangent,
    routes,
    gates,
    starts,
    norm1_gain,
    w_query,
    w_key,
    w_value,
    w_out,
    norm2_gain,
    w_gate,
    w_up,
    w_down,
):
    planes = group // 4
    r, f = lax.axis_index("rep"), lax.axis_index("fsdp")
    xb, yb, c, z = r % 2, (f // 2) % 2, f % 2, f // 4
    mine = xb * 4 + yb * 2 + c

    def perm(to):
        return [
            (a * group + b, to(a, b)[0] * group + to(a, b)[1])
            for a in range(reps)
            for b in range(group)
        ]

    def pp(value, to):
        return lax.ppermute(value, AXES, perm(to))

    def go(value, dx, dy, dc):
        return pp(value, lambda a, b: (a ^ dx, b ^ (dy * 2 + dc)))

    def along(value, k):
        return pp(value, lambda a, b: (a, (b + 4 * k) % group))

    def all_reps(value):
        step = 2
        while step < reps:
            value = value + pp(value, lambda a, b, s=step: (a ^ s, b))
            step *= 2
        return value

    length, width = tokens.shape
    ds = w_query.shape[0]
    hs = w_down.shape[0]
    hid = w_gate.shape[2]
    kvd = w_key.shape[1]
    half_rows = length // 2

    mix = width + 2 * kvd
    columns = mix + width + 256
    half = columns // 2
    gains = jnp.stack([norm1_gain.astype(BF), norm2_gain.astype(BF)], axis=1)
    front_own = jnp.concatenate(
        [
            w_query.astype(BF),
            w_key.astype(BF),
            w_value.astype(BF),
            w_out.astype(BF),
            gains,
            jnp.zeros((ds, 254), BF),
        ],
        axis=1,
    )
    experts = jnp.arange(EXP, dtype=jnp.int32)[:, None, None]
    share = jnp.sum(jnp.where(routes[None] == experts, gates[None], 0.0), axis=2)
    shares = []
    for j in range(PLANE):
        block = lax.dynamic_slice(share, ((mine ^ j) * EPD, 0), (EPD, length))
        shares.append(block if j == 0 else go(block, j // 4, (j // 2) % 2, j % 2))
    shares = jnp.concatenate(shares, axis=1)

    front, wall_a, wall_b, grads_all, rows_all, gains_all, q, kk, vv, att, residual, n1 = forward(
        starts,
        tokens,
        cotangent,
        lax.dynamic_slice(front_own, (0, xb * half), (ds, half)),
        w_gate,
        w_up,
        w_down,
        planes,
        group,
    )
    grads_all = grads_all.reshape(PLANE * length, width)
    rows_all = rows_all.reshape(PLANE * length, width)
    before, pack_grads = (), []
    for e, wall in enumerate((wall_a, wall_b)):
        *before, pack_grad = expert(
            rows_all, grads_all, shares[e][:, None], wall.reshape(width, 3 * hid), before, group
        )
        pack_grads.append(pack_grad)
    out_sum, row_sum = before
    pack_a, pack_b = [grad.reshape(planes, 4 * ds, 3 * hid) for grad in pack_grads]
    grad_normed_two, before_a = scatter_plane(
        row_sum.reshape(PLANE, length, width), pack_a, planes, group
    )
    input_grad, out_term, before_b, front_grad, shards_a = backward(
        starts,
        grad_normed_two,
        cotangent,
        tokens,
        residual,
        front,
        gains_all,
        q,
        kk,
        vv,
        att,
        n1,
        out_sum.reshape(PLANE, length, width),
        pack_a,
        before_a,
        pack_b,
        planes,
        group,
    )
    output = residual + out_term
    front_total, shards_b = scatter_front(front_grad, pack_b, before_b, planes, group)
    total = all_reps(front_total)
    gate_shard, up_shard, down_shard = unpack([all_reps(shards_a), all_reps(shards_b)], hs)
    other = go(total, 1, 0, 0)
    front_shard = jnp.where(
        xb == 0,
        jnp.concatenate([total, other], axis=1),
        jnp.concatenate([other, total], axis=1),
    ).astype(F32)
    return (
        output,
        input_grad,
        front_shard[:, mix + width],
        front_shard[:, :width],
        front_shard[:, width : width + kvd],
        front_shard[:, width + kvd : mix],
        front_shard[:, mix : mix + width],
        front_shard[:, mix + width + 1],
        gate_shard,
        up_shard,
        down_shard,
    )


def solution(mesh):
    reps, group = mesh.shape["rep"], mesh.shape["fsdp"]
    both, one = P(AXES, None), P("fsdp")
    flat, deep = P("fsdp", None), P("fsdp", None, None)

    def whole(*args):
        return shards(reps, group, *args)

    return jax.shard_map(
        whole,
        mesh=mesh,
        in_specs=(both, both, both, both, P(AXES), one, flat, flat, flat, flat, one, deep, deep, deep),
        out_specs=(both, both, one, flat, flat, flat, flat, one, deep, deep, deep),
        check_vma=False,
    )
```

time: 1020 us -> 644 us (0.63)
  Pallas kernels: 348 us -> 594 us
  matrix products: 237 us -> 0 us
  waiting for transfers between devices: 190 us -> 8.1 us
  local copies, waits for them, and re-layouts: 130 us -> 12.8 us
  other arithmetic: 62.3 us -> 11.6 us
  starting transfers between devices: 33.5 us -> 7.63 us
    pallas_call x11 -> x7, Pallas kernels: 348 us -> 594 us  [the longest x1 222 us: forward(): pl.pallas_call(kernel, out_shape=[shape((width, 2 * half), BF), shape((pl...]
    dot_general x23 -> x0, matrix products: 226 us -> none  [the longest x6 73.9 us: dot_nt(): lax.dot_general(a, b, (((1,), (1,)), ((), ())), preferred_element_type=F32)]
    ppermute x45 -> x8, waiting for transfers between devices: 190 us -> 8.1 us  [pp(): return lax.ppermute(value, AXES, perm(to))]
    unnamed x191 -> x23, local copies, waits for them, and re-layouts: 39.8 us -> 4.17 us
    ppermute x45 -> x8, starting transfers between devices: 33.5 us -> 7.63 us  [pp(): return lax.ppermute(value, AXES, perm(to))]
    concatenate x2 -> x0, local copies, waits for them, and re-layouts: 20.5 us -> none  [the longest x1 19.6 us: shards(): jnp.concatenate([grad_mix_w.astype(BF), grad_out_w.astype(BF), grad_gain_...]
    slice x9 -> x0, local copies, waits for them, and re-layouts: 14.6 us -> none  [the longest x2 5.04 us: shards(): query_raw = mixed[:, :width].reshape(length, HEADS, HEAD)]
    convert_element_type x4 -> x0, other arithmetic: 14.4 us -> none  [the longest x1 6.64 us: shards(): logit_grad = (attn_probs * (grad_probs - inner_sum)).astype(BF)]
  transfers between devices with their start and end apart: 45 -> 8, of which waited for: 15 -> 3; matrix products, arithmetic and copies ran while one was open for 33% -> 2% of each run, Pallas kernels for 26% -> 36%
where the time goes in v3:
time: 644 us; the launch traced here: 636 us
  Pallas kernels  594 us (92%)
  local copies, waits for them, and re-layouts  12.8 us (2%)
  other arithmetic  11.6 us (2%)
  waiting for transfers between devices  8.1 us (1%)
  starting transfers between devices  7.63 us (1%)
    pallas_call x1, Pallas kernels, forward(): pl.pallas_call(kernel, out_shape=[shape((width, 2 * half), BF), shape((pl...  222 us
    pallas_call x2, Pallas kernels, expert(): pl.pallas_call(kernel, grid=(count // tile,), in_specs=[tiles, tiles, pl....  110 us
    pallas_call x1, Pallas kernels, backward(): pl.pallas_call(kernel, in_specs=[pl.BlockSpec(memory_space=pltpu.SMEM)] +...  103 us
    pallas_call x1, Pallas kernels, scatter_front(): pl.pallas_call(kernel, out_shape=[jax.ShapeDtypeStruct((ds, half), BF), j...  98.8 us
    pallas_call x1, Pallas kernels, scatter_plane(): pl.pallas_call(kernel, out_shape=[jax.ShapeDtypeStruct((length, width), F...  56.1 us
  transfers between devices with their start and end apart: 8, of which 3 were waited for; matrix products, arithmetic and copies ran while one was open for 2% of the time, Pallas kernels for 36%

profile of v3, /device:TPU:0, one launch (start us, length us, event | category | flops | bytes accessed | tf_op | source)
XLA Modules:
  0.0 635.6 jit_solution(12154728801852164756)
XLA Ops:
  0.7 0.8 select_reduce_fusion
  1.5 0.6 constant_dynamic-slice_fusion
  2.2 3.3 collective-permute-start.6
  5.5 0.6 collective-permute-start.5
  6.1 1.4 collective-permute-start.4
  7.5 0.3 collective-permute-start.3
  7.8 0.2 collective-permute-start
  8.7 0.7 convert_bitcast_fusion.1
  9.3 0.7 convert_bitcast_fusion
  10.0 0.1 copy.36
  10.1 0.1 copy.35
  10.2 0.9 convert_element_type.34
  11.2 0.9 convert_element_type.35
  12.1 1.1 convert_element_type.33
  13.2 1.1 convert_element_type.36
  14.3 0.3 concatenate.12
  14.6 0.8 constant_dynamic-slice_fusion.7.own_ref
  15.4 0.8 negate_select_fusion
  16.2 0.9 pad_maximum_fusion.tab_ref
  17.0 221.8 %shard_map.221 = (bf16[1536,4352]{1,0:T(8,128)(2,1)}, bf16[4,4,96,1536]{3,2,1,0:T(8,128)(2,1)}, bf16[4,4,96,1536]{3,2,1,0:T(8,128)(2,1)}, bf16[8,384,1536]{2,1,0...) custom-call(s32[1]{0:T(128)S(6)} %copy.47.starts_ref, ...), custom_call_target="tpu_custom_call" | custom-call | flops 149999992832 | bytes 20000000 | tf_op jit(solution)/shard_map/pallas_call | solution.py:466
  238.8 0.0 collective-permute-done
  238.8 0.4 collective-permute-start.1
  239.3 0.7 constant_dynamic-update-slice_fusion.6
  239.9 2.5 collective-permute-done.1
  242.5 3.0 collective-permute-done.2
  245.5 0.0 collective-permute-done.3
  245.5 0.7 constant_dynamic-update-slice_fusion.3
  246.2 0.7 constant_dynamic-update-slice_fusion.2
  246.9 0.0 collective-permute-done.5
  246.9 0.7 constant_dynamic-update-slice_fusion.1
  247.6 0.0 collective-permute-done.6
  247.6 0.7 constant_dynamic-update-slice_fusion
  248.3 1.7 copy.37.refs_2_
  250.0 1.7 copy.38.refs_2_
  251.6 54.1 %shard_map.222 = (bf16[3072,1536]{1,0:T(8,128)(2,1)}, bf16[3072,1536]{1,0:T(8,128)(2,1)}, bf16[1536,1536]{1,0:T(8,128)(2,1)}) custom-call(bf16[3072,1536]{1,0:T(8,128)(2,1)} %bitcast.18, bf16[3072,1536]{1,0:T(8,128)(2,1)} %bitcast.16, f32[3072,1]{1,0:T(8,128)} %copy.37.refs_2_, bf16[1536,1536]{1,0:T(8,128)(2,1)} %bitcast.23), custom_call_target="tpu_custom_call" | custom-call | flops 44000002048 | bytes 50000000 | tf_op jit(solution)/shard_map/pallas_call | solution.py:562
  305.7 56.2 %shard_map.223 = (bf16[3072,1536]{1,0:T(8,128)(2,1)}, bf16[3072,1536]{1,0:T(8,128)(2,1)}, bf16[1536,1536]{1,0:T(8,128)(2,1)}) custom-call(bf16[3072,1536]{1,0:T(8,128)(2,1)} %bitcast.19, bf16[3072,1536]{1,0:T(8,128)(2,1)} %bitcast.17, f32[3072,1]{1,0:T(8,128)} %copy.38.refs_2_, bf16[1536,1536]{1,0:T(8,128)(2,1)} %bitcast.22, ...), custom_call_target="tpu_custom_call" | custom-call | flops 44000002048 | bytes 50000000 | tf_op jit(solution)/shard_map/pallas_call | solution.py:562
  361.9 56.1 %shard_map.224 = (f32[384,1536]{1,0:T(8,128)}, bf16[384,1536]{1,0:T(8,128)(2,1)}) custom-call(bf16[8,384,1536]{2,1,0:T(8,128)(2,1)} %bitcast.21, bf16[4,384,1536]{2,1,0:T(8,128)(2,1)} %bitcast.26), custom_call_target="tpu_custom_call" | custom-call | flops 44999999488 | bytes 20000000 | tf_op jit(solution)/shard_map/pallas_call | solution.py:1059
  418.0 102.7 %shard_map.225 = (f32[384,1536]{1,0:T(8,128)}, f32[384,1536]{1,0:T(8,128)}, bf16[384,1536]{1,0:T(8,128)(2,1)}, bf16[1536,4352]{1,0:T(8,128)(2,1)}, bf16[8,96,1536]{2,1,0:T(8,128)(2,1)}) custom-call(s32[1]{0:T(128)S(6)} %copy.47.starts_ref, f32[384,1536]{1,0:T(8,128)} %get-tuple-element.50.d_ref, bf16[384,1536]{1,0:T(8,128)(2,1)} %cot_ref.3, ...), custom_call_target="tpu_custom_call" | custom-call | flops 80000000000 | bytes 50000000 | tf_op jit(solution)/shard_map/pallas_call | solution.py:964
  520.7 98.8 %shard_map.226 = (bf16[96,2176]{1,0:T(8,128)(2,1)}, bf16[8,96,1536]{2,1,0:T(8,128)(2,1)}) custom-call(bf16[1536,4352]{1,0:T(8,128)(2,1)} %get-tuple-element.63.g_ref, bf16[4,384,1536]{2,1,0:T(8,128)(2,1)} %bitcast.25, bf16[384,1536]{1,0:T(8,128)(2,1)} %get-tuple-element.64.before_ref), custom_call_target="tpu_custom_call" | custom-call | flops 49999998976 | bytes 20000000 | tf_op jit(solution)/shard_map/pallas_call | solution.py:1229
  619.6 1.4 collective-permute-start.7
  621.0 3.6 add.91
  624.6 4.1 shard_map.227
  628.7 2.5 collective-permute-done.7
  631.2 0.2 fusion
  631.4 0.7 slice_reduce_fusion
  632.1 0.8 fusion.9
  632.9 1.1 fusion.8
  634.0 1.4 copy.48
  (24 shorter events, 0.1 us)
Async XLA Ops:
  2.2 245.4 %collective-permute-start.6 = (f32[2,384]{1,0:T(2,128)}, f32[2,384]{1,0:T(2,128)}, u32[]{:S(2)}, u32[]{:S(2)}) collective-permute-start(f32[2,384]{1,0:T(2,128)} %get-tuple-element.79), channel_id=1, source_target_pairs={{0,19},{1,18},{2,17},{3,16},{4,23},{5,22},{6,21},{7,20},{8,27},{9,... | collective-permute-start | bytes 9224 | tf_op jit(solution)/shard_map/ppermute | solution.py:1349
  5.5 241.4 %collective-permute-start.5 = (f32[2,384]{1,0:T(2,128)}, f32[2,384]{1,0:T(2,128)}, u32[]{:S(2)}, u32[]{:S(2)}) collective-permute-start(f32[2,384]{1,0:T(2,128)} %get-tuple-element.80), channel_id=1, source_target_pairs={{0,18},{1,19},{2,16},{3,17},{4,22},{5,23},{6,20},{7,21},{8,26},{9,... | collective-permute-start | bytes 9224 | tf_op jit(solution)/shard_map/ppermute | solution.py:1349
  6.1 240.1 %collective-permute-start.4 = (f32[2,384]{1,0:T(2,128)}, f32[2,384]{1,0:T(2,128)}, u32[]{:S(2)}, u32[]{:S(2)}) collective-permute-start(f32[2,384]{1,0:T(2,128)} %get-tuple-element.81), channel_id=1, source_target_pairs={{0,17},{1,16},{2,19},{3,18},{4,21},{5,20},{6,23},{7,22},{8,25},{9,... | collective-permute-start | bytes 9224 | tf_op jit(solution)/shard_map/ppermute | solution.py:1349
  7.5 238.0 %collective-permute-start.3 = (f32[2,384]{1,0:T(2,128)}, f32[2,384]{1,0:T(2,128)}, u32[]{:S(2)}, u32[]{:S(2)}) collective-permute-start(f32[2,384]{1,0:T(2,128)} %get-tuple-element.82), channel_id=1, source_target_pairs={{0,16},{1,17},{2,18},{3,19},{4,20},{5,21},{6,22},{7,23},{8,24},{9,... | collective-permute-start | bytes 9224 | tf_op jit(solution)/shard_map/ppermute | solution.py:1349
  7.8 231.0 %collective-permute-start = (f32[2,384]{1,0:T(2,128)}, f32[2,384]{1,0:T(2,128)}, u32[]{:S(2)}, u32[]{:S(2)}) collective-permute-start(f32[2,384]{1,0:T(2,128)} %get-tuple-element.85), channel_id=1, source_target_pairs={{0,1},{1,0},{2,3},{3,2},{4,5},{5,4},{6,7},{7,6},{8,9},{9,8},{10,11... | collective-permute-start | bytes 9224 | tf_op jit(solution)/shard_map/ppermute | solution.py:1349
  17.0 221.8 %copy-start.7 = (f32[2,384]{1,0:T(2,128)S(1)}, f32[2,384]{1,0:T(2,128)}, u32[]{:S(2)}) copy-start(f32[2,384]{1,0:T(2,128)} %get-tuple-element.84) | copy-start | bytes 9220
  17.0 222.2 %copy-start.5 = (f32[2,3072]{1,0:T(2,128)S(1)}, f32[2,3072]{1,0:T(2,128)}, u32[]{:S(2)}) copy-start(f32[2,3072]{1,0:T(2,128)} %get-tuple-element.86) | copy-start | bytes 73732
  17.0 225.5 %copy-start.6 = (f32[2,384]{1,0:T(2,128)S(1)}, f32[2,384]{1,0:T(2,128)}, u32[]{:S(2)}) copy-start(f32[2,384]{1,0:T(2,128)} %get-tuple-element.83) | copy-start | bytes 9220
  238.8 3.7 collective-permute-start.1
  242.5 3.0 collective-permute-start.2
  520.7 100.2 %copy-start.2 = (f32[384,1536]{1,0:T(8,128)S(1)}, f32[384,1536]{1,0:T(8,128)}, u32[]{:S(2)}) copy-start(f32[384,1536]{1,0:T(8,128)} %get-tuple-element.41.res_hbm) | copy-start | bytes 7077892
  619.6 11.6 %collective-permute-start.7 = (bf16[96,2176]{1,0:T(8,128)(2,1)}, bf16[96,2176]{1,0:T(8,128)(2,1)S(1)}, u32[]{:S(2)}, u32[]{:S(2)}) collective-permute-start(bf16[96,2176]{1,0:T(8,128)(2,1)} %get-tuple-element.65), channel_id=1, source_target_pairs={{0,16},{1,17},{2,18},{3,19},{4,20},{5,21},{6,22},{7,23},{8,24},{9,... | collective-permute-start | bytes 1253384 | tf_op jit(solution)/shard_map/ppermute | solution.py:1349
  621.0 3.6 copy-start
  621.0 3.6 copy-start.1
  624.6 6.6 %copy-start.4 = (bf16[96,2176]{1,0:T(8,128)(2,1)S(1)}, bf16[96,2176]{1,0:T(8,128)(2,1)}, u32[]{:S(2)}) copy-start(bf16[96,2176]{1,0:T(8,128)(2,1)} %get-tuple-element.65) | copy-start | bytes 1253380
  628.7 5.3 copy-start.3

commit v4 on v3

--- a/solution.py
+++ b/solution.py
@@ -86,7 +86,7 @@
             )
         pl.semaphore_wait(semaphore, len(devices))
 
-    def send(self, src, dst, device):
+    def make(self, src, dst, device):
         n = len(self.copies)
         copy = pltpu.make_async_remote_copy(
             src_ref=src,
@@ -96,8 +96,12 @@
             device_id=device,
             device_id_type=pl.DeviceIdType.MESH,
         )
+        self.copies.append(copy)
+        return copy
+
+    def send(self, src, dst, device):
+        copy = self.make(src, dst, device)
         copy.start()
-        self.copies.append(copy)
         return copy
 
     def finish(self):
@@ -187,7 +191,6 @@
         wall_a,
         wall_b,
         grads_out,
-        rows_out,
         gain_ref,
         q_ref,
         kk_ref,
@@ -195,9 +198,9 @@
         att_ref,
         res_ref,
         n1_ref,
+        n2_ref,
         front,
         bias,
-        n2_ref,
         packed,
         raw_in,
         raw_down,
@@ -341,7 +344,6 @@
             spread(k)
             onward(k - 1)
         ring_first(0, first_exchange)
-        ring_first(1, second_exchange)
         onward(planes - 1)
         for k, span, copy in far:
             copy.wait_recv()
@@ -431,7 +433,7 @@
 
         attend((0, PAIRS // 2))
         gather_middle(*grads)
-        ring_next(1)
+        ring_next(0)
         attend((PAIRS // 2, PAIRS))
         for n in range(width // block):
             cols = slice(n * block, (n + 1) * block)
@@ -445,31 +447,23 @@
             n2_ref[chunk] = (r * inv * gain_ref[1:2, :]).astype(BF)
 
         row_loop(length, 64, norm_two)
-        rows = gather_start(n2_ref, rows_out)
-        rows_copy = pltpu.make_async_copy(n2_ref, rows_out.at[0], local_sems.at[5])
-        rows_copy.start()
         gather_last(*grads)
-        gather_middle(*rows)
-        ring_next(0)
-        gather_last(*rows)
-        for e in (1, 0):
-            while ring[e][0] < planes:
-                ring_next(e)
-        for copy in grads[1]["core"] + rows[1]["core"]:
+        while ring[0][0] < planes:
+            ring_next(0)
+        for copy in grads[1]["core"] + second_exchange:
             copy.wait_recv()
-        for copy in locals_ + [front_copy, cot_copy, rows_copy]:
+        for copy in locals_ + [front_copy, cot_copy]:
             copy.wait()
         at.finish()
 
     shape = jax.ShapeDtypeStruct
-    count = planes - 1 + planes * 11 + 2 * 3 + 2 * (4 + planes - 2) + 2 * 13
+    count = planes - 1 + planes * 11 + 2 * 3 + 4 + planes - 2 + 13
     return pl.pallas_call(
         kernel,
         out_shape=[
             shape((width, 2 * half), BF),
             shape((planes, 4, ds, wide), BF),
             shape((planes, 4, ds, wide), BF),
-            shape((PLANE, length, width), BF),
             shape((PLANE, length, width), BF),
             shape((8, width), F32),
             shape((length, width), BF),
@@ -478,22 +472,22 @@
             shape((length, width), BF),
             shape((length, width), F32),
             shape((length, width), BF),
+            shape((length, width), BF),
         ],
         in_specs=[pl.BlockSpec(memory_space=pltpu.SMEM)]
         + [whole_vmem()] * 3
         + [anywhere()] * 3
         + [whole_vmem()],
-        out_specs=[anywhere()] * 5 + [whole_vmem()] * 7,
+        out_specs=[anywhere()] * 4 + [whole_vmem()] * 8,
         scratch_shapes=[
             pltpu.VMEM((width, 2 * half), BF),
             pltpu.VMEM((length, length), F32),
-            pltpu.VMEM((length, width), BF),
             pltpu.VMEM((4, EPD, ds, wide), BF),
             pltpu.VMEM((2, 2, ds, hid), F32),
             pltpu.VMEM((2, hs, width), F32),
         ]
         + dma_pairs(count)
-        + [pltpu.SemaphoreType.DMA((6,)), pltpu.SemaphoreType.DMA((2, 3))],
+        + [pltpu.SemaphoreType.DMA((5,)), pltpu.SemaphoreType.DMA((2, 3))],
         compiler_params=comm_params(0),
         cost_estimate=pl.CostEstimate(
             flops=150_000_000_000, bytes_accessed=20_000_000, transcendentals=0
@@ -501,143 +495,79 @@
     )(starts, tokens, cotangent, own, w_gate, w_up, w_down, tables)
 
 
-def expert(rows, grads, share, pack, before, group):
-    count, width = rows.shape
-    hid = width // 3
-    tile = 512
-    ds, hs, blocks = width // group, hid // group, width // hid
-
-    def kernel(*refs):
-        x_ref, g_ref, s_ref, w_ref = refs[:4]
-        old = refs[4:6] if before else None
-        o_ref, dx_ref, dw_ref, down, in_sum, down_sum, pre, act = refs[6 if before else 4 :]
-        step = pl.program_id(0)
-
-        @pl.when(step == 0)
-        def _():
-            for s in range(group):
-                for b in range(blocks):
-                    down[s * hs : (s + 1) * hs, b * hid : (b + 1) * hid] = w_ref[
-                        s * ds + b * hs : s * ds + (b + 1) * hs, 2 * hid :
-                    ]
-            in_sum[...] = jnp.zeros_like(in_sum)
-            down_sum[...] = jnp.zeros_like(down_sum)
-
-        half = hid // 2
-        for n in range(2):
-            cols = slice(n * half, (n + 1) * half)
-            up_cols = slice(hid + n * half, hid + (n + 1) * half)
-            gate = dot(x_ref[...], w_ref[:, cols])
-            up = dot(x_ref[...], w_ref[:, up_cols])
-            inner = dot_nt(g_ref[...], down[cols, :]) * s_ref[...]
-            sig = jax.nn.sigmoid(gate)
-            swish = gate * sig
-            act[:, cols] = (s_ref[...] * (swish * up)).astype(BF)
-            pre[:, cols] = (inner * up * sig * (1.0 + gate * (1.0 - sig))).astype(BF)
-            pre[:, up_cols] = (inner * swish).astype(BF)
-        for n in range(width // hid):
-            cols = slice(n * hid, (n + 1) * hid)
-            out = dot(act[...], down[:, cols])
-            dx = dot_nt(pre[...], w_ref[cols, : 2 * hid])
-            if before:
-                out = out + old[0][:, cols].astype(F32)
-                dx = dx + old[1][:, cols].astype(F32)
-            o_ref[:, cols] = out.astype(BF)
-            dx_ref[:, cols] = dx.astype(BF)
-            in_sum[cols, :] += dot_tn(x_ref[:, cols], pre[...])
-            down_sum[:, cols] += dot_tn(act[...], g_ref[:, cols])
-
-        @pl.when(step == count // tile - 1)
-        def _():
-            dw_ref[:, : 2 * hid] = in_sum[...].astype(BF)
-            for s in range(group):
-                for b in range(blocks):
-                    dw_ref[s * ds + b * hs : s * ds + (b + 1) * hs, 2 * hid :] = down_sum[
-                        s * hs : (s + 1) * hs, b * hid : (b + 1) * hid
-                    ].astype(BF)
-
-    tiles = pl.BlockSpec((tile, width), lambda i: (i, 0))
-    whole = pl.BlockSpec((width, width), lambda i: (0, 0))
-    shape = jax.ShapeDtypeStruct
-    return pl.pallas_call(
-        kernel,
-        grid=(count // tile,),
-        in_specs=[tiles, tiles, pl.BlockSpec((tile, 1), lambda i: (i, 0)), whole]
-        + [tiles] * len(before),
-        out_specs=[tiles, tiles, whole],
-        out_shape=[shape((count, width), BF), shape((count, width), BF), shape((width, width), BF)],
-        scratch_shapes=[
-            pltpu.VMEM((hid, width), BF),
-            pltpu.VMEM((width, 2 * hid), F32),
-            pltpu.VMEM((hid, width), F32),
-            pltpu.VMEM((tile, 2 * hid), BF),
-            pltpu.VMEM((tile, hid), BF),
-        ],
-        compiler_params=pltpu.CompilerParams(vmem_limit_bytes=58 * 2**20),
-        cost_estimate=pl.CostEstimate(
-            flops=44_000_000_000, bytes_accessed=50_000_000, transcendentals=0
-        ),
-    )(rows, grads, share, pack, *before)
-
-
 class PlaneSum:
-    def __init__(self, at, odd, even, from_core, far, near):
+    def __init__(self, at, length, odd, even, from_core, far, near):
         self.at, self.odd, self.even, self.core = at, odd, even, from_core
         self.far, self.near = far, near
-        self.length = from_core.shape[1]
+        self.length = length
         self.half = self.length // 2
         self.low, self.high = pl.ds(0, self.half), pl.ds(self.half, self.half)
-
-    def start(self):
         self.arrive = {
-            j: self.at.send(self.odd(j), self.core.at[j], self.at.core) for j in (3, 2, 1, 0)
+            j: at.make(odd(j), self.part(j, pl.ds(0, length)), at.core) for j in (3, 2, 1, 0)
         }
+        low, high = self.low, self.high
+        self.far_y = at.make(self.part(3, low), far.at[0], at.y)
+        self.far_x = at.make(self.part(3, high), far.at[1], at.x)
+        self.x_high = at.make(self.part(2, high), near.at[0, high], at.x)
+        self.y_low = at.make(self.part(1, low), near.at[1, low], at.y)
+        self.x_low = at.make(self.part(2, low), near.at[0, low], at.x)
+        self.y_high = at.make(self.part(1, high), near.at[1, high], at.y)
+
+    def rows(self, j, chunk, base=0):
+        return pl.ds(pl.multiple_of(chunk.start + j * self.length + base, 16), chunk.size)
+
+    def part(self, j, rows):
+        return self.core.at[pl.ds(j * self.length + rows.start, rows.size)]
+
+    def start(self, j):
+        self.arrive[j].start()
 
     def add_core(self, j):
         self.arrive[j].wait_recv()
         core = self.core
 
         def store(chunk, total):
-            core[j, chunk] = total.astype(BF)
-
-        add_rows(store, [lambda q: self.even(j, q), lambda q: core[j, q]], self.length)
+            core[self.rows(j, chunk)] = total.astype(BF)
+
+        add_rows(store, [lambda q: self.even(j, q), lambda q: core[self.rows(j, q)]], self.length)
 
     def add_far(self, j, n, base):
         core, far = self.core, self.far
 
-        def moved(chunk):
-            return pl.ds(pl.multiple_of(chunk.start + base, 16), chunk.size)
-
         def store(chunk, total):
-            core[j, moved(chunk)] = total.astype(BF)
-
-        add_rows(store, [lambda q: core[j, moved(q)], lambda q: far[n, q]], self.half)
-
-    def neighbours(self):
-        at, core, far, near, low, high = self.at, self.core, self.far, self.near, self.low, self.high
+            core[self.rows(j, chunk, base)] = total.astype(BF)
+
+        add_rows(store, [lambda q: core[self.rows(j, q, base)], lambda q: far[n, q]], self.half)
+
+    def send_far(self):
         self.add_core(3)
-        self.far_y = at.send(core.at[3, low], far.at[0], at.y)
-        self.far_x = at.send(core.at[3, high], far.at[1], at.x)
+        self.far_y.start()
+        self.far_x.start()
+
+    def send_x(self):
         self.add_core(2)
-        self.last = [at.send(core.at[2, high], near.at[0, high], at.x)]
+        self.x_high.start()
+
+    def send_y(self):
         self.add_core(1)
-        self.last.append(at.send(core.at[1, low], near.at[1, low], at.y))
-
-    def onward(self):
-        at, core, near, low, high = self.at, self.core, self.near, self.low, self.high
+        self.y_low.start()
+
+    def onward_x(self):
         self.far_y.wait_recv()
         self.add_far(2, 0, 0)
-        self.last.append(at.send(core.at[2, low], near.at[0, low], at.x))
+        self.x_low.start()
+
+    def onward_y(self):
         self.far_x.wait_recv()
         self.add_far(1, 1, self.half)
-        self.last.append(at.send(core.at[1, high], near.at[1, high], at.y))
+        self.y_high.start()
 
     def end(self, store):
         self.arrive[0].wait_recv()
-        for copy in self.last:
+        for copy in (self.x_high, self.y_low, self.x_low, self.y_high):
             copy.wait_recv()
         core, near = self.core, self.near
-        terms = [lambda q: self.even(0, q), lambda q: core[0, q]]
+        terms = [lambda q: self.even(0, q), lambda q: core[q]]
         terms += [lambda q: near[0, q], lambda q: near[1, q]]
         add_rows(store, terms, self.length)
 
@@ -647,9 +577,10 @@
 class RingSum:
     def __init__(self, at, pack, own, own_sem):
         self.at, self.pack, self.own, self.own_sem = at, pack, own, own_sem
+        self.index = [(at.z + at.planes - k) % at.planes for k in range(at.planes)]
 
     def block(self, k):
-        return self.pack.at[(self.at.z + self.at.planes - k) % self.at.planes]
+        return self.pack.at[self.index[k]]
 
     def fetch(self, k):
         self.fetched = pltpu.make_async_copy(self.block(k), self.own, self.own_sem)
@@ -665,23 +596,35 @@
 
     def first(self, slots):
         self.slots, self.step = slots, 1
-        self.copy = self.at.send(self.block(1), slots[0], self.at.along[1])
-        self.fetch(2)
+        sources = [self.block(1)] + slots[:-1]
+        self.sent = [
+            self.at.make(src, dst, self.at.along[1]) for src, dst in zip(sources, slots)
+        ]
+        self.fetches = {
+            k: pltpu.make_async_copy(self.block(k), self.own, self.own_sem)
+            for k in range(2, len(slots) + 1)
+        }
+        self.sent[0].start()
+        self.begin_fetch(2)
+
+    def begin_fetch(self, k):
+        if k in self.fetches:
+            self.fetched = self.fetches[k]
+            self.fetched.start()
 
     def next(self):
         if self.step < len(self.slots):
             here = self.slots[self.step - 1]
-            self.copy.wait_recv()
+            self.sent[self.step - 1].wait_recv()
             self.add(here, here)
-            self.copy = self.at.send(here, self.slots[self.step], self.at.along[1])
+            self.sent[self.step].start()
             self.step += 1
-            if self.step < len(self.slots):
-                self.fetch(self.step + 1)
+            self.begin_fetch(self.step + 1)
 
     def rest(self):
         while self.step < len(self.slots):
             self.next()
-        self.copy.wait_recv()
+        self.sent[-1].wait_recv()
 
     def last(self, before, sent, landing):
         self.add(before, sent)
@@ -693,6 +636,323 @@
         self.copy.wait_recv()
         self.add(self.landing, self.landing)
         return self.landing
+
+
+def run_experts(tokens, grads, shares, wall_a, wall_b, planes, group):
+    pairs, count, width = grads.shape
+    length = count // 2
+    piece, wide = wall_a.shape[1:]
+    hid = wide // 3
+    ds, hs, blocks = width // group, hid // group, width // hid
+    half = length // 2
+    low, high, full = pl.ds(0, half), pl.ds(half, half), pl.ds(0, length)
+
+    def kernel(
+        n2_hbm,
+        g_hbm,
+        share_ref,
+        wall_a_ref,
+        wall_b_ref,
+        out_hbm,
+        pack_a,
+        pack_b,
+        sum_ref,
+        passed,
+        xs,
+        dxs,
+        w_a,
+        w_b,
+        down_a,
+        down_b,
+        in_sum,
+        down_sum,
+        g_tile,
+        o_tile,
+        pre,
+        act,
+        far,
+        near,
+        ring_slots,
+        own,
+        free,
+        send_sems,
+        recv_sems,
+        local_sems,
+    ):
+        at = Links(planes, group, send_sems, recv_sems)
+        at.barrier([at.x, at.y, at.core] + at.along[1:])
+        index = [(at.z + planes - k) % planes for k in range(planes)]
+
+        def local(src, dst, n):
+            copy = pltpu.make_async_copy(src, dst, local_sems.at[n])
+            copy.start()
+            return copy
+
+        def slot(j, rows=full):
+            return xs.at[j // 2, pl.ds(j % 2 * length + rows.start, rows.size)]
+
+        pieces = [
+            w_b.at[pl.ds(pl.multiple_of(index[k] * piece, 16), piece)] for k in range(planes)
+        ]
+
+        local(n2_hbm, slot(0), 0).wait()
+        x_low = at.send(slot(0, low), slot(4, low), at.x)
+        y_high = at.send(slot(0, high), slot(2, high), at.y)
+        x_high = at.send(slot(0, high), slot(4, high), at.x)
+        y_low = at.send(slot(0, low), slot(2, low), at.y)
+        near_core = at.send(slot(0), slot(1), at.core)
+        ring = [at.make(wall_b_ref.at[at.z], pieces[0], at.along[1])]
+        ring += [at.make(piece_ref, piece_ref, at.along[1]) for piece_ref in pieces[1:-1]]
+        ring[0].start()
+        load_b = local(wall_b_ref.at[at.z], pieces[0], 1)
+        loads = [
+            local(wall_a_ref.at[n], w_a.at[pl.ds(n * piece, piece)], 2 + n) for n in range(planes)
+        ]
+        state = {"ring": 0}
+        far_low = at.make(slot(4, low), slot(6, low), at.y)
+        far_high = at.make(slot(2, high), slot(6, high), at.x)
+        passed_on = {
+            (j, rows.start): at.make(slot(j, rows), slot(j + 1, rows), at.core)
+            for j in (4, 2, 6)
+            for rows in (low, high)
+        }
+
+        def ring_next():
+            ring[state["ring"]].wait_recv()
+            state["ring"] += 1
+            if state["ring"] < planes - 1:
+                ring[state["ring"]].start()
+
+        def core_arrival(j):
+            passed_on[j, low.start].wait_recv()
+            passed_on[j, high.start].wait_recv()
+
+        def spread():
+            x_low.wait_recv()
+            far_low.start()
+            passed_on[4, low.start].start()
+            y_high.wait_recv()
+            far_high.start()
+            passed_on[2, high.start].start()
+            x_high.wait_recv()
+            passed_on[4, high.start].start()
+            y_low.wait_recv()
+            passed_on[2, low.start].start()
+            core_arrival(4)
+
+        def spread_far():
+            far_low.wait_recv()
+            passed_on[6, low.start].start()
+            far_high.wait_recv()
+            passed_on[6, high.start].start()
+            core_arrival(6)
+
+        def unpack_down(w, down):
+            for s in range(group):
+                for b in range(blocks):
+                    down[s * hs : (s + 1) * hs, b * hid : (b + 1) * hid] = w[
+                        s * ds + b * hs : s * ds + (b + 1) * hs, 2 * hid :
+                    ]
+
+        def clear():
+            def body(chunk):
+                in_sum[chunk] = jnp.zeros((chunk.size, 2 * hid), F32)
+
+            row_loop(width, 64, body)
+
+            def body_down(chunk):
+                down_sum[chunk] = jnp.zeros((chunk.size, width), F32)
+
+            row_loop(hid, 64, body_down)
+
+        def out_copy(pair):
+            return pltpu.make_async_copy(o_tile, out_hbm.at[pair], local_sems.at[0])
+
+        def tile(e, step, pair, w, down, middle):
+            g_load = pltpu.make_async_copy(g_hbm.at[pair], g_tile, local_sems.at[1])
+            g_load.start()
+            x = xs.at[pair]
+            share = share_ref[pair].T[:, e : e + 1]
+            part = hid // 2
+            for n in range(2):
+                cols = slice(n * part, (n + 1) * part)
+                up_cols = slice(hid + n * part, hid + (n + 1) * part)
+                gate = dot(x[...], w[:, cols])
+                up = dot(x[...], w[:, up_cols])
+                if n == 0:
+                    g_load.wait()
+                inner = dot_nt(g_tile[...], down[cols, :]) * share
+                sig = jax.nn.sigmoid(gate)
+                swish = gate * sig
+                act[:, cols] = (share * (swish * up)).astype(BF)
+                pre[:, cols] = (inner * up * sig * (1.0 + gate * (1.0 - sig))).astype(BF)
+                pre[:, up_cols] = (inner * swish).astype(BF)
+            middle()
+
+            @pl.when(step > 0)
+            def _():
+                out_copy(pair).wait()
+
+            if e > 0:
+                before = pltpu.make_async_copy(out_hbm.at[pair], o_tile, local_sems.at[2])
+                before.start()
+                before.wait()
+            for n in range(width // hid):
+                cols = slice(n * hid, (n + 1) * hid)
+                out = dot(act[...], down[:, cols])
+                dx = dot_nt(pre[...], w[cols, : 2 * hid])
+                if e > 0:
+                    out = out + o_tile[:, cols].astype(F32)
+                    dx = dx + dxs[pair, :, cols].astype(F32)
+                o_tile[:, cols] = out.astype(BF)
+                dxs[pair, :, cols] = dx.astype(BF)
+                in_sum[cols, :] += dot_tn(x[:, cols], pre[...])
+                down_sum[:, cols] += dot_tn(act[...], g_tile[:, cols])
+            out_copy(pair).start()
+
+        def pack(target):
+            out_copy(0).wait()
+            copies = [None, None]
+            for n in range(planes):
+                base = n % 2 * piece
+                if copies[n % 2] is not None:
+                    copies[n % 2].wait()
+
+                def body(chunk, n=n, base=base):
+                    rows = pl.ds(pl.multiple_of(chunk.start + base, 16), chunk.size)
+                    source = pl.ds(pl.multiple_of(chunk.start + n * piece, 16), chunk.size)
+                    o_tile[rows, : 2 * hid] = in_sum[source].astype(BF)
+
+                row_loop(piece, 32, body)
+                for s in range(4):
+                    for b in range(blocks):
+                        row = base + s * ds + b * hs
+                        o_tile[row : row + hs, 2 * hid :] = down_sum[
+                            (n * 4 + s) * hs : (n * 4 + s + 1) * hs, b * hid : (b + 1) * hid
+                        ].astype(BF)
+                copies[n % 2] = local(o_tile.at[pl.ds(base, piece)], target.at[n], 3 + n % 2)
+            for copy in copies:
+                copy.wait()
+
+        clear()
+        for copy in loads:
+            copy.wait()
+        load_b.wait()
+        unpack_down(w_a, down_a)
+        near_core.wait_recv()
+
+        @pl.loop(0, pairs)
+        def _(step):
+            @pl.when(step == 1)
+            def _():
+                spread()
+                ring_next()
+
+            @pl.when(step == 2)
+            def _():
+                core_arrival(2)
+
+            @pl.when(step == 3)
+            def _():
+                spread_far()
+                ring_next()
+
+            tile(0, step, 2 * step % 3 + step // 3 * 3, w_a, down_a, lambda: None)
+
+        pl.semaphore_signal(free, inc=1, device_id=at.core, device_id_type=pl.DeviceIdType.MESH)
+        pack(pack_a)
+        sums = RingSum(at, pack_a, own, local_sems.at[5])
+        sums.first([ring_slots.at[n] for n in range(planes - 3)] + [passed])
+        clear()
+        while state["ring"] < planes - 1:
+            ring_next()
+        unpack_down(w_b, down_b)
+        pl.semaphore_wait(free, 1)
+        plane = PlaneSum(
+            at,
+            length,
+            lambda j: dxs.at[j, pl.ds(length, length)],
+            lambda j, q: dxs[j, q],
+            w_a,
+            far,
+            near,
+        )
+
+        @pl.loop(0, pairs)
+        def _(step):
+            def middle():
+                @pl.when(step == 1)
+                def _():
+                    plane.send_far()
+
+                @pl.when(step == 2)
+                def _():
+                    plane.send_x()
+                    sums.next()
+
+                @pl.when(step == 3)
+                def _():
+                    plane.send_y()
+                    plane.onward_y()
+
+            tile(1, step, pairs - 1 - step, w_b, down_b, middle)
+            for n in range(pairs):
+
+                @pl.when(step == n)
+                def _(n=n):
+                    plane.start(pairs - 1 - n)
+                    if n == 2:
+                        plane.onward_x()
+
+        pack(pack_b)
+
+        def store(chunk, total):
+            sum_ref[chunk] = total
+
+        plane.end(store)
+        sums.rest()
+        at.finish()
+
+    shape = jax.ShapeDtypeStruct
+    return pl.pallas_call(
+        kernel,
+        in_specs=[anywhere()] * 2 + [whole_vmem()] + [anywhere()] * 2,
+        out_specs=[anywhere()] * 3 + [whole_vmem()] * 2,
+        out_shape=[
+            shape((pairs, count, width), BF),
+            shape((planes, piece, wide), BF),
+            shape((planes, piece, wide), BF),
+            shape((length, width), F32),
+            shape((piece, wide), BF),
+        ],
+        scratch_shapes=[
+            pltpu.VMEM((pairs, count, width), BF),
+            pltpu.VMEM((pairs, count, width), BF),
+            pltpu.VMEM((width, wide), BF),
+            pltpu.VMEM((width, wide), BF),
+            pltpu.VMEM((hid, width), BF),
+            pltpu.VMEM((hid, width), BF),
+            pltpu.VMEM((width, 2 * hid), F32),
+            pltpu.VMEM((hid, width), F32),
+            pltpu.VMEM((count, width), BF),
+            pltpu.VMEM((count, width), BF),
+            pltpu.VMEM((count, 2 * hid), BF),
+            pltpu.VMEM((count, hid), BF),
+            pltpu.VMEM((2, half, width), BF),
+            pltpu.VMEM((2, length, width), BF),
+            pltpu.VMEM((planes - 3, piece, wide), BF),
+            pltpu.VMEM((piece, wide), BF),
+            pltpu.SemaphoreType.REGULAR,
+        ]
+        + dma_pairs(13 + planes - 1 + PlaneSum.copies + planes - 2)
+        + [pltpu.SemaphoreType.DMA((2 + planes,))],
+        compiler_params=pltpu.CompilerParams(
+            collective_id=2, has_side_effects=True, vmem_limit_bytes=63 * 2**20
+        ),
+        cost_estimate=pl.CostEstimate(
+            flops=100_000_000_000, bytes_accessed=50_000_000, transcendentals=0
+        ),
+    )(tokens, grads, shares, wall_a, wall_b)
 
 
 class Exchange:
@@ -823,9 +1083,16 @@
             w_hbm.at[:, pl.ds(mix, width)], w_ref.at[:, pl.ds(0, width)], 1
         )
         plane = PlaneSum(
-            at, lambda j: outs_ref.at[2 * j + 1], lambda j, q: even[j, q], from_core, far, near
+            at,
+            length,
+            lambda j: outs_ref.at[2 * j + 1],
+            lambda j, q: even[j, q],
+            from_core,
+            far,
+            near,
         )
-        plane.start()
+        for j in (3, 2, 1, 0):
+            plane.start(j)
         ring_a = RingSum(at, pack_a_ref, own_a, local_sems.at[6])
         ring_b = RingSum(at, pack_b_ref, own_b, local_sems.at[7])
         ring_a.fetch(planes - 1)
@@ -875,7 +1142,9 @@
         load_n1 = local(n1_hbm, mixed, 0)
         for copy in loads:
             copy.wait()
-        plane.neighbours()
+        plane.send_far()
+        plane.send_x()
+        plane.send_y()
         key_sum[...] = jnp.zeros_like(key_sum)
         value_sum[...] = jnp.zeros_like(value_sum)
 
@@ -901,7 +1170,8 @@
                     grad_mix[rows, cols] = back.astype(BF)
 
         attend(0, PAIRS // 3)
-        plane.onward()
+        plane.onward_x()
+        plane.onward_y()
         exchange = Exchange(at, ring_a.total(), shards_ref, ds)
         exchange.start(local_sems.at[10])
         attend(PAIRS // 3, 2 * PAIRS // 3)
@@ -985,7 +1255,7 @@
             pltpu.VMEM((width, mix), BF),
             pltpu.VMEM((2, width, block), BF),
             pltpu.VMEM((4, length, width), BF),
-            pltpu.VMEM((4, length, width), BF),
+            pltpu.VMEM((4 * length, width), BF),
             pltpu.VMEM((2, length // 2, width), BF),
             pltpu.VMEM((2, length, width), BF),
             pltpu.VMEM((piece, wide), BF),
@@ -1023,64 +1293,6 @@
     )
 
 
-def scatter_plane(partial, pack, planes, group):
-    slots, length, width = partial.shape
-    half = length // 2
-    block, wide = pack.shape[1:]
-
-    def kernel(
-        p_ref, pack_ref, out_ref, passed, even, from_core, far, near, ring_slots, own, send_sems, recv_sems, local_sems
-    ):
-        at = Links(planes, group, send_sems, recv_sems)
-        at.barrier([at.x, at.y, at.core] + at.along[1:])
-        ring = RingSum(at, pack_ref, own, local_sems.at[4])
-        loads = []
-        for j in range(4):
-            loads.append(pltpu.make_async_copy(p_ref.at[2 * j], even.at[j], local_sems.at[j]))
-            loads[-1].start()
-        plane = PlaneSum(
-            at, lambda j: p_ref.at[2 * j + 1], lambda j, q: even[j, q], from_core, far, near
-        )
-        plane.start()
-        ring.first([ring_slots.at[n] for n in range(planes - 3)] + [passed])
-        for copy in loads:
-            copy.wait()
-        plane.neighbours()
-        plane.onward()
-        ring.next()
-
-        def store(chunk, total):
-            out_ref[chunk] = total
-
-        plane.end(store)
-        ring.rest()
-        at.finish()
-
-    return pl.pallas_call(
-        kernel,
-        out_shape=[
-            jax.ShapeDtypeStruct((length, width), F32),
-            jax.ShapeDtypeStruct((block, wide), BF),
-        ],
-        in_specs=[anywhere(), anywhere()],
-        out_specs=[whole_vmem(), whole_vmem()],
-        scratch_shapes=[
-            pltpu.VMEM((4, length, width), BF),
-            pltpu.VMEM((4, length, width), BF),
-            pltpu.VMEM((2, half, width), BF),
-            pltpu.VMEM((2, length, width), BF),
-            pltpu.VMEM((planes - 3, block, wide), BF),
-            pltpu.VMEM((block, wide), BF),
-        ]
-        + dma_pairs(PlaneSum.copies + planes - 2)
-        + [pltpu.SemaphoreType.DMA((5,))],
-        compiler_params=comm_params(2),
-        cost_estimate=pl.CostEstimate(
-            flops=45_000_000_000, bytes_accessed=20_000_000, transcendentals=0
-        ),
-    )(partial, pack)
-
-
 def scatter_front(grad, pack, before, planes, group):
     rows, columns = grad.shape
     ds, half = rows // (4 * planes), columns // 2
@@ -1389,9 +1601,11 @@
     for j in range(PLANE):
         block = lax.dynamic_slice(share, ((mine ^ j) * EPD, 0), (EPD, length))
         shares.append(block if j == 0 else go(block, j // 4, (j // 2) % 2, j % 2))
-    shares = jnp.concatenate(shares, axis=1)
-
-    front, wall_a, wall_b, grads_all, rows_all, gains_all, q, kk, vv, att, residual, n1 = forward(
+    pairs = PLANE // 2
+    shares = jnp.concatenate(shares, axis=1).reshape(EPD, pairs, 2 * length).transpose(1, 0, 2)
+    shares = jnp.pad(shares, ((0, 0), (0, 8 - EPD), (0, 0)))
+
+    front, wall_a, wall_b, grads_all, gains_all, q, kk, vv, att, residual, n1, n2 = forward(
         starts,
         tokens,
         cotangent,
@@ -1402,18 +1616,14 @@
         planes,
         group,
     )
-    grads_all = grads_all.reshape(PLANE * length, width)
-    rows_all = rows_all.reshape(PLANE * length, width)
-    before, pack_grads = (), []
-    for e, wall in enumerate((wall_a, wall_b)):
-        *before, pack_grad = expert(
-            rows_all, grads_all, shares[e][:, None], wall.reshape(width, 3 * hid), before, group
-        )
-        pack_grads.append(pack_grad)
-    out_sum, row_sum = before
-    pack_a, pack_b = [grad.reshape(planes, 4 * ds, 3 * hid) for grad in pack_grads]
-    grad_normed_two, before_a = scatter_plane(
-        row_sum.reshape(PLANE, length, width), pack_a, planes, group
+    out_sum, pack_a, pack_b, grad_normed_two, before_a = run_experts(
+        n2,
+        grads_all.reshape(pairs, 2 * length, width),
+        shares,
+        wall_a.reshape(planes, 4 * ds, 3 * hid),
+        wall_b.reshape(planes, 4 * ds, 3 * hid),
+        planes,
+        group,
     )
     input_grad, out_term, before_b, front_grad, shards_a = backward(
         starts,

time: 644 us -> 567 us (0.88)
  Pallas kernels: 594 us -> 519 us
    pallas_call x1, Pallas kernels: 222 us -> 149 us  [forward(): pl.pallas_call(kernel, out_shape=[shape((width, 2 * half), BF), shape((pl...]
    pallas_call x3 -> x1, Pallas kernels: 166 us -> 166 us  [run_experts(): pl.pallas_call(kernel, in_specs=[anywhere()] * 2 + [whole_vmem()] + [anyw...]
  transfers between devices with their start and end apart: 8 -> 8, of which waited for: 3 -> 3; matrix products, arithmetic and copies ran while one was open for 2% -> 3% of each run, Pallas kernels for 36% -> 27%
where the time goes in v4:
time: 567 us; the launch traced here: 559 us
  Pallas kernels  519 us (92%)
  other arithmetic  11.6 us (2%)
  local copies, waits for them, and re-layouts  10.1 us (2%)
  starting transfers between devices  8.52 us (2%)
  waiting for transfers between devices  7.5 us (1%)
    pallas_call x1, Pallas kernels, run_experts(): pl.pallas_call(kernel, in_specs=[anywhere()] * 2 + [whole_vmem()] + [anyw...  166 us
    pallas_call x1, Pallas kernels, forward(): pl.pallas_call(kernel, out_shape=[shape((width, 2 * half), BF), shape((pl...  149 us
    pallas_call x1, Pallas kernels, backward(): pl.pallas_call(kernel, in_specs=[pl.BlockSpec(memory_space=pltpu.SMEM)] +...  102 us
    pallas_call x1, Pallas kernels, scatter_front(): pl.pallas_call(kernel, out_shape=[jax.ShapeDtypeStruct((ds, half), BF), j...  98.3 us
  transfers between devices with their start and end apart: 8, of which 3 were waited for; matrix products, arithmetic and copies ran while one was open for 3% of the time, Pallas kernels for 27%

profile of v4, /device:TPU:0, one launch (start us, length us, event | category | flops | bytes accessed | tf_op | source)
XLA Modules:
  0.0 558.9 jit_solution(3027962738075780426)
XLA Ops:
  0.7 0.8 select_reduce_fusion
  1.5 0.6 constant_dynamic-slice_fusion
  2.2 3.3 collective-permute-start.6
  5.5 0.6 collective-permute-start.5
  6.1 1.4 collective-permute-start.4
  7.5 0.3 collective-permute-start.3
  7.8 0.2 collective-permute-start
  8.7 0.7 convert_bitcast_fusion.1
  9.3 0.7 convert_bitcast_fusion
  10.0 0.1 copy.34
  10.1 0.1 copy.33
  10.2 0.9 convert_element_type.36
  11.2 0.9 convert_element_type.37
  12.1 1.1 convert_element_type.35
  13.2 1.1 convert_element_type.38
  14.3 0.3 concatenate.12
  14.6 0.8 constant_dynamic-slice_fusion.7.own_ref
  15.4 0.8 negate_select_fusion
  16.2 0.9 pad_maximum_fusion.tab_ref
  17.0 148.8 %shard_map.221 = (bf16[1536,4352]{1,0:T(8,128)(2,1)}, bf16[4,4,96,1536]{3,2,1,0:T(8,128)(2,1)}, bf16[4,4,96,1536]{3,2,1,0:T(8,128)(2,1)}, bf16[8,384,1536]{2,1,0...) custom-call(s32[1]{0:T(128)S(6)} %copy.43.starts_ref, ...), custom_call_target="tpu_custom_call" | custom-call | flops 149999992832 | bytes 20000000 | tf_op jit(solution)/shard_map/pallas_call | solution.py:461
  165.9 0.0 collective-permute-done
  165.9 0.0 copy-done.7
  165.9 1.6 collective-permute-start.1
  167.5 0.7 constant_dynamic-update-slice_fusion.6
  168.2 1.4 collective-permute-done.1
  169.6 0.0 collective-permute-start.2
  169.6 3.0 collective-permute-done.2
  172.6 0.0 collective-permute-done.3
  172.6 0.7 constant_dynamic-update-slice_fusion.3
  173.3 0.0 collective-permute-done.4
  173.3 0.7 constant_dynamic-update-slice_fusion.2
  174.0 0.0 collective-permute-done.5
  174.0 0.7 constant_dynamic-update-slice_fusion.1
  174.7 0.0 collective-permute-done.6
  174.7 0.7 constant_dynamic-update-slice_fusion
  175.4 0.6 pad.4.share_ref
  176.0 166.1 %shard_map.222 = (bf16[4,768,1536]{2,1,0:T(8,128)(2,1)}, bf16[4,384,1536]{2,1,0:T(8,128)(2,1)}, bf16[4,384,1536]{2,1,0:T(8,128)(2,1)}, f32[384,1536]{1,0:T(8,128)}, bf16[384,1536]{1,0:T(8,128)(2,1)}) custom-call(bf16[384,1536]{1,0:T(8,128)(2,1)} %get-tuple-element.39.n2_hbm, bf16[4,768,1536]{2,1,0:T(8,128)(2,1)} %bitcast.12, f32[4,8,768]{2,1,0:T(8,128)} %pad.4.share_ref, ...), custom_call_target="tpu_custom_call" | custom-call | flops 99999997952 | bytes 50000000 | tf_op jit(solution)/shard_map/pallas_call | solution.py:917
  342.1 101.9 %shard_map.223 = (f32[384,1536]{1,0:T(8,128)}, f32[384,1536]{1,0:T(8,128)}, bf16[384,1536]{1,0:T(8,128)(2,1)}, bf16[1536,4352]{1,0:T(8,128)(2,1)}, bf16[8,96,1536]{2,1,0:T(8,128)(2,1)}) custom-call(s32[1]{0:T(128)S(6)} %copy.43.starts_ref, f32[384,1536]{1,0:T(8,128)} %get-tuple-element.43.d_ref, bf16[384,1536]{1,0:T(8,128)(2,1)} %cot_ref.3, ...), custom_call_target="tpu_custom_call" | custom-call | flops 80000000000 | bytes 50000000 | tf_op jit(solution)/shard_map/pallas_call | solution.py:1234
  444.0 98.3 %shard_map.224 = (bf16[96,2176]{1,0:T(8,128)(2,1)}, bf16[8,96,1536]{2,1,0:T(8,128)(2,1)}) custom-call(bf16[1536,4352]{1,0:T(8,128)(2,1)} %get-tuple-element.57.g_ref, bf16[4,384,1536]{2,1,0:T(8,128)(2,1)} %get-tuple-element.54.pack_b_ref.pack_ref, bf16[384,1536]{1,0:T(8,128)(2,1)} %get-tuple-element.58.before_ref), custom_call_target="tpu_custom_call" | custom-call | flops 49999998976 | bytes 20000000 | tf_op jit(solution)/shard_map/pallas_call | solution.py:1441
  542.3 1.1 collective-permute-start.7
  543.4 3.6 add.93
  547.0 4.1 shard_map.225
  551.2 3.1 collective-permute-done.7
  554.2 0.2 fusion
  554.4 0.7 slice_reduce_fusion
  555.1 0.8 fusion.9
  555.9 1.1 fusion.8
  557.0 1.4 copy.44
  (20 shorter events, 0.1 us)
Async XLA Ops:
  2.2 172.5 %collective-permute-start.6 = (f32[2,384]{1,0:T(2,128)}, f32[2,384]{1,0:T(2,128)}, u32[]{:S(2)}, u32[]{:S(2)}) collective-permute-start(f32[2,384]{1,0:T(2,128)} %get-tuple-element.71), channel_id=1, source_target_pairs={{0,19},{1,18},{2,17},{3,16},{4,23},{5,22},{6,21},{7,20},{8,27},{9,... | collective-permute-start | bytes 9224 | tf_op jit(solution)/shard_map/ppermute | solution.py:1561
  5.5 168.5 %collective-permute-start.5 = (f32[2,384]{1,0:T(2,128)}, f32[2,384]{1,0:T(2,128)}, u32[]{:S(2)}, u32[]{:S(2)}) collective-permute-start(f32[2,384]{1,0:T(2,128)} %get-tuple-element.72), channel_id=1, source_target_pairs={{0,18},{1,19},{2,16},{3,17},{4,22},{5,23},{6,20},{7,21},{8,26},{9,... | collective-permute-start | bytes 9224 | tf_op jit(solution)/shard_map/ppermute | solution.py:1561
  6.1 167.2 %collective-permute-start.4 = (f32[2,384]{1,0:T(2,128)}, f32[2,384]{1,0:T(2,128)}, u32[]{:S(2)}, u32[]{:S(2)}) collective-permute-start(f32[2,384]{1,0:T(2,128)} %get-tuple-element.73), channel_id=1, source_target_pairs={{0,17},{1,16},{2,19},{3,18},{4,21},{5,20},{6,23},{7,22},{8,25},{9,... | collective-permute-start | bytes 9224 | tf_op jit(solution)/shard_map/ppermute | solution.py:1561
  7.5 165.1 %collective-permute-start.3 = (f32[2,384]{1,0:T(2,128)}, f32[2,384]{1,0:T(2,128)}, u32[]{:S(2)}, u32[]{:S(2)}) collective-permute-start(f32[2,384]{1,0:T(2,128)} %get-tuple-element.74), channel_id=1, source_target_pairs={{0,16},{1,17},{2,18},{3,19},{4,20},{5,21},{6,22},{7,23},{8,24},{9,... | collective-permute-start | bytes 9224 | tf_op jit(solution)/shard_map/ppermute | solution.py:1561
  7.8 158.1 %collective-permute-start = (f32[2,384]{1,0:T(2,128)}, f32[2,384]{1,0:T(2,128)}, u32[]{:S(2)}, u32[]{:S(2)}) collective-permute-start(f32[2,384]{1,0:T(2,128)} %get-tuple-element.77), channel_id=1, source_target_pairs={{0,1},{1,0},{2,3},{3,2},{4,5},{5,4},{6,7},{7,6},{8,9},{9,8},{10,11... | collective-permute-start | bytes 9224 | tf_op jit(solution)/shard_map/ppermute | solution.py:1561
  17.0 148.9 %copy-start.7 = (f32[2,384]{1,0:T(2,128)S(1)}, f32[2,384]{1,0:T(2,128)}, u32[]{:S(2)}) copy-start(f32[2,384]{1,0:T(2,128)} %get-tuple-element.76) | copy-start | bytes 9220
  17.0 150.5 %copy-start.5 = (f32[2,3072]{1,0:T(2,128)S(1)}, f32[2,3072]{1,0:T(2,128)}, u32[]{:S(2)}) copy-start(f32[2,3072]{1,0:T(2,128)} %get-tuple-element.78) | copy-start | bytes 73732
  17.0 152.5 %copy-start.6 = (f32[2,384]{1,0:T(2,128)S(1)}, f32[2,384]{1,0:T(2,128)}, u32[]{:S(2)}) copy-start(f32[2,384]{1,0:T(2,128)} %get-tuple-element.75) | copy-start | bytes 9220
  165.9 3.7 collective-permute-start.1
  169.6 3.0 collective-permute-start.2
  444.0 99.4 %copy-start.2 = (f32[384,1536]{1,0:T(8,128)S(1)}, f32[384,1536]{1,0:T(8,128)}, u32[]{:S(2)}) copy-start(f32[384,1536]{1,0:T(8,128)} %get-tuple-element.38.res_hbm) | copy-start | bytes 7077892
  542.3 11.9 %collective-permute-start.7 = (bf16[96,2176]{1,0:T(8,128)(2,1)}, bf16[96,2176]{1,0:T(8,128)(2,1)S(1)}, u32[]{:S(2)}, u32[]{:S(2)}) collective-permute-start(bf16[96,2176]{1,0:T(8,128)(2,1)} %get-tuple-element.59), channel_id=1, source_target_pairs={{0,16},{1,17},{2,18},{3,19},{4,20},{5,21},{6,22},{7,23},{8,24},{9,... | collective-permute-start | bytes 1253384 | tf_op jit(solution)/shard_map/ppermute | solution.py:1561
  543.4 3.6 copy-start
  543.4 3.6 copy-start.1
  547.0 7.2 %copy-start.4 = (bf16[96,2176]{1,0:T(8,128)(2,1)S(1)}, bf16[96,2176]{1,0:T(8,128)(2,1)}, u32[]{:S(2)}) copy-start(bf16[96,2176]{1,0:T(8,128)(2,1)} %get-tuple-element.59) | copy-start | bytes 1253380
  551.1 5.9 %copy-start.3 = (f32[384,1536]{1,0:T(8,128)S(1)}, f32[384,1536]{1,0:T(8,128)}, u32[]{:S(2)}) copy-start(f32[384,1536]{1,0:T(8,128)} %get-tuple-element.94) | copy-start | bytes 7077892

commit v5 on v4

--- a/solution.py
+++ b/solution.py
@@ -75,6 +75,8 @@
         self.y = (r, f + 2 - 4 * self.yb)
         self.core = (r, f + 1 - 2 * self.c)
         self.diagonal = (r, f + 3 - 4 * self.yb - 2 * self.c)
+        self.others = {1: self.core, 2: self.y, 3: self.diagonal, 4: self.x}
+        self.others.update({4 + n: (self.x[0], self.others[n][1]) for n in (1, 2, 3)})
         self.along = [None] + [(r, (f + 4 * k) % group) for k in range(1, planes)]
         self.planes, self.send_sems, self.recv_sems, self.copies = planes, send_sems, recv_sems, []
 
@@ -165,15 +167,93 @@
 LANES = 2 * HEAD
 
 
-def forward(starts, tokens, cotangent, own, w_gate, w_up, w_down, planes, group):
+class FrontGather:
+    def __init__(self, at, own, full, base, part, own_sem):
+        self.at, self.own, self.full, self.base = at, own, full, base
+        self.ds, self.half = own.shape
+        self.first, self.second = (0, part), (part, self.half - part)
+        self.every = (0, self.half)
+        self.own_copy = pltpu.make_async_copy(own, self.region(0, 0, 0, self.every), own_sem)
+        self.x_first, self.x_second, self.y_first, self.y_second, self.far = [], [], [], [], []
+
+    def region(self, k, dx, dy, span):
+        at = self.at
+        row = (((at.z + at.planes - k) % at.planes) * 4 + (at.yb + dy) % 2 * 2 + at.c) * self.ds
+        col = self.base + (at.xb + dx) % 2 * self.half + span[0]
+        return self.full.at[
+            pl.ds(pl.multiple_of(row, 16), self.ds), pl.ds(pl.multiple_of(col, 128), span[1])
+        ]
+
+    def pass_on(self, k, dx, dy, span, device):
+        here = self.region(k, dx, dy, span)
+        return self.at.send(here, here, device)
+
+    def start(self):
+        at = self.at
+        self.own_copy.start()
+        here = self.region(0, 0, 0, self.every)
+        self.arrive = [None] + [at.send(self.own, here, at.along[k]) for k in range(1, at.planes)]
+
+    def start_plane(self):
+        here = self.region(0, 0, 0, self.every)
+        self.to_core = [self.at.send(self.own, here, self.at.core)]
+        self.spread(0)
+
+    def spread(self, k):
+        at = self.at
+        for device, span, copies in (
+            (at.x, self.first, self.x_first),
+            (at.y, self.second, self.y_second),
+            (at.x, self.second, self.x_second),
+            (at.y, self.first, self.y_first),
+        ):
+            here = self.region(k, 0, 0, span)
+            src = self.own.at[:, pl.ds(span[0], span[1])] if k == 0 else here
+            copies.append(at.send(src, here, device))
+        if k > 0:
+            self.to_core.append(self.pass_on(k, 0, 0, self.every, at.core))
+
+    def advance(self, k):
+        self.arrive[k].wait_recv()
+        self.spread(k)
+
+    def onward(self, k):
+        at = self.at
+        self.x_first[k].wait_recv()
+        self.far.append((k, self.first, self.pass_on(k, 1, 0, self.first, at.y)))
+        self.y_second[k].wait_recv()
+        self.far.append((k, self.second, self.pass_on(k, 0, 1, self.second, at.x)))
+        self.x_second[k].wait_recv()
+        self.to_core.append(self.pass_on(k, 1, 0, self.every, at.core))
+        self.y_first[k].wait_recv()
+        self.to_core.append(self.pass_on(k, 0, 1, self.every, at.core))
+
+    def finish_far(self):
+        for k, span, copy in self.far:
+            copy.wait_recv()
+            self.to_core.append(self.pass_on(k, 1, 1, span, self.at.core))
+
+    def finish(self):
+        for copy in self.to_core:
+            copy.wait_recv()
+        self.own_copy.wait()
+
+    @staticmethod
+    def copies(planes):
+        return planes - 1 + planes * 11
+
+
+def forward(
+    starts, tokens, cotangent, own_mix, own_out, shares, w_gate, w_up, w_down, planes, group
+):
     length, width = tokens.shape
-    ds, half = own.shape
+    ds = own_mix.shape[0]
     hid, hs = w_gate.shape[2], w_down.shape[0]
     wide = 3 * hid
-    part = share_of(half, 0.25)
-    first, second, every = (0, part), (part, half - part), (0, half)
     kvd = KV_HEADS * HEAD
     mix = width + 2 * kvd
+    base = 2 * own_mix.shape[1]
+    columns = base + width
     row_half = length // 2
     low_rows, high_rows = pl.ds(0, row_half), pl.ds(row_half, row_half)
     tables = turn_tables(length)
@@ -182,7 +262,9 @@
         starts_ref,
         x_ref,
         cot_ref,
-        own_ref,
+        own_mix_ref,
+        own_out_ref,
+        share_ref,
         gate_hbm,
         up_hbm,
         down_hbm,
@@ -191,6 +273,7 @@
         wall_a,
         wall_b,
         grads_out,
+        shares_out,
         gain_ref,
         q_ref,
         kk_ref,
@@ -210,7 +293,7 @@
         load_sems,
     ):
         at = Links(planes, group, send_sems, recv_sems)
-        at.barrier([at.x, at.y, at.core, at.diagonal] + at.along[1:])
+        at.barrier(list(at.others.values()) + at.along[1:])
         walls = (wall_a, wall_b)
         shard = at.yb * 2 + at.c
 
@@ -291,69 +374,42 @@
             else:
                 ring[e] = (planes, [])
 
-        def region(k, dx, dy, span):
-            row = (((at.z + planes - k) % planes) * 4 + (at.yb + dy) % 2 * 2 + at.c) * ds
-            col = (at.xb + dx) % 2 * half + span[0]
-            return front.at[
-                pl.ds(pl.multiple_of(row, 16), ds), pl.ds(pl.multiple_of(col, 128), span[1])
-            ]
-
-        def pass_on(k, dx, dy, span, device):
-            here = region(k, dx, dy, span)
-            return at.send(here, here, device)
-
-        x_first, x_second, y_first, y_second, far = [], [], [], [], []
-
-        def spread(k):
-            for device, span, copies in (
-                (at.x, first, x_first),
-                (at.y, second, y_second),
-                (at.x, second, x_second),
-                (at.y, first, y_first),
-            ):
-                here = region(k, 0, 0, span)
-                src = own_ref.at[:, pl.ds(span[0], span[1])] if k == 0 else here
-                copies.append(at.send(src, here, device))
-            if k > 0:
-                to_core.append(pass_on(k, 0, 0, every, at.core))
-
-        def onward(k):
-            x_first[k].wait_recv()
-            far.append((k, first, pass_on(k, 1, 0, first, at.y)))
-            y_second[k].wait_recv()
-            far.append((k, second, pass_on(k, 0, 1, second, at.x)))
-            x_second[k].wait_recv()
-            to_core.append(pass_on(k, 1, 0, every, at.core))
-            y_first[k].wait_recv()
-            to_core.append(pass_on(k, 0, 1, every, at.core))
-
-        own_copy = pltpu.make_async_copy(own_ref, region(0, 0, 0, every), local_sems.at[2])
-        own_copy.start()
-        arrive = [None] + [
-            at.send(own_ref, region(0, 0, 0, every), at.along[k]) for k in range(1, planes)
-        ]
-        to_core = [at.send(own_ref, region(0, 0, 0, every), at.core)]
-        spread(0)
+        mixing = FrontGather(
+            at, own_mix_ref, front, 0, share_of(base // 2, 0.25), local_sems.at[2]
+        )
+        closing = FrontGather(
+            at, own_out_ref, front, base, share_of(width // 2, 0.25), local_sems.at[5]
+        )
+
+        def share_slot(j):
+            return shares_out.at[j // 2, :, pl.ds(j % 2 * length, length)]
+
+        mixing.start()
+        mixing.start_plane()
+        closing.start()
         pack(0)
         first_exchange = exchange(0)
+        place = at.xb * 4 + shard
+        locals_.append(pltpu.make_async_copy(share_ref.at[place], share_slot(0), local_sems.at[6]))
+        locals_[-1].start()
+        got_shares = []
+        for j, device in at.others.items():
+            other = (
+                (at.xb + j // 4) % 2 * 4 + (at.yb + j // 2 % 2) % 2 * 2 + (at.c + j % 2) % 2
+            )
+            got_shares.append(at.send(share_ref.at[other], share_slot(j), device))
         pack(1)
-        second_exchange = exchange(1)
         fill_bias(bias, starts_ref[0])
         for k in range(1, planes):
-            arrive[k].wait_recv()
-            spread(k)
-            onward(k - 1)
+            mixing.advance(k)
+            mixing.onward(k - 1)
         ring_first(0, first_exchange)
-        onward(planes - 1)
-        for k, span, copy in far:
-            copy.wait_recv()
-            to_core.append(pass_on(k, 1, 1, span, at.core))
-        for copy in to_core:
-            copy.wait_recv()
-        own_copy.wait()
-        front_copy = pltpu.make_async_copy(front, front_out, local_sems.at[3])
-        front_copy.start()
-
+        mixing.onward(planes - 1)
+        mixing.finish_far()
+        closing.start_plane()
+        for k in range(1, planes):
+            closing.advance(k)
+        mixing.finish()
         def gather_start(src, out):
             def slot(j, rows=pl.ds(0, length)):
                 return out.at[j, rows]
@@ -385,11 +441,7 @@
             got["far_high"].wait_recv()
             got["core"].append(at.send(slot(6, high_rows), slot(7, high_rows), at.core))
 
-        grads = gather_start(cot_ref, grads_out)
-        cot_copy = pltpu.make_async_copy(cot_ref, grads_out.at[0], local_sems.at[4])
-        cot_copy.start()
-
-        gain_ref[...] = front[:, mix + width : mix + width + 128].astype(F32).T[:8]
+        gain_ref[...] = front[:, mix : mix + 128].astype(F32).T[:8]
 
         def norm(chunk):
             x = x_ref[chunk].astype(F32)
@@ -407,38 +459,48 @@
                     turned_low = turned(values, tab_ref, 1.0).astype(BF).astype(F32)
                     q_ref[:, col : col + LANES] = (turned_low * (1.0 / math.sqrt(HEAD))).astype(BF)
                 else:
-                    target, base = (kk_ref, width) if col < width + kvd else (vv_ref, width + kvd)
+                    target, start = (kk_ref, width) if col < width + kvd else (vv_ref, width + kvd)
                     if col < width + kvd:
                         values = turned(values, tab_ref, 1.0)
 
                     def store(side, head, side_values, target=target):
                         target[side, head] = side_values
 
-                    both_sides(values, store, (col - base) // LANES)
+                    both_sides(values, store, (col - start) // LANES)
         ring_next(0)
+        grads = gather_start(cot_ref, grads_out)
+        cot_copy = pltpu.make_async_copy(cot_ref, grads_out.at[0], local_sems.at[4])
+        cot_copy.start()
+
 
         def attend(pairs):
             @pl.loop(*pairs)
             def _(p):
                 cols = pl.ds(pl.multiple_of(p * LANES, LANES), LANES)
-                for n in range(length // 128):
-                    rows = slice(n * 128, (n + 1) * 128)
-                    total = None
-                    for side in range(2):
-                        head = (2 * p + side) // GROUP
-                        probs = softmax_rows(q_ref[rows, cols], kk_ref[side, head], bias[rows])
-                        term = dot(probs.astype(BF), vv_ref[side, head])
-                        total = term if total is None else total + term
-                    att_ref[rows, cols] = total.astype(BF)
-
-        attend((0, PAIRS // 2))
+                total = None
+                for side in range(2):
+                    head = (2 * p + side) // GROUP
+                    probs = softmax_rows(q_ref[:, cols], kk_ref[side, head], bias[...])
+                    term = dot(probs.astype(BF), vv_ref[side, head])
+                    total = term if total is None else total + term
+                att_ref[:, cols] = total.astype(BF)
+
+        attend((0, PAIRS // 3))
+        for k in range(planes):
+            closing.onward(k)
+        attend((PAIRS // 3, 2 * PAIRS // 3))
         gather_middle(*grads)
+        second_exchange = exchange(1)
+        attend((2 * PAIRS // 3, PAIRS))
+        closing.finish_far()
+        closing.finish()
+        front_copy = pltpu.make_async_copy(front, front_out, local_sems.at[3])
+        front_copy.start()
         ring_next(0)
-        attend((PAIRS // 2, PAIRS))
         for n in range(width // block):
             cols = slice(n * block, (n + 1) * block)
             res_ref[:, cols] = x_ref[:, cols].astype(F32) + dot(
-                att_ref[...], front[:, mix + n * block : mix + (n + 1) * block]
+                att_ref[...], front[:, base + n * block : base + (n + 1) * block]
             )
 
         def norm_two(chunk):
@@ -450,21 +512,22 @@
         gather_last(*grads)
         while ring[0][0] < planes:
             ring_next(0)
-        for copy in grads[1]["core"] + second_exchange:
+        for copy in grads[1]["core"] + second_exchange + got_shares:
             copy.wait_recv()
         for copy in locals_ + [front_copy, cot_copy]:
             copy.wait()
         at.finish()
 
     shape = jax.ShapeDtypeStruct
-    count = planes - 1 + planes * 11 + 2 * 3 + 4 + planes - 2 + 13
+    count = 2 * FrontGather.copies(planes) + 2 * 3 + 4 + planes - 2 + 13 + 7
     return pl.pallas_call(
         kernel,
         out_shape=[
-            shape((width, 2 * half), BF),
+            shape((width, columns), BF),
             shape((planes, 4, ds, wide), BF),
             shape((planes, 4, ds, wide), BF),
             shape((PLANE, length, width), BF),
+            shape((PLANE // 2, 8, 2 * length), F32),
             shape((8, width), F32),
             shape((length, width), BF),
             shape((2, KV_HEADS, length, LANES), BF),
@@ -475,24 +538,26 @@
             shape((length, width), BF),
         ],
         in_specs=[pl.BlockSpec(memory_space=pltpu.SMEM)]
-        + [whole_vmem()] * 3
+        + [whole_vmem()] * 5
         + [anywhere()] * 3
         + [whole_vmem()],
-        out_specs=[anywhere()] * 4 + [whole_vmem()] * 8,
+        out_specs=[anywhere()] * 5 + [whole_vmem()] * 8,
         scratch_shapes=[
-            pltpu.VMEM((width, 2 * half), BF),
+            pltpu.VMEM((width, columns), BF),
             pltpu.VMEM((length, length), F32),
             pltpu.VMEM((4, EPD, ds, wide), BF),
             pltpu.VMEM((2, 2, ds, hid), F32),
             pltpu.VMEM((2, hs, width), F32),
         ]
         + dma_pairs(count)
-        + [pltpu.SemaphoreType.DMA((5,)), pltpu.SemaphoreType.DMA((2, 3))],
+        + [pltpu.SemaphoreType.DMA((7,)), pltpu.SemaphoreType.DMA((2, 3))],
         compiler_params=comm_params(0),
         cost_estimate=pl.CostEstimate(
             flops=150_000_000_000, bytes_accessed=20_000_000, transcendentals=0
         ),
-    )(starts, tokens, cotangent, own, w_gate, w_up, w_down, tables)
+    )(
+        starts, tokens, cotangent, own_mix, own_out, shares, w_gate, w_up, w_down, tables
+    )
 
 
 class PlaneSum:
@@ -1024,6 +1089,7 @@
     piece, wide = pack_a.shape[1:]
     ds = piece // 4
     extra = columns - mix - width
+    part = block // 2
 
     def kernel(
         starts_ref,
@@ -1080,7 +1146,7 @@
 
         load_res = local(res_hbm, in_ref, 0)
         load_out_w = local(
-            w_hbm.at[:, pl.ds(mix, width)], w_ref.at[:, pl.ds(0, width)], 1
+            w_hbm.at[:, pl.ds(mix + extra, width)], w_ref.at[:, pl.ds(0, width)], 1
         )
         plane = PlaneSum(
             at,
@@ -1103,14 +1169,15 @@
         turn = [0]
 
         def put(values, column, count):
-            n = turn[0] % 2
-            turn[0] += 1
-            if staged[n] is not None:
-                staged[n].wait()
-            stage[n, :, :count] = values
-            staged[n] = local(
-                stage.at[n, :, pl.ds(0, count)], grad_hbm.at[:, pl.ds(column, count)], 8 + n
-            )
+            for base in range(0, count, part):
+                n = turn[0] % 2
+                turn[0] += 1
+                if staged[n] is not None:
+                    staged[n].wait()
+                stage[n] = values[:, base : base + part]
+                staged[n] = local(
+                    stage.at[n], grad_hbm.at[:, pl.ds(column + base, part)], 8 + n
+                )
 
         fill_bias(bias, starts_ref[0])
         gain_sum[...] = jnp.zeros_like(gain_sum)
@@ -1138,7 +1205,7 @@
         load_mix_w = local(w_hbm.at[:, pl.ds(0, mix)], w_ref, 1)
         for n in range(width // block):
             cols = slice(n * block, (n + 1) * block)
-            put(dot_tn(att_ref[...], mixed[:, cols]).astype(BF), mix + n * block, block)
+            put(dot_tn(att_ref[...], mixed[:, cols]).astype(BF), mix + extra + n * block, block)
         load_n1 = local(n1_hbm, mixed, 0)
         for copy in loads:
             copy.wait()
@@ -1152,22 +1219,20 @@
             @pl.loop(lower, upper)
             def _(p):
                 cols = pl.ds(pl.multiple_of(p * LANES, LANES), LANES)
-                for n in range(length // 128):
-                    rows = slice(n * 128, (n + 1) * 128)
-                    total = None
-                    for side in range(2):
-                        head = (2 * p + side) // GROUP
-                        query, grad = q_ref[rows, cols], context[rows, cols]
-                        probs = softmax_rows(query, kk_ref[side, head], bias[rows])
-                        grad_probs = dot_nt(grad, vv_ref[side, head])
-                        value_sum[side, head] += dot_tn(probs.astype(BF), grad)
-                        inner = jnp.sum(probs * grad_probs, axis=1, keepdims=True)
-                        logit = (probs * (grad_probs - inner)).astype(BF)
-                        term = dot(logit, kk_ref[side, head])
-                        total = term if total is None else total + term
-                        key_sum[side, head] += dot_tn(logit, query)
-                    back = turned(total, tab_ref.at[:, rows], -1.0) * (1.0 / math.sqrt(HEAD))
-                    grad_mix[rows, cols] = back.astype(BF)
+                total = None
+                for side in range(2):
+                    head = (2 * p + side) // GROUP
+                    query, grad = q_ref[:, cols], context[:, cols]
+                    probs = softmax_rows(query, kk_ref[side, head], bias[...])
+                    grad_probs = dot_nt(grad, vv_ref[side, head])
+                    value_sum[side, head] += dot_tn(probs.astype(BF), grad)
+                    inner = jnp.sum(probs * grad_probs, axis=1, keepdims=True)
+                    logit = (probs * (grad_probs - inner)).astype(BF)
+                    term = dot(logit, kk_ref[side, head])
+                    total = term if total is None else total + term
+                    key_sum[side, head] += dot_tn(logit, query)
+                back = turned(total, tab_ref, -1.0) * (1.0 / math.sqrt(HEAD))
+                grad_mix[:, cols] = back.astype(BF)
 
         attend(0, PAIRS // 3)
         plane.onward_x()
@@ -1218,7 +1283,7 @@
 
         row_loop(length, 32, input_grad)
         gain_rows = jnp.concatenate([gain_sum[...].T, jnp.zeros((width, extra - 8), F32)], axis=1)
-        put(gain_rows.astype(BF), mix + width, extra)
+        put(gain_rows.astype(BF), mix, extra)
 
         def store(chunk, total):
             sum_ref[chunk] = total
@@ -1253,7 +1318,7 @@
             pltpu.VMEM((2, KV_HEADS, length, LANES), F32),
             pltpu.VMEM((2, KV_HEADS, length, LANES), F32),
             pltpu.VMEM((width, mix), BF),
-            pltpu.VMEM((2, width, block), BF),
+            pltpu.VMEM((2, width, part), BF),
             pltpu.VMEM((4, length, width), BF),
             pltpu.VMEM((4 * length, width), BF),
             pltpu.VMEM((2, length // 2, width), BF),
@@ -1468,13 +1533,14 @@
     )(grad, pack, before)
 
 
-def unpack(packs, hs):
+def unpack(packs, residual, term, hs):
     ds, wide = packs[0].shape[1:]
     hid = wide // 3
     blocks = ds // hs
 
     def kernel(*refs):
-        ins, (gate_out, up_out, down_out, raw_in, raw_down, sems) = refs[:EPD], refs[EPD:]
+        ins, (res_ref, term_ref) = refs[:EPD], refs[EPD : EPD + 2]
+        gate_out, up_out, down_out, sum_ref, raw_in, raw_down, sems = refs[EPD + 2 :]
         copies = {}
         for n, (p, e) in enumerate((p, e) for p in range(PLANE) for e in range(EPD)):
             slot = n % 4
@@ -1504,6 +1570,11 @@
             ]
             for copy in copies[n]:
                 copy.start()
+
+        def add(chunk):
+            sum_ref[chunk] = res_ref[chunk] + term_ref[chunk]
+
+        row_loop(residual.shape[0], 32, add)
         for n in range(EXP - 4, EXP):
             for copy in copies[n]:
                 copy.wait()
@@ -1511,12 +1582,13 @@
     shape = jax.ShapeDtypeStruct
     return pl.pallas_call(
         kernel,
-        in_specs=[whole_vmem()] * EPD,
-        out_specs=[anywhere()] * 3,
+        in_specs=[whole_vmem()] * (EPD + 2),
+        out_specs=[anywhere()] * 3 + [whole_vmem()],
         out_shape=[
             shape((ds, EXP, hid), F32),
             shape((ds, EXP, hid), F32),
             shape((hs, EXP, blocks * hid), F32),
+            shape(residual.shape, F32),
         ],
         scratch_shapes=[
             pltpu.VMEM((4, 2, ds, hid), F32),
@@ -1524,7 +1596,7 @@
             pltpu.SemaphoreType.DMA((4, 3)),
         ],
         compiler_params=pltpu.CompilerParams(vmem_limit_bytes=32 * 2**20),
-    )(*packs)
+    )(*packs, residual, term)
 
 
 def shards(
@@ -1581,35 +1653,35 @@
     half_rows = length // 2
 
     mix = width + 2 * kvd
-    columns = mix + width + 256
-    half = columns // 2
+    gain_end = mix + 256
     gains = jnp.stack([norm1_gain.astype(BF), norm2_gain.astype(BF)], axis=1)
-    front_own = jnp.concatenate(
+    own_mix = jnp.concatenate(
         [
             w_query.astype(BF),
             w_key.astype(BF),
             w_value.astype(BF),
-            w_out.astype(BF),
             gains,
             jnp.zeros((ds, 254), BF),
         ],
         axis=1,
     )
+
+    def rep_half(own):
+        half = own.shape[1] // 2
+        return lax.dynamic_slice(own, (0, xb * half), (ds, half))
+
     experts = jnp.arange(EXP, dtype=jnp.int32)[:, None, None]
     share = jnp.sum(jnp.where(routes[None] == experts, gates[None], 0.0), axis=2)
-    shares = []
-    for j in range(PLANE):
-        block = lax.dynamic_slice(share, ((mine ^ j) * EPD, 0), (EPD, length))
-        shares.append(block if j == 0 else go(block, j // 4, (j // 2) % 2, j % 2))
     pairs = PLANE // 2
-    shares = jnp.concatenate(shares, axis=1).reshape(EPD, pairs, 2 * length).transpose(1, 0, 2)
-    shares = jnp.pad(shares, ((0, 0), (0, 8 - EPD), (0, 0)))
-
-    front, wall_a, wall_b, grads_all, gains_all, q, kk, vv, att, residual, n1, n2 = forward(
+    share = jnp.pad(share.reshape(PLANE, EPD, length), ((0, 0), (0, 8 - EPD), (0, 0)))
+
+    front, wall_a, wall_b, grads_all, shares, gains_all, q, kk, vv, att, residual, n1, n2 = forward(
         starts,
         tokens,
         cotangent,
-        lax.dynamic_slice(front_own, (0, xb * half), (ds, half)),
+        rep_half(own_mix),
+        rep_half(w_out.astype(BF)),
+        share,
         w_gate,
         w_up,
         w_down,
@@ -1645,10 +1717,11 @@
         planes,
         group,
     )
-    output = residual + out_term
     front_total, shards_b = scatter_front(front_grad, pack_b, before_b, planes, group)
     total = all_reps(front_total)
-    gate_shard, up_shard, down_shard = unpack([all_reps(shards_a), all_reps(shards_b)], hs)
+    gate_shard, up_shard, down_shard, output = unpack(
+        [all_reps(shards_a), all_reps(shards_b)], residual, out_term, hs
+    )
     other = go(total, 1, 0, 0)
     front_shard = jnp.where(
         xb == 0,
@@ -1658,12 +1731,12 @@
     return (
         output,
         input_grad,
-        front_shard[:, mix + width],
+        front_shard[:, mix],
         front_shard[:, :width],
         front_shard[:, width : width + kvd],
         front_shard[:, width + kvd : mix],
-        front_shard[:, mix : mix + width],
-        front_shard[:, mix + width + 1],
+        front_shard[:, gain_end:],
+        front_shard[:, mix + 1],
         gate_shard,
         up_shard,
         down_shard,

time: 567 us -> 553 us (0.975)
  starting transfers between devices: 8.52 us -> 0.39 us
  waiting for transfers between devices: 7.5 us -> 0.89 us
    ppermute x8 -> x1, starting transfers between devices: 8.52 us -> 0.39 us  [pp(): return lax.ppermute(value, AXES, perm(to))]
    ppermute x8 -> x1, waiting for transfers between devices: 7.5 us -> 0.89 us  [pp(): return lax.ppermute(value, AXES, perm(to))]
  transfers between devices with their start and end apart: 8 -> 1, of which waited for: 3 -> 1; matrix products, arithmetic and copies ran while one was open for 3% -> 0% of each run, Pallas kernels for 27% -> 1%
where the time goes in v5:
time: 553 us; the launch traced here: 544 us
  Pallas kernels  523 us (95%)
  local copies, waits for them, and re-layouts  11.7 us (2%)
  other arithmetic  6.88 us (1%)
    pallas_call x1, Pallas kernels, run_experts(): pl.pallas_call(kernel, in_specs=[anywhere()] * 2 + [whole_vmem()] + [anyw...  164 us
    pallas_call x1, Pallas kernels, forward(): pl.pallas_call(kernel, out_shape=[shape((width, columns), BF), shape((pla...  153 us
    pallas_call x1, Pallas kernels, backward(): pl.pallas_call(kernel, in_specs=[pl.BlockSpec(memory_space=pltpu.SMEM)] +...  101 us
    pallas_call x1, Pallas kernels, scatter_front(): pl.pallas_call(kernel, out_shape=[jax.ShapeDtypeStruct((ds, half), BF), j...  98.6 us
  transfers between devices with their start and end apart: 1, of which 1 were waited for; matrix products, arithmetic and copies ran while one was open for 0% of the time, Pallas kernels for 1%

profile of v5, /device:TPU:0, one launch (start us, length us, event | category | flops | bytes accessed | tf_op | source)
XLA Modules:
  0.0 544.4 jit_solution(3801784079755548313)
XLA Ops:
  0.6 0.0 copy-start
  1.4 0.7 convert_bitcast_fusion.1
  2.1 0.7 convert_bitcast_fusion
  2.7 0.1 copy.34
  2.9 0.1 copy.33
  3.0 0.8 select_reduce_fusion
  3.8 0.9 convert_element_type.36
  4.7 0.9 convert_element_type.37
  5.7 1.1 convert_element_type.35
  6.8 0.7 pad.4.share_ref
  7.5 0.0 copy-done
  7.5 0.7 dynamic-slice_convert_fusion.own_out_ref
  8.1 0.3 concatenate.9
  8.4 0.7 constant_dynamic-slice_fusion.own_mix_ref
  9.1 0.8 negate_select_fusion
  9.9 0.9 pad_maximum_fusion.tab_ref
  10.8 152.9 %shard_map.221 = (bf16[1536,4352]{1,0:T(8,128)(2,1)}, bf16[4,4,96,1536]{3,2,1,0:T(8,128)(2,1)}, bf16[4,4,96,1536]{3,2,1,0:T(8,128)(2,1)}, bf16[8,384,1536]{2,1,0...) custom-call(s32[1]{0:T(128)S(6)} %copy.36.starts_ref, ...), custom_call_target="tpu_custom_call" | custom-call | flops 149999992832 | bytes 20000000 | tf_op jit(solution)/shard_map/pallas_call | solution.py:523
  163.6 164.3 %shard_map.222 = (bf16[4,768,1536]{2,1,0:T(8,128)(2,1)}, bf16[4,384,1536]{2,1,0:T(8,128)(2,1)}, bf16[4,384,1536]{2,1,0:T(8,128)(2,1)}, f32[384,1536]{1,0:T(8,128)}, bf16[384,1536]{1,0:T(8,128)(2,1)}) custom-call(bf16[384,1536]{1,0:T(8,128)(2,1)} %get-tuple-element.40.n2_hbm, bf16[4,768,1536]{2,1,0:T(8,128)(2,1)} %bitcast.9, ...), custom_call_target="tpu_custom_call" | custom-call | flops 99999997952 | bytes 50000000 | tf_op jit(solution)/shard_map/pallas_call | solution.py:982
  328.0 101.3 %shard_map.223 = (f32[384,1536]{1,0:T(8,128)}, f32[384,1536]{1,0:T(8,128)}, bf16[384,1536]{1,0:T(8,128)(2,1)}, bf16[1536,4352]{1,0:T(8,128)(2,1)}, bf16[8,96,1536]{2,1,0:T(8,128)(2,1)}) custom-call(s32[1]{0:T(128)S(6)} %copy.36.starts_ref, f32[384,1536]{1,0:T(8,128)} %get-tuple-element.45.d_ref, bf16[384,1536]{1,0:T(8,128)(2,1)} %cot_ref.3, ...), custom_call_target="tpu_custom_call" | custom-call | flops 80000000000 | bytes 50000000 | tf_op jit(solution)/shard_map/pallas_call | solution.py:1299
  429.3 0.0 copy-start.2
  429.3 98.6 %shard_map.224 = (bf16[96,2176]{1,0:T(8,128)(2,1)}, bf16[8,96,1536]{2,1,0:T(8,128)(2,1)}) custom-call(bf16[1536,4352]{1,0:T(8,128)(2,1)} %get-tuple-element.59.g_ref, bf16[4,384,1536]{2,1,0:T(8,128)(2,1)} %get-tuple-element.57.pack_b_ref.pack_ref, bf16[384,1536]{1,0:T(8,128)(2,1)} %get-tuple-element.60.before_ref), custom_call_target="tpu_custom_call" | custom-call | flops 49999998976 | bytes 20000000 | tf_op jit(solution)/shard_map/pallas_call | solution.py:1506
  527.9 0.4 collective-permute-start
  528.3 0.0 copy-done.2
  528.3 0.0 copy-start.3
  528.3 1.7 copy-done.3
  530.0 0.0 copy-start.4
  530.0 1.7 copy-done.4
  531.7 0.0 copy-start.5
  531.7 1.7 copy-done.5
  533.3 0.0 copy-start.7
  533.3 5.5 %shard_map.225 = (f32[96,16,512]{2,1,0:T(8,128)}, f32[96,16,512]{2,1,0:T(8,128)}, f32[32,16,1536]{2,1,0:T(8,128)}, f32[384,1536]{1,0:T(8,128)}) custom-call(bf16[8,96,1536]{2,1,0:T(8,128)(2,1)S(1)} %copy-done.4, bf16[8,96,1536]{2,1,0:T(8,128)(2,1)S(1)} %copy-done.5, f32[384,1536]{1,0:T(8,128)S(1)} %copy-done.2, f32[384,1536]{1,0:T(8,128)S(1)} %copy-done.3), custom_call_target="tpu_custom_call" | custom-call | tf_op jit(solution)/shard_map/pallas_call | solution.py:1583
  538.8 0.0 copy-start.6
  538.8 0.9 collective-permute-done
  539.7 0.0 copy-done.7
  539.7 0.2 fusion
  539.9 0.7 slice_reduce_fusion
  540.6 0.8 fusion.9
  541.4 1.1 fusion.8
  542.5 0.0 copy-start.1
  542.5 0.0 copy-done.6
  542.5 1.4 copy.37
  543.9 0.0 copy-done.1
  (4 shorter events, 0.0 us)
Async XLA Ops:
  0.6 6.8 %copy-start = (f32[96,1536]{1,0:T(8,128)S(1)}, f32[96,1536]{1,0:T(8,128)}, u32[]{:S(2)}) copy-start(f32[96,1536]{1,0:T(8,128)} %param.23) | copy-start | bytes 1769476
  429.3 99.0 %copy-start.2 = (f32[384,1536]{1,0:T(8,128)S(1)}, f32[384,1536]{1,0:T(8,128)}, u32[]{:S(2)}) copy-start(f32[384,1536]{1,0:T(8,128)} %get-tuple-element.53.res_hbm.refs_2_) | copy-start | bytes 7077892
  527.9 11.8 %collective-permute-start = (bf16[96,2176]{1,0:T(8,128)(2,1)}, bf16[96,2176]{1,0:T(8,128)(2,1)S(1)}, u32[]{:S(2)}, u32[]{:S(2)}) collective-permute-start(bf16[96,2176]{1,0:T(8,128)(2,1)} %get-tuple-element.65), channel_id=1, source_target_pairs={{0,16},{1,17},{2,18},{3,19},{4,20},{5,21},{6,22},{7,23},{8,24},{9,... | collective-permute-start | bytes 1253384 | tf_op jit(solution)/shard_map/ppermute | solution.py:1633
  528.3 1.7 copy-start.3
  530.0 1.7 copy-start.4
  531.7 1.7 copy-start.5
  533.3 6.4 %copy-start.7 = (bf16[96,2176]{1,0:T(8,128)(2,1)S(1)}, bf16[96,2176]{1,0:T(8,128)(2,1)}, u32[]{:S(2)}) copy-start(bf16[96,2176]{1,0:T(8,128)(2,1)} %get-tuple-element.65) | copy-start | bytes 1253380
  538.8 3.7 copy-start.6
  542.5 1.4 copy-start.1

commit v6 on v5

--- a/solution.py
+++ b/solution.py
@@ -275,6 +275,13 @@
         grads_out,
         shares_out,
         gain_ref,
+        q_out,
+        kk_out,
+        vv_out,
+        att_out,
+        res_out,
+        n1_out,
+        n2_out,
         q_ref,
         kk_ref,
         vv_ref,
@@ -342,6 +349,14 @@
             locals_.append(copy)
 
         locals_ = []
+
+        def put(*pairs):
+            for src, dst in pairs:
+                n = len(stored)
+                stored.append(pltpu.make_async_copy(src, dst, local_sems.at[7 + n]))
+                stored[n].start()
+
+        stored = []
 
         def exchange(e):
             copies = []
@@ -468,6 +483,7 @@
 
                     both_sides(values, store, (col - start) // LANES)
         ring_next(0)
+        put((q_ref, q_out), (kk_ref, kk_out), (vv_ref, vv_out), (n1_ref, n1_out))
         grads = gather_start(cot_ref, grads_out)
         cot_copy = pltpu.make_async_copy(cot_ref, grads_out.at[0], local_sems.at[4])
         cot_copy.start()
@@ -492,6 +508,7 @@
         gather_middle(*grads)
         second_exchange = exchange(1)
         attend((2 * PAIRS // 3, PAIRS))
+        put((att_ref, att_out))
         closing.finish_far()
         closing.finish()
         front_copy = pltpu.make_async_copy(front, front_out, local_sems.at[3])
@@ -509,12 +526,13 @@
             n2_ref[chunk] = (r * inv * gain_ref[1:2, :]).astype(BF)
 
         row_loop(length, 64, norm_two)
+        put((n2_ref, n2_out), (res_ref, res_out))
         gather_last(*grads)
         while ring[0][0] < planes:
             ring_next(0)
         for copy in grads[1]["core"] + second_exchange + got_shares:
             copy.wait_recv()
-        for copy in locals_ + [front_copy, cot_copy]:
+        for copy in locals_ + stored + [front_copy, cot_copy]:
             copy.wait()
         at.finish()
 
@@ -541,8 +559,15 @@
         + [whole_vmem()] * 5
         + [anywhere()] * 3
         + [whole_vmem()],
-        out_specs=[anywhere()] * 5 + [whole_vmem()] * 8,
+        out_specs=[anywhere()] * 5 + [whole_vmem()] + [anywhere()] * 7,
         scratch_shapes=[
+            pltpu.VMEM((length, width), BF),
+            pltpu.VMEM((2, KV_HEADS, length, LANES), BF),
+            pltpu.VMEM((2, KV_HEADS, length, LANES), BF),
+            pltpu.VMEM((length, width), BF),
+            pltpu.VMEM((length, width), F32),
+            pltpu.VMEM((length, width), BF),
+            pltpu.VMEM((length, width), BF),
             pltpu.VMEM((width, columns), BF),
             pltpu.VMEM((length, length), F32),
             pltpu.VMEM((4, EPD, ds, wide), BF),
@@ -550,7 +575,7 @@
             pltpu.VMEM((2, hs, width), F32),
         ]
         + dma_pairs(count)
-        + [pltpu.SemaphoreType.DMA((7,)), pltpu.SemaphoreType.DMA((2, 3))],
+        + [pltpu.SemaphoreType.DMA((14,)), pltpu.SemaphoreType.DMA((2, 3))],
         compiler_params=comm_params(0),
         cost_estimate=pl.CostEstimate(
             flops=150_000_000_000, bytes_accessed=20_000_000, transcendentals=0
@@ -799,6 +824,7 @@
             y_high.wait_recv()
             far_high.start()
             passed_on[2, high.start].start()
+            ring_next()
             x_high.wait_recv()
             passed_on[4, high.start].start()
             y_low.wait_recv()
@@ -911,7 +937,6 @@
             @pl.when(step == 1)
             def _():
                 spread()
-                ring_next()
 
             @pl.when(step == 2)
             def _():
@@ -920,9 +945,13 @@
             @pl.when(step == 3)
             def _():
                 spread_far()
-                ring_next()
-
-            tile(0, step, 2 * step % 3 + step // 3 * 3, w_a, down_a, lambda: None)
+
+            def middle():
+                @pl.when(step == 2)
+                def _():
+                    ring_next()
+
+            tile(0, step, 2 * step % 3 + step // 3 * 3, w_a, down_a, middle)
 
         pl.semaphore_signal(free, inc=1, device_id=at.core, device_id_type=pl.DeviceIdType.MESH)
         pack(pack_a)
@@ -1097,11 +1126,11 @@
         cot_ref,
         tab_ref,
         gain_ref,
-        q_ref,
-        kk_ref,
-        vv_ref,
-        att_ref,
         before_ref,
+        q_hbm,
+        kk_hbm,
+        vv_hbm,
+        att_hbm,
         x_hbm,
         n1_hbm,
         res_hbm,
@@ -1114,6 +1143,10 @@
         passed_b,
         grad_hbm,
         shards_ref,
+        q_ref,
+        kk_ref,
+        vv_ref,
+        att_ref,
         bias,
         gain_sum,
         mixed,
@@ -1145,6 +1178,11 @@
             return copy
 
         load_res = local(res_hbm, in_ref, 0)
+        load_att = local(att_hbm, att_ref, 12)
+        load_heads = [
+            local(src, dst, 13 + n)
+            for n, (src, dst) in enumerate(((q_hbm, q_ref), (kk_hbm, kk_ref), (vv_hbm, vv_ref)))
+        ]
         load_out_w = local(
             w_hbm.at[:, pl.ds(mix + extra, width)], w_ref.at[:, pl.ds(0, width)], 1
         )
@@ -1203,6 +1241,7 @@
             cols = slice(n * block, (n + 1) * block)
             context[:, cols] = dot_nt(mixed[...], w_ref[cols, :width]).astype(BF)
         load_mix_w = local(w_hbm.at[:, pl.ds(0, mix)], w_ref, 1)
+        load_att.wait()
         for n in range(width // block):
             cols = slice(n * block, (n + 1) * block)
             put(dot_tn(att_ref[...], mixed[:, cols]).astype(BF), mix + extra + n * block, block)
@@ -1234,6 +1273,8 @@
                 back = turned(total, tab_ref, -1.0) * (1.0 / math.sqrt(HEAD))
                 grad_mix[:, cols] = back.astype(BF)
 
+        for copy in load_heads:
+            copy.wait()
         attend(0, PAIRS // 3)
         plane.onward_x()
         plane.onward_y()
@@ -1299,8 +1340,8 @@
     return pl.pallas_call(
         kernel,
         in_specs=[pl.BlockSpec(memory_space=pltpu.SMEM)]
-        + [whole_vmem()] * 9
-        + [anywhere()] * 7,
+        + [whole_vmem()] * 5
+        + [anywhere()] * 11,
         out_specs=[whole_vmem()] * 3 + [anywhere()] * 2,
         out_shape=[
             shape((length, width), F32),
@@ -1310,6 +1351,10 @@
             shape((PLANE, ds, wide), BF),
         ],
         scratch_shapes=[
+            pltpu.VMEM((length, width), BF),
+            pltpu.VMEM((2, KV_HEADS, length, LANES), BF),
+            pltpu.VMEM((2, KV_HEADS, length, LANES), BF),
+            pltpu.VMEM((length, width), BF),
             pltpu.VMEM((length, length), F32),
             pltpu.VMEM((8, width), F32),
             pltpu.VMEM((length, width), BF),
@@ -1330,7 +1375,7 @@
             pltpu.VMEM((planes - 3, piece, wide), BF),
         ]
         + dma_pairs(PlaneSum.copies + 1 + Exchange.copies + planes - 2)
-        + [pltpu.SemaphoreType.DMA((12,))],
+        + [pltpu.SemaphoreType.DMA((16,))],
         compiler_params=pltpu.CompilerParams(
             collective_id=1, has_side_effects=True, vmem_limit_bytes=62 * 2**20
         ),
@@ -1343,11 +1388,11 @@
         cotangent,
         tables,
         gains,
+        before_a,
         q,
         kk,
         vv,
         att,
-        before_a,
         tokens,
         n1,
         residual,
@@ -1361,7 +1406,7 @@
 def scatter_front(grad, pack, before, planes, group):
     rows, columns = grad.shape
     ds, half = rows // (4 * planes), columns // 2
-    part = share_of(half, 0.6)
+    part = share_of(half, 0.66)
     first, second = pl.ds(0, part), pl.ds(part, half - part)
     block, wide = pack.shape[1:]
 
@@ -1382,6 +1427,7 @@
         own,
         passed,
         landing,
+        rows_own,
         send_sems,
         recv_sems,
         local_sems,
@@ -1399,9 +1445,15 @@
             return pl.ds(pl.multiple_of((at.xb + dx) % 2 * half, 128), half)
 
         order = list(range(1, planes)) + [0]
-        arrive = {}
+        arrive, loads = {}, {}
         for k in order:
             for dy in (1, 0):
+                loads[k, dy] = pltpu.make_async_copy(
+                    g_ref.at[pl.ds(row(k, dy, at.c), ds)],
+                    rows_own.at[k, dy],
+                    local_sems.at[2 + 2 * k + dy],
+                )
+                loads[k, dy].start()
                 arrive[k, dy] = at.send(
                     g_ref.at[pl.ds(row(k, dy, 1 - at.c), ds)], from_core.at[k, dy], at.core
                 )
@@ -1410,6 +1462,7 @@
         x_second, y_first, x_first, y_second, to_x, to_y = {}, {}, {}, {}, {}, {}
         for k in order:
             for dy in (1, 0):
+                loads[k, dy].wait()
                 arrive[k, dy].wait_recv()
                 for dx in (1, 0):
 
@@ -1419,10 +1472,7 @@
                     add_rows(
                         store,
                         [
-                            lambda q, k=k, dx=dx, dy=dy: g_ref[
-                                pl.ds(pl.multiple_of(row(k, dy, at.c) + q.start, 16), q.size),
-                                column(dx),
-                            ],
+                            lambda q, k=k, dx=dx, dy=dy: rows_own[k, dy, q, column(dx)],
                             lambda q, k=k, dx=dx, dy=dy: from_core[k, dy, q, column(dx)],
                         ],
                         ds,
@@ -1509,7 +1559,7 @@
             jax.ShapeDtypeStruct((ds, half), BF),
             jax.ShapeDtypeStruct((PLANE, ds, wide), BF),
         ],
-        in_specs=[whole_vmem(), anywhere(), whole_vmem()],
+        in_specs=[anywhere(), anywhere(), whole_vmem()],
         out_specs=[whole_vmem(), anywhere()],
         scratch_shapes=[
             pltpu.VMEM((planes, 2, ds, columns), BF),
@@ -1523,9 +1573,10 @@
             pltpu.VMEM((block, wide), BF),
             pltpu.VMEM((block, wide), BF),
             pltpu.VMEM((block, wide), BF),
+            pltpu.VMEM((planes, 2, ds, columns), BF),
         ]
         + dma_pairs(planes * 8 + planes - 1 + 1 + Exchange.copies)
-        + [pltpu.SemaphoreType.DMA((2,))],
+        + [pltpu.SemaphoreType.DMA((2 + 2 * planes,))],
         compiler_params=comm_params(3),
         cost_estimate=pl.CostEstimate(
             flops=50_000_000_000, bytes_accessed=20_000_000, transcendentals=0
@@ -1539,11 +1590,21 @@
     blocks = ds // hs
 
     def kernel(*refs):
-        ins, (res_ref, term_ref) = refs[:EPD], refs[EPD : EPD + 2]
-        gate_out, up_out, down_out, sum_ref, raw_in, raw_down, sems = refs[EPD + 2 :]
+        sources = refs[: EPD + 2]
+        gate_out, up_out, down_out, sum_ref, raw_in, raw_down = refs[EPD + 2 : EPD + 8]
+        held, (sems, load_sems) = refs[EPD + 8 : -2], refs[-2:]
+        ins, (res_ref, term_ref) = held[:EPD], held[EPD:]
+        loads = [
+            pltpu.make_async_copy(src, dst, load_sems.at[n])
+            for n, (src, dst) in enumerate(zip(sources, held))
+        ]
+        for copy in loads:
+            copy.start()
         copies = {}
-        for n, (p, e) in enumerate((p, e) for p in range(PLANE) for e in range(EPD)):
+        for n, (e, p) in enumerate((e, p) for e in range(EPD) for p in range(PLANE)):
             slot = n % 4
+            if p == 0:
+                loads[e].wait()
             if n >= 4:
                 for copy in copies[n - 4]:
                     copy.wait()
@@ -1574,6 +1635,8 @@
         def add(chunk):
             sum_ref[chunk] = res_ref[chunk] + term_ref[chunk]
 
+        for copy in loads[EPD:]:
+            copy.wait()
         row_loop(residual.shape[0], 32, add)
         for n in range(EXP - 4, EXP):
             for copy in copies[n]:
@@ -1582,7 +1645,7 @@
     shape = jax.ShapeDtypeStruct
     return pl.pallas_call(
         kernel,
-        in_specs=[whole_vmem()] * (EPD + 2),
+        in_specs=[anywhere()] * (EPD + 2),
         out_specs=[anywhere()] * 3 + [whole_vmem()],
         out_shape=[
             shape((ds, EXP, hid), F32),
@@ -1593,9 +1656,11 @@
         scratch_shapes=[
             pltpu.VMEM((4, 2, ds, hid), F32),
             pltpu.VMEM((4, hs, blocks * hid), F32),
-            pltpu.SemaphoreType.DMA((4, 3)),
-        ],
-        compiler_params=pltpu.CompilerParams(vmem_limit_bytes=32 * 2**20),
+        ]
+        + [pltpu.VMEM(packs[0].shape, BF)] * EPD
+        + [pltpu.VMEM(residual.shape, F32)] * 2
+        + [pltpu.SemaphoreType.DMA((4, 3)), pltpu.SemaphoreType.DMA((EPD + 2,))],
+        compiler_params=pltpu.CompilerParams(vmem_limit_bytes=60 * 2**20),
     )(*packs, residual, term)
 
 

time: 553 us -> 545 us (0.986)
  transfers between devices with their start and end apart: 1 -> 1, of which waited for: 1 -> 1; matrix products, arithmetic and copies ran while one was open for 0% -> 0% of each run, Pallas kernels for 1% -> 2%
where the time goes in v6:
time: 545 us; the launch traced here: 537 us
  Pallas kernels  518 us (95%)
  other arithmetic  6.88 us (1%)
  local copies, waits for them, and re-layouts  6.68 us (1%)
    pallas_call x1, Pallas kernels, run_experts(): pl.pallas_call(kernel, in_specs=[anywhere()] * 2 + [whole_vmem()] + [anyw...  161 us
    pallas_call x1, Pallas kernels, forward(): pl.pallas_call(kernel, out_shape=[shape((width, columns), BF), shape((pla...  150 us
    pallas_call x1, Pallas kernels, backward(): pl.pallas_call(kernel, in_specs=[pl.BlockSpec(memory_space=pltpu.SMEM)] +...  103 us
    pallas_call x1, Pallas kernels, scatter_front(): pl.pallas_call(kernel, out_shape=[jax.ShapeDtypeStruct((ds, half), BF), j...  95.7 us
  transfers between devices with their start and end apart: 1, of which 1 were waited for; matrix products, arithmetic and copies ran while one was open for 0% of the time, Pallas kernels for 2%

profile of v6, /device:TPU:0, one launch (start us, length us, event | category | flops | bytes accessed | tf_op | source)
XLA Modules:
  0.0 536.9 jit_solution(4150211507211698732)
XLA Ops:
  0.6 0.0 copy-start
  1.4 0.7 convert_bitcast_fusion.1
  2.1 0.7 convert_bitcast_fusion
  2.7 0.1 copy.34
  2.9 0.1 copy.33
  3.0 0.8 select_reduce_fusion
  3.8 0.9 convert_element_type.36
  4.7 0.9 convert_element_type.37
  5.7 1.1 convert_element_type.35
  6.8 0.7 pad.4.share_ref
  7.5 0.0 copy-done
  7.5 0.7 dynamic-slice_convert_fusion.own_out_ref
  8.1 0.3 concatenate.9
  8.4 0.7 constant_dynamic-slice_fusion.own_mix_ref
  9.1 0.8 negate_select_fusion
  9.9 0.9 pad_maximum_fusion.tab_ref
  10.8 149.7 %shard_map.221 = (bf16[1536,4352]{1,0:T(8,128)(2,1)}, bf16[4,4,96,1536]{3,2,1,0:T(8,128)(2,1)}, bf16[4,4,96,1536]{3,2,1,0:T(8,128)(2,1)}, bf16[8,384,1536]{2,1,0...) custom-call(s32[1]{0:T(128)S(6)} %copy.36.starts_ref, ...), custom_call_target="tpu_custom_call" | custom-call | flops 149999992832 | bytes 20000000 | tf_op jit(solution)/shard_map/pallas_call | solution.py:541
  160.4 160.9 %shard_map.222 = (bf16[4,768,1536]{2,1,0:T(8,128)(2,1)}, bf16[4,384,1536]{2,1,0:T(8,128)(2,1)}, bf16[4,384,1536]{2,1,0:T(8,128)(2,1)}, f32[384,1536]{1,0:T(8,128)}, bf16[384,1536]{1,0:T(8,128)(2,1)}) custom-call(bf16[384,1536]{1,0:T(8,128)(2,1)} %get-tuple-element.40.n2_hbm, bf16[4,768,1536]{2,1,0:T(8,128)(2,1)} %bitcast.9, ...), custom_call_target="tpu_custom_call" | custom-call | flops 99999997952 | bytes 50000000 | tf_op jit(solution)/shard_map/pallas_call | solution.py:1011
  321.4 103.2 %shard_map.223 = (f32[384,1536]{1,0:T(8,128)}, f32[384,1536]{1,0:T(8,128)}, bf16[384,1536]{1,0:T(8,128)(2,1)}, bf16[1536,4352]{1,0:T(8,128)(2,1)}, bf16[8,96,1536]{2,1,0:T(8,128)(2,1)}) custom-call(s32[1]{0:T(128)S(6)} %copy.36.starts_ref, f32[384,1536]{1,0:T(8,128)} %get-tuple-element.45.d_ref, bf16[384,1536]{1,0:T(8,128)(2,1)} %cot_ref.3, ...), custom_call_target="tpu_custom_call" | custom-call | flops 80000000000 | bytes 50000000 | tf_op jit(solution)/shard_map/pallas_call | solution.py:1340
  424.5 95.7 %shard_map.224 = (bf16[96,2176]{1,0:T(8,128)(2,1)}, bf16[8,96,1536]{2,1,0:T(8,128)(2,1)}) custom-call(bf16[1536,4352]{1,0:T(8,128)(2,1)} %get-tuple-element.59.g_ref, bf16[4,384,1536]{2,1,0:T(8,128)(2,1)} %get-tuple-element.57.pack_b_ref.pack_ref, bf16[384,1536]{1,0:T(8,128)(2,1)} %get-tuple-element.60.before_ref), custom_call_target="tpu_custom_call" | custom-call | flops 49999998976 | bytes 20000000 | tf_op jit(solution)/shard_map/pallas_call | solution.py:1556
  520.3 1.6 collective-permute-start
  521.9 0.0 copy-start.3
  521.9 8.1 %shard_map.225 = (f32[96,16,512]{2,1,0:T(8,128)}, f32[96,16,512]{2,1,0:T(8,128)}, f32[32,16,1536]{2,1,0:T(8,128)}, f32[384,1536]{1,0:T(8,128)}) custom-call(bf16[8,96,1536]{2,1,0:T(8,128)(2,1)} %get-tuple-element.58.refs_0_, bf16[8,96,1536]{2,1,0:T(8,128)(2,1)} %get-tuple-element.61.refs_1_, f32[384,1536]{1,0:T(8,128)} %get-tuple-element.53.res_hbm.refs_2_, ...), custom_call_target="tpu_custom_call" | custom-call | tf_op jit(solution)/shard_map/pallas_call | solution.py:1646
  530.0 0.0 copy-start.2
  530.0 2.2 collective-permute-done
  532.2 0.0 copy-done.3
  532.2 0.2 fusion
  532.4 0.7 slice_reduce_fusion
  533.1 0.8 fusion.9
  533.8 1.1 fusion.8
  535.0 0.0 copy-start.1
  535.0 0.0 copy-done.2
  535.0 1.4 copy.37
  536.4 0.0 copy-done.1
  (4 shorter events, 0.0 us)
Async XLA Ops:
  0.6 6.8 %copy-start = (f32[96,1536]{1,0:T(8,128)S(1)}, f32[96,1536]{1,0:T(8,128)}, u32[]{:S(2)}) copy-start(f32[96,1536]{1,0:T(8,128)} %param.23) | copy-start | bytes 1769476
  520.3 11.9 %collective-permute-start = (bf16[96,2176]{1,0:T(8,128)(2,1)}, bf16[96,2176]{1,0:T(8,128)(2,1)S(1)}, u32[]{:S(2)}, u32[]{:S(2)}) collective-permute-start(bf16[96,2176]{1,0:T(8,128)(2,1)} %get-tuple-element.65), channel_id=1, source_target_pairs={{0,16},{1,17},{2,18},{3,19},{4,20},{5,21},{6,22},{7,23},{8,24},{9,... | collective-permute-start | bytes 1253384 | tf_op jit(solution)/shard_map/ppermute | solution.py:1698
  521.9 10.3 %copy-start.3 = (bf16[96,2176]{1,0:T(8,128)(2,1)S(1)}, bf16[96,2176]{1,0:T(8,128)(2,1)}, u32[]{:S(2)}) copy-start(bf16[96,2176]{1,0:T(8,128)(2,1)} %get-tuple-element.65) | copy-start | bytes 1253380
  530.0 5.0 copy-start.2
  535.0 1.4 copy-start.1

commit v7 on v6

--- a/solution.py
+++ b/solution.py
@@ -2,6 +2,7 @@
 
 import jax
 import jax.numpy as jnp
+import numpy as np
 from jax import lax
 from jax.experimental import pallas as pl
 from jax.experimental.pallas import tpu as pltpu
@@ -22,13 +23,15 @@
 
 
 def turn_tables(length):
-    positions = jnp.arange(length, dtype=F32)[:, None]
-    lanes = jnp.arange(2 * HEAD)
-    rates = jnp.exp((lanes % (HEAD // 2)).astype(F32) * (-2.0 * math.log(10000.0) / HEAD))
+    positions = np.arange(length, dtype=np.float32)[:, None]
+    lanes = np.arange(2 * HEAD)
+    powers = (lanes % (HEAD // 2)).astype(np.float32)
+    rates = np.exp(powers * np.float32(-2.0 * math.log(10000.0) / HEAD))
     angles = positions * rates[None, :]
     low = (lanes % HEAD < HEAD // 2)[None, :]
-    sines = jnp.sin(angles)
-    return jnp.stack([jnp.cos(angles), jnp.where(low, -sines, 0.0), jnp.where(low, 0.0, sines)])
+    sines = np.sin(angles)
+    tables = [np.cos(angles), np.where(low, -sines, 0.0), np.where(low, 0.0, sines)]
+    return jnp.asarray(np.stack(tables).astype(np.float32))
 
 
 def turned(values, tables, sign):
@@ -1514,8 +1517,6 @@
                 step,
             )
             y_second[k] = at.send(kept.at[k, 0, 1, :, second], near_y.at[k, :, second], at.y)
-        exchange = Exchange(at, ring.total(), shards_ref, ds)
-        exchange.start(local_sems.at[1])
         arrive_z = {}
         for k in order:
             for copies in (x_second, y_first, x_first, y_second):
@@ -1536,6 +1537,9 @@
             )
             if k > 0:
                 arrive_z[k] = at.send(total_ref.at[k], from_z.at[k], at.along[k])
+            if k == order[1]:
+                exchange = Exchange(at, ring.total(), shards_ref, ds)
+                exchange.start(local_sems.at[1])
         exchange.onward()
         for k in range(1, planes):
             arrive_z[k].wait_recv()

time: 545 us -> 543 us (level)
  no operation moved by 1% of the time
where the time goes in v7:
time: 543 us; the launch traced here: 535 us
  Pallas kernels  518 us (95%)
  local copies, waits for them, and re-layouts  6.68 us (1%)
    pallas_call x1, Pallas kernels, run_experts(): pl.pallas_call(kernel, in_specs=[anywhere()] * 2 + [whole_vmem()] + [anyw...  161 us
    pallas_call x1, Pallas kernels, forward(): pl.pallas_call(kernel, out_shape=[shape((width, columns), BF), shape((pla...  150 us
    pallas_call x1, Pallas kernels, backward(): pl.pallas_call(kernel, in_specs=[pl.BlockSpec(memory_space=pltpu.SMEM)] +...  103 us
    pallas_call x1, Pallas kernels, scatter_front(): pl.pallas_call(kernel, out_shape=[jax.ShapeDtypeStruct((ds, half), BF), j...  95.7 us
  transfers between devices with their start and end apart: 1, of which 1 were waited for; matrix products, arithmetic and copies ran while one was open for 0% of the time, Pallas kernels for 2%

profile of v7, /device:TPU:0, one launch (start us, length us, event | category | flops | bytes accessed | tf_op | source)
XLA Modules:
  0.0 535.2 jit_solution(9731364636885809395)
XLA Ops:
  0.6 0.0 copy-start
  1.4 0.7 convert_bitcast_fusion.1
  2.0 0.7 convert_bitcast_fusion
  2.7 0.1 copy.36
  2.8 0.1 copy.35
  3.0 0.8 select_reduce_fusion
  3.8 0.9 convert_element_type.24
  4.7 0.9 convert_element_type.25
  5.7 1.1 convert_element_type.23
  6.8 0.7 pad.4.share_ref
  7.4 0.0 copy-done
  7.4 0.7 dynamic-slice_convert_fusion.own_out_ref
  8.1 0.3 concatenate.9
  8.4 0.7 constant_dynamic-slice_fusion.own_mix_ref
  9.1 149.6 %shard_map.239 = (bf16[1536,4352]{1,0:T(8,128)(2,1)}, bf16[4,4,96,1536]{3,2,1,0:T(8,128)(2,1)}, bf16[4,4,96,1536]{3,2,1,0:T(8,128)(2,1)}, bf16[8,384,1536]{2,1,0...) custom-call(s32[1]{0:T(128)S(6)} %copy.38.starts_ref, ...), custom_call_target="tpu_custom_call" | custom-call | flops 149999992832 | bytes 20000000 | tf_op jit(solution)/shard_map/pallas_call | solution.py:544
  158.8 160.9 %shard_map.240 = (bf16[4,768,1536]{2,1,0:T(8,128)(2,1)}, bf16[4,384,1536]{2,1,0:T(8,128)(2,1)}, bf16[4,384,1536]{2,1,0:T(8,128)(2,1)}, f32[384,1536]{1,0:T(8,128)}, bf16[384,1536]{1,0:T(8,128)(2,1)}) custom-call(bf16[384,1536]{1,0:T(8,128)(2,1)} %get-tuple-element.40.n2_hbm, bf16[4,768,1536]{2,1,0:T(8,128)(2,1)} %bitcast.9, ...), custom_call_target="tpu_custom_call" | custom-call | flops 99999997952 | bytes 50000000 | tf_op jit(solution)/shard_map/pallas_call | solution.py:1014
  319.7 103.3 %shard_map.241 = (f32[384,1536]{1,0:T(8,128)}, f32[384,1536]{1,0:T(8,128)}, bf16[384,1536]{1,0:T(8,128)(2,1)}, bf16[1536,4352]{1,0:T(8,128)(2,1)}, bf16[8,96,1536]{2,1,0:T(8,128)(2,1)}) custom-call(s32[1]{0:T(128)S(6)} %copy.38.starts_ref, f32[384,1536]{1,0:T(8,128)} %get-tuple-element.45.d_ref, bf16[384,1536]{1,0:T(8,128)(2,1)} %cot_ref.3, ...), custom_call_target="tpu_custom_call" | custom-call | flops 80000000000 | bytes 50000000 | tf_op jit(solution)/shard_map/pallas_call | solution.py:1343
  423.0 95.7 %shard_map.242 = (bf16[96,2176]{1,0:T(8,128)(2,1)}, bf16[8,96,1536]{2,1,0:T(8,128)(2,1)}) custom-call(bf16[1536,4352]{1,0:T(8,128)(2,1)} %get-tuple-element.59.g_ref, bf16[4,384,1536]{2,1,0:T(8,128)(2,1)} %get-tuple-element.57.pack_b_ref.pack_ref, bf16[384,1536]{1,0:T(8,128)(2,1)} %get-tuple-element.60.before_ref), custom_call_target="tpu_custom_call" | custom-call | flops 49999998976 | bytes 20000000 | tf_op jit(solution)/shard_map/pallas_call | solution.py:1560
  518.6 1.6 collective-permute-start
  520.2 0.0 copy-start.3
  520.2 8.1 %shard_map.243 = (f32[96,16,512]{2,1,0:T(8,128)}, f32[96,16,512]{2,1,0:T(8,128)}, f32[32,16,1536]{2,1,0:T(8,128)}, f32[384,1536]{1,0:T(8,128)}) custom-call(bf16[8,96,1536]{2,1,0:T(8,128)(2,1)} %get-tuple-element.58.refs_0_, bf16[8,96,1536]{2,1,0:T(8,128)(2,1)} %get-tuple-element.61.refs_1_, f32[384,1536]{1,0:T(8,128)} %get-tuple-element.53.res_hbm.refs_2_, ...), custom_call_target="tpu_custom_call" | custom-call | tf_op jit(solution)/shard_map/pallas_call | solution.py:1650
  528.4 0.0 copy-start.2
  528.4 2.2 collective-permute-done
  530.5 0.0 copy-done.3
  530.5 0.2 fusion
  530.7 0.7 slice_reduce_fusion
  531.4 0.8 fusion.2
  532.2 1.1 fusion.1
  533.3 0.0 copy-start.1
  533.3 0.0 copy-done.2
  533.3 1.4 copy.39
  534.7 0.0 copy-done.1
  (2 shorter events, 0.0 us)
Async XLA Ops:
  0.6 6.8 %copy-start = (f32[96,1536]{1,0:T(8,128)S(1)}, f32[96,1536]{1,0:T(8,128)}, u32[]{:S(2)}) copy-start(f32[96,1536]{1,0:T(8,128)} %param.25) | copy-start | bytes 1769476
  518.6 11.9 %collective-permute-start = (bf16[96,2176]{1,0:T(8,128)(2,1)}, bf16[96,2176]{1,0:T(8,128)(2,1)S(1)}, u32[]{:S(2)}, u32[]{:S(2)}) collective-permute-start(bf16[96,2176]{1,0:T(8,128)(2,1)} %get-tuple-element.65), channel_id=1, source_target_pairs={{0,16},{1,17},{2,18},{3,19},{4,20},{5,21},{6,22},{7,23},{8,24},{9,... | collective-permute-start | bytes 1253384 | tf_op jit(solution)/shard_map/ppermute | solution.py:1702
  520.2 10.3 %copy-start.3 = (bf16[96,2176]{1,0:T(8,128)(2,1)S(1)}, bf16[96,2176]{1,0:T(8,128)(2,1)}, u32[]{:S(2)}) copy-start(bf16[96,2176]{1,0:T(8,128)(2,1)} %get-tuple-element.65) | copy-start | bytes 1253380
  528.4 5.0 copy-start.2
  533.3 1.4 copy-start.1

commit v8 on v7

--- a/solution.py
+++ b/solution.py
@@ -862,6 +862,11 @@
         def out_copy(pair):
             return pltpu.make_async_copy(o_tile, out_hbm.at[pair], local_sems.at[0])
 
+        def out_free(step, pair):
+            @pl.when(step > 0)
+            def _():
+                out_copy(pair).wait()
+
         def tile(e, step, pair, w, down, middle):
             g_load = pltpu.make_async_copy(g_hbm.at[pair], g_tile, local_sems.at[1])
             g_load.start()
@@ -875,6 +880,10 @@
                 up = dot(x[...], w[:, up_cols])
                 if n == 0:
                     g_load.wait()
+                    if e > 0:
+                        out_free(step, pair)
+                        before = pltpu.make_async_copy(out_hbm.at[pair], o_tile, local_sems.at[2])
+                        before.start()
                 inner = dot_nt(g_tile[...], down[cols, :]) * share
                 sig = jax.nn.sigmoid(gate)
                 swish = gate * sig
@@ -882,15 +891,10 @@
                 pre[:, cols] = (inner * up * sig * (1.0 + gate * (1.0 - sig))).astype(BF)
                 pre[:, up_cols] = (inner * swish).astype(BF)
             middle()
-
-            @pl.when(step > 0)
-            def _():
-                out_copy(pair).wait()
-
             if e > 0:
-                before = pltpu.make_async_copy(out_hbm.at[pair], o_tile, local_sems.at[2])
-                before.start()
                 before.wait()
+            else:
+                out_free(step, pair)
             for n in range(width // hid):
                 cols = slice(n * hid, (n + 1) * hid)
                 out = dot(act[...], down[:, cols])

time: 543 us -> 538 us (level)
  no operation moved by 1% of the time
where the time goes in v8:
time: 538 us; the launch traced here: 530 us
  Pallas kernels  513 us (95%)
  local copies, waits for them, and re-layouts  6.68 us (1%)
    pallas_call x1, Pallas kernels, run_experts(): pl.pallas_call(kernel, in_specs=[anywhere()] * 2 + [whole_vmem()] + [anyw...  156 us
    pallas_call x1, Pallas kernels, forward(): pl.pallas_call(kernel, out_shape=[shape((width, columns), BF), shape((pla...  150 us
    pallas_call x1, Pallas kernels, backward(): pl.pallas_call(kernel, in_specs=[pl.BlockSpec(memory_space=pltpu.SMEM)] +...  103 us
    pallas_call x1, Pallas kernels, scatter_front(): pl.pallas_call(kernel, out_shape=[jax.ShapeDtypeStruct((ds, half), BF), j...  95.7 us
  transfers between devices with their start and end apart: 1, of which 1 were waited for; matrix products, arithmetic and copies ran while one was open for 0% of the time, Pallas kernels for 2%

profile of v8, /device:TPU:0, one launch (start us, length us, event | category | flops | bytes accessed | tf_op | source)
XLA Modules:
  0.0 530.2 jit_solution(11064706171997653117)
XLA Ops:
  0.6 0.0 copy-start
  1.4 0.7 convert_bitcast_fusion.1
  2.0 0.7 convert_bitcast_fusion
  2.7 0.1 copy.36
  2.8 0.1 copy.35
  3.0 0.8 select_reduce_fusion
  3.8 0.9 convert_element_type.24
  4.7 0.9 convert_element_type.25
  5.7 1.1 convert_element_type.23
  6.8 0.7 pad.4.share_ref
  7.4 0.0 copy-done
  7.4 0.7 dynamic-slice_convert_fusion.own_out_ref
  8.1 0.3 concatenate.9
  8.4 0.7 constant_dynamic-slice_fusion.own_mix_ref
  9.1 149.6 %shard_map.239 = (bf16[1536,4352]{1,0:T(8,128)(2,1)}, bf16[4,4,96,1536]{3,2,1,0:T(8,128)(2,1)}, bf16[4,4,96,1536]{3,2,1,0:T(8,128)(2,1)}, bf16[8,384,1536]{2,1,0...) custom-call(s32[1]{0:T(128)S(6)} %copy.38.starts_ref, ...), custom_call_target="tpu_custom_call" | custom-call | flops 149999992832 | bytes 20000000 | tf_op jit(solution)/shard_map/pallas_call | solution.py:544
  158.8 155.9 %shard_map.240 = (bf16[4,768,1536]{2,1,0:T(8,128)(2,1)}, bf16[4,384,1536]{2,1,0:T(8,128)(2,1)}, bf16[4,384,1536]{2,1,0:T(8,128)(2,1)}, f32[384,1536]{1,0:T(8,128)}, bf16[384,1536]{1,0:T(8,128)(2,1)}) custom-call(bf16[384,1536]{1,0:T(8,128)(2,1)} %get-tuple-element.40.n2_hbm, bf16[4,768,1536]{2,1,0:T(8,128)(2,1)} %bitcast.9, ...), custom_call_target="tpu_custom_call" | custom-call | flops 99999997952 | bytes 50000000 | tf_op jit(solution)/shard_map/pallas_call | solution.py:1018
  314.7 103.2 %shard_map.241 = (f32[384,1536]{1,0:T(8,128)}, f32[384,1536]{1,0:T(8,128)}, bf16[384,1536]{1,0:T(8,128)(2,1)}, bf16[1536,4352]{1,0:T(8,128)(2,1)}, bf16[8,96,1536]{2,1,0:T(8,128)(2,1)}) custom-call(s32[1]{0:T(128)S(6)} %copy.38.starts_ref, f32[384,1536]{1,0:T(8,128)} %get-tuple-element.45.d_ref, bf16[384,1536]{1,0:T(8,128)(2,1)} %cot_ref.3, ...), custom_call_target="tpu_custom_call" | custom-call | flops 80000000000 | bytes 50000000 | tf_op jit(solution)/shard_map/pallas_call | solution.py:1347
  417.9 95.7 %shard_map.242 = (bf16[96,2176]{1,0:T(8,128)(2,1)}, bf16[8,96,1536]{2,1,0:T(8,128)(2,1)}) custom-call(bf16[1536,4352]{1,0:T(8,128)(2,1)} %get-tuple-element.59.g_ref, bf16[4,384,1536]{2,1,0:T(8,128)(2,1)} %get-tuple-element.57.pack_b_ref.pack_ref, bf16[384,1536]{1,0:T(8,128)(2,1)} %get-tuple-element.60.before_ref), custom_call_target="tpu_custom_call" | custom-call | flops 49999998976 | bytes 20000000 | tf_op jit(solution)/shard_map/pallas_call | solution.py:1564
  513.6 1.7 collective-permute-start
  515.3 0.0 copy-start.3
  515.3 8.1 %shard_map.243 = (f32[96,16,512]{2,1,0:T(8,128)}, f32[96,16,512]{2,1,0:T(8,128)}, f32[32,16,1536]{2,1,0:T(8,128)}, f32[384,1536]{1,0:T(8,128)}) custom-call(bf16[8,96,1536]{2,1,0:T(8,128)(2,1)} %get-tuple-element.58.refs_0_, bf16[8,96,1536]{2,1,0:T(8,128)(2,1)} %get-tuple-element.61.refs_1_, f32[384,1536]{1,0:T(8,128)} %get-tuple-element.53.res_hbm.refs_2_, ...), custom_call_target="tpu_custom_call" | custom-call | tf_op jit(solution)/shard_map/pallas_call | solution.py:1654
  523.4 0.0 copy-start.2
  523.4 2.1 collective-permute-done
  525.5 0.0 copy-done.3
  525.6 0.2 fusion
  525.7 0.7 slice_reduce_fusion
  526.4 0.8 fusion.2
  527.2 1.1 fusion.1
  528.3 0.0 copy-start.1
  528.3 0.0 copy-done.2
  528.3 1.4 copy.39
  529.8 0.0 copy-done.1
  (2 shorter events, 0.0 us)
Async XLA Ops:
  0.6 6.8 %copy-start = (f32[96,1536]{1,0:T(8,128)S(1)}, f32[96,1536]{1,0:T(8,128)}, u32[]{:S(2)}) copy-start(f32[96,1536]{1,0:T(8,128)} %param.25) | copy-start | bytes 1769476
  513.6 11.9 %collective-permute-start = (bf16[96,2176]{1,0:T(8,128)(2,1)}, bf16[96,2176]{1,0:T(8,128)(2,1)S(1)}, u32[]{:S(2)}, u32[]{:S(2)}) collective-permute-start(bf16[96,2176]{1,0:T(8,128)(2,1)} %get-tuple-element.65), channel_id=1, source_target_pairs={{0,16},{1,17},{2,18},{3,19},{4,20},{5,21},{6,22},{7,23},{8,24},{9,... | collective-permute-start | bytes 1253384 | tf_op jit(solution)/shard_map/ppermute | solution.py:1706
  515.3 10.3 %copy-start.3 = (bf16[96,2176]{1,0:T(8,128)(2,1)S(1)}, bf16[96,2176]{1,0:T(8,128)(2,1)}, u32[]{:S(2)}) copy-start(bf16[96,2176]{1,0:T(8,128)(2,1)} %get-tuple-element.65) | copy-start | bytes 1253380
  523.4 4.9 copy-start.2
  528.3 1.4 copy-start.1
